TPU v7x, 128 devices: a whole 4x4x4 slice. The times are simulated.
128 devices in a mesh: node: 32 (over y, x, z_lo), local: 4 (over z_hi, core).
Axes of the slice: x: 4, y: 4, z: 4 (z_hi: 2, z_lo: 2; z = z_hi * 2 + z_lo), core: 2. Of those that a mesh axis runs over, the one named last changes fastest.
Arguments:
- tokens: bfloat16 [16384, 4096], P(('node', 'local')), may hold values from -6 to 6
- grad_out: bfloat16 [16384, 4096], P(('node', 'local')), may hold values from -6 to 6
- router_logits: float32 [16384, 128], P(('node', 'local')), may hold values from -20 to 280
- group_id: int32 [16384], P(('node', 'local')), may hold values from 0 to 15, as said below
- expert_ids: int32 [16384, 2], P(('node', 'local')), may hold values from 0 to 7, as said below
- w_gate: bfloat16 [32, 4096, 1536], P('node', None, 'local'), may hold values from -0.09375 to 0.09375
- w_up: bfloat16 [32, 4096, 1536], P('node', None, 'local'), may hold values from -0.09375 to 0.09375
- w_down: bfloat16 [32, 1536, 4096], P('node', 'local'), may hold values from -0.15625 to 0.15625
Outputs:
- mixed: bfloat16 [16384, 4096], P(('node', 'local'))
- d_tokens: bfloat16 [16384, 4096], P(('node', 'local'))
- d_logits: float32 [16384, 128], P(('node', 'local'))
- grad_gate: bfloat16 [32, 4096, 1536], P('node', None, 'local')
- grad_up: bfloat16 [32, 4096, 1536], P('node', None, 'local')
- grad_down: bfloat16 [32, 1536, 4096], P('node', 'local')
Inputs may be any that keep to these rules, and one draw needn't show every extreme that they name: `group_id`: A token is computed here when its group is below 4. Among the tokens of one device no expert of those groups is named by more than 6 tokens, and one such expert is named by exactly 6 tokens of every device. `expert_ids`: the two numbers of a token differ; both name experts of the token's group.
All inputs are finite; a program needn't handle non-finite values.
Results may differ from a plain program's by a relative error of at most 0.0065.
Values may be sent and summed in bfloat16 or wider, within the bound.
No kernel may reach another device: no remote copies, remote signals or barrier semaphores. Data moves between devices by JAX's collectives and lax.ppermute only.
A program may use at most 192 MiB of HBM per device.

v0:
```python
import functools

import jax
import jax.numpy as jnp
import numpy as np
from jax import lax
from jax.experimental import pallas as pl
from jax.experimental.pallas import tpu as pltpu
from jax.sharding import Mesh, PartitionSpec as P

GSIZE = 8
CAP = 6
CUT = 4
TEAM = 8
LINES = CUT * CAP
BUSY = 200_000_000_000
WIDE = ("y", "x", "l", "h")
ALL = ("y", "x", "l", "h", "c")
NODE = ("y", "x", "l")
LOCAL = ("h", "c")
F32 = jnp.float32
BF16 = jnp.bfloat16


def dot(a, b, dims=((1,), (0,))):
    return lax.dot_general(a, b, (dims, ((), ())), preferred_element_type=F32)


def across(a, b):
    return dot(a, b, ((1,), (1,)))


def call(kernel, name, outs, flops=1, **more):
    return pl.pallas_call(
        kernel,
        out_shape=outs,
        name=name,
        cost_estimate=pl.CostEstimate(flops=flops, bytes_accessed=1, transcendentals=0),
        compiler_params=pltpu.CompilerParams(vmem_limit_bytes=52 << 20),
        **more,
    )


def whole(shape):
    return pl.BlockSpec(shape, lambda *_: (0,) * len(shape))


def gate_weights(logits, group_ids, chosen, inside):
    probabilities = jax.nn.softmax(logits, axis=-1)
    columns = jnp.arange(logits.shape[1], dtype=jnp.int32)
    member = ((columns // GSIZE)[None, :] == group_ids[:, None]).astype(logits.dtype)
    group_mass = jnp.sum(probabilities * member, axis=1)
    picked = jnp.sum(
        jnp.where(chosen[:, :, None] == columns[None, None, :], logits[:, None, :], 0.0), axis=2
    )
    pair_share = jax.nn.softmax(picked, axis=-1)
    return jnp.where(inside[:, None], group_mass[:, None] * pair_share, 0.0)


def exchange(value):
    blocks = value.reshape(-1, LINES, value.shape[-1])
    out = lax.all_to_all(blocks, WIDE, split_axis=0, concat_axis=0, tiled=True)
    return out.reshape(value.shape)


def swap(value):
    return lax.ppermute(value, "c", [(0, 1), (1, 0)])


def order_matrix(copies):
    line = np.arange(TEAM * copies * LINES)
    member, chunk, slot = line // (copies * LINES), line // CAP % CUT, line % CAP
    wanted = (chunk * TEAM + member) * CAP + slot
    return (wanted[:, None] == np.arange(TEAM * LINES)[None, :]).astype(BF16)


def gathered(ref, start, width):
    team = pl.ds(start, TEAM * CAP)
    return jnp.concatenate([ref[team, j * width : (j + 1) * width] for j in range(CUT)], axis=0)


def slots_kernel(expert_total, group_ref, expert_ref, rows_ref, spread_ref, out_ref, slot_ref, held):
    team = pl.program_id(0)
    width = out_ref.shape[1]

    @pl.when(team == 0)
    def _():
        count = group_ref.shape[1]
        group = group_ref[...]
        inside = group < expert_total // GSIZE
        down = lax.broadcasted_iota(jnp.int32, (count, count), 0)
        along = lax.broadcasted_iota(jnp.int32, (count, count), 1)
        expert = lax.broadcasted_iota(jnp.int32, (expert_total, count), 0)
        targets, hots = [], []
        for k in range(2):
            column = expert_ref[:, k : k + 1].astype(F32)
            row = jnp.sum(jnp.where(down == along, column, 0.0), axis=0, keepdims=True)
            target = jnp.where(inside, group * GSIZE + row.astype(jnp.int32), expert_total)
            targets.append(target)
            hots.append((expert == target).astype(F32))
        before = (down < along).astype(F32).astype(BF16)
        earlier = dot((hots[0] + hots[1]).astype(BF16), before)
        place = lax.broadcasted_iota(jnp.int32, (expert_total * CAP, count), 0)
        picked = None
        for k in range(2):
            rank = jnp.sum(hots[k] * earlier, axis=0, keepdims=True).astype(jnp.int32)
            slot = jnp.where(inside, targets[k] * CAP + rank, -1)
            slot_ref[k : k + 1, :] = slot
            match = place == slot
            picked = match if picked is None else picked | match
        picked = picked.astype(F32).astype(BF16)
        held[...] = dot(picked, rows_ref[...]).astype(BF16)

    start = pl.multiple_of(team * (TEAM * CAP), 16)
    out_ref[...] = dot(spread_ref[...], gathered(held, start, width)).astype(BF16)


def pack_tokens(group_id, expert_ids, tokens, spread, expert_total):
    count, model_width = tokens.shape
    width = model_width // CUT
    teams, lines = expert_total // TEAM, spread.shape[0]
    return call(
        functools.partial(slots_kernel, expert_total),
        "pack_tokens",
        (
            jax.ShapeDtypeStruct((teams * lines, width), BF16),
            jax.ShapeDtypeStruct((2, count), jnp.int32),
        ),
        grid=(teams,),
        in_specs=[
            whole((1, count)),
            whole(expert_ids.shape),
            whole(tokens.shape),
            whole(spread.shape),
        ],
        out_specs=(pl.BlockSpec((lines, width), lambda t: (t, 0)), whole((2, count))),
        scratch_shapes=[pltpu.VMEM((expert_total * CAP, model_width), BF16)],
    )(group_id[None], expert_ids, tokens, spread)


def grads_kernel(slot_ref, weight_ref, rows_ref, spread_ref, out_ref, held):
    team = pl.program_id(0)
    width = out_ref.shape[1]

    @pl.when(team == 0)
    def _():
        place = lax.broadcasted_iota(jnp.int32, (held.shape[0], slot_ref.shape[1]), 0)
        first, second = place == slot_ref[0:1, :], place == slot_ref[1:2, :]
        weight = jnp.where(first, weight_ref[0:1, :], 0.0)
        weight += jnp.where(second, weight_ref[1:2, :], 0.0)
        weight = jnp.sum(weight, axis=1, keepdims=True)
        picked = (first | second).astype(F32).astype(BF16)
        held[...] = (dot(picked, rows_ref[...]) * weight).astype(BF16)

    start = pl.multiple_of(team * (TEAM * CAP), 16)
    out_ref[...] = dot(spread_ref[...], gathered(held, start, width)).astype(BF16)


def pack_grads(slot, weights, grad_out, spread, expert_total):
    count, model_width = grad_out.shape
    width = model_width // CUT
    teams, lines = expert_total // TEAM, spread.shape[0]
    return call(
        grads_kernel,
        "pack_grads",
        jax.ShapeDtypeStruct((teams * lines, width), BF16),
        grid=(teams,),
        in_specs=[
            whole((2, count)),
            whole((2, count)),
            whole(grad_out.shape),
            whole(spread.shape),
        ],
        out_specs=pl.BlockSpec((lines, width), lambda t: (t, 0)),
        scratch_shapes=[pltpu.VMEM((expert_total * CAP, model_width), BF16)],
    )(slot, weights, grad_out, spread)


def put_in_order(lines_ref, order_ref, rows_ref):
    width = lines_ref.shape[1]
    step, rows = TEAM * LINES, TEAM * CAP
    for t in range(lines_ref.shape[0] // step):
        moved = dot(order_ref[...], lines_ref[t * step : (t + 1) * step]).astype(BF16)
        for j in range(CUT):
            columns = slice(j * width, (j + 1) * width)
            rows_ref[t * rows : (t + 1) * rows, columns] = moved[j * rows : (j + 1) * rows]


def forward_kernel(
    lines_ref, order_ref, gate_ref, up_ref, down_ref, rows_ref, g_ref, u_ref, hidden_ref, *out_ref
):
    step = pl.program_id(0)
    width = lines_ref.shape[1]

    @pl.when(step == 0)
    def _():
        put_in_order(lines_ref, order_ref, rows_ref)
        g_ref[...] = jnp.zeros_like(g_ref)
        u_ref[...] = jnp.zeros_like(u_ref)

    rows = rows_ref[:, pl.ds(pl.multiple_of(step * width, width), width)]
    g_ref[...] += dot(rows, gate_ref[...])
    u_ref[...] += dot(rows, up_ref[...])

    @pl.when(step == pl.num_programs(0) - 1)
    def _():
        gate = g_ref[...]
        hidden = (gate * jax.nn.sigmoid(gate) * u_ref[...]).astype(BF16)
        hidden_ref[...] = hidden
        for ref in out_ref:
            for j in range(CUT):
                part = slice(j * width, (j + 1) * width)
                ref[:, part] = dot(hidden, down_ref[:, part]).astype(BF16)


def forward(lines, order, w_gate, w_up, w_down, own):
    width = lines.shape[1]
    half, model_width = lines.shape[0] // CUT, CUT * width
    units = w_down.shape[1]
    wide = jax.ShapeDtypeStruct((half, model_width), BF16)
    weight_spec = pl.BlockSpec((None, width, units), lambda k: (0, k, 0))
    act = whole((half, units))
    outs = [wide] + [jax.ShapeDtypeStruct((half, units), t) for t in (F32, F32, BF16)]
    if not own:
        outs.append(wide)
    down_shape = (None, units, model_width if not own else width)
    return call(
        forward_kernel,
        "forward_own" if own else "forward_other",
        outs,
        BUSY,
        grid=(CUT,),
        in_specs=[
            whole(lines.shape),
            whole(order.shape),
            weight_spec,
            weight_spec,
            pl.BlockSpec(down_shape, lambda k: (0, 0, 0)),
        ],
        out_specs=[whole(wide.shape), act, act, act, whole(wide.shape)][: len(outs)],
    )(lines, order, w_gate, w_up, w_down)


def backward_kernel(
    lines_ref, order_ref, down_ref, g_ref, u_ref, gate_ref, up_ref, rows_ref, dg_ref, du_ref, *more
):
    step = pl.program_id(0)
    width = lines_ref.shape[1]
    *out_ref, total = more

    @pl.when(step == 0)
    def _():
        put_in_order(lines_ref, order_ref, rows_ref)
        total[...] = jnp.zeros_like(total)

    rows = rows_ref[:, pl.ds(pl.multiple_of(step * width, width), width)]
    total[...] += across(rows, down_ref[...])

    @pl.when(step == pl.num_programs(0) - 1)
    def _():
        gate, grad_hidden = g_ref[...], total[...]
        sigmoid_gate = jax.nn.sigmoid(gate)
        dg = grad_hidden * u_ref[...] * sigmoid_gate * (1.0 + gate * (1.0 - sigmoid_gate))
        dg = dg.astype(BF16)
        du = (grad_hidden * (gate * sigmoid_gate)).astype(BF16)
        dg_ref[...] = dg
        du_ref[...] = du
        for ref in out_ref:
            for j in range(CUT):
                part = slice(j * width, (j + 1) * width)
                ref[:, part] = (
                    across(dg, gate_ref[part, :]) + across(du, up_ref[part, :])
                ).astype(BF16)


def backward(lines, order, w_down, gate_pre, up_pre, w_gate, w_up, own):
    width = lines.shape[1]
    half, model_width = lines.shape[0] // CUT, CUT * width
    units = w_down.shape[1]
    wide = jax.ShapeDtypeStruct((half, model_width), BF16)
    weight_shape = (None, model_width if not own else units, units)
    weight_spec = pl.BlockSpec(weight_shape, lambda k: (0, 0, 0))
    act = whole((half, units))
    outs = [wide] + [jax.ShapeDtypeStruct((half, units), BF16)] * 2
    if not own:
        outs.append(wide)
    return call(
        backward_kernel,
        "backward_own" if own else "backward_other",
        outs,
        BUSY,
        grid=(CUT,),
        in_specs=[
            whole(lines.shape),
            whole(order.shape),
            pl.BlockSpec((None, units, width), lambda k: (0, 0, k)),
            act,
            act,
            weight_spec,
            weight_spec,
        ],
        out_specs=[whole(wide.shape), act, act, whole(wide.shape)][: len(outs)],
        scratch_shapes=[pltpu.VMEM((half, units), F32)],
    )(lines, order, w_down, gate_pre, up_pre, w_gate, w_up)


def out_kernel(hidden_ref, down_ref, total_ref):
    total_ref[...] = dot(hidden_ref[...], down_ref[...])


def product_out(hidden, w_down):
    half, units = hidden.shape
    model_width = w_down.shape[2]
    width = model_width // CUT
    return call(
        out_kernel,
        "product_out",
        jax.ShapeDtypeStruct((half, model_width), F32),
        BUSY,
        grid=(CUT,),
        in_specs=[
            whole((half, units)),
            pl.BlockSpec((None, units, width), lambda k: (0, 0, k)),
        ],
        out_specs=pl.BlockSpec((half, width), lambda k: (0, k)),
    )(hidden, w_down)


def in_kernel(dg_ref, du_ref, gate_ref, up_ref, total_ref):
    total_ref[...] = across(dg_ref[...], gate_ref[...]) + across(du_ref[...], up_ref[...])


def product_in(dg, du, w_gate, w_up):
    half, units = dg.shape
    model_width = w_gate.shape[1]
    width = model_width // CUT
    weight_spec = pl.BlockSpec((None, width, units), lambda k: (0, k, 0))
    return call(
        in_kernel,
        "product_in",
        jax.ShapeDtypeStruct((half, model_width), F32),
        BUSY,
        grid=(CUT,),
        in_specs=[whole((half, units)), whole((half, units)), weight_spec, weight_spec],
        out_specs=pl.BlockSpec((half, width), lambda k: (0, k)),
    )(dg, du, w_gate, w_up)


def lines_kernel(total_ref, arrived_ref, order_ref, out_ref):
    width = out_ref.shape[1]
    rows, step = TEAM * CAP, TEAM * LINES
    for t in range(total_ref.shape[0] // rows):
        team = slice(t * rows, (t + 1) * rows)
        pieces = []
        for j in range(CUT):
            part = slice(j * width, (j + 1) * width)
            pieces.append((total_ref[team, part] + arrived_ref[team, part].astype(F32)).astype(BF16))
        held = jnp.concatenate(pieces, axis=0)
        out_ref[t * step : (t + 1) * step, :] = dot(order_ref[...], held).astype(BF16)


def to_lines(total, arrived, order):
    half, model_width = total.shape
    width = model_width // CUT
    parts = 4
    rows = half // parts
    return call(
        lines_kernel,
        "to_lines",
        jax.ShapeDtypeStruct((half * CUT, width), BF16),
        grid=(parts,),
        in_specs=[
            pl.BlockSpec((rows, model_width), lambda k: (k, 0)),
            pl.BlockSpec((rows, model_width), lambda k: (k, 0)),
            whole(order.shape),
        ],
        out_specs=pl.BlockSpec((rows * CUT, width), lambda k: (k, 0)),
    )(total, arrived, order)


def mix_kernel(first_ref, second_ref, lines_ref, grad_ref, weight_ref, mixed_ref, score_ref):
    step = pl.program_id(0)
    count, piece = grad_ref.shape[0], lines_ref.shape[1]
    width = grad_ref.shape[1] // CUT

    @pl.when(step == 0)
    def _():
        score_ref[...] = jnp.zeros_like(score_ref)

    first = dot(first_ref[...], lines_ref[...])
    second = dot(second_ref[...], lines_ref[...])
    for j in range(CUT):
        rows = slice(j * count, (j + 1) * count)
        columns = pl.ds(pl.multiple_of(j * width + step * piece, piece), piece)
        grad = grad_ref[:, columns].astype(F32)
        mixed_ref[:, columns] = (
            weight_ref[:, 0:1] * first[rows] + weight_ref[:, 1:2] * second[rows]
        ).astype(BF16)
        score_ref[:, 0:1] += jnp.sum(grad * first[rows], axis=1, keepdims=True)
        score_ref[:, 1:2] += jnp.sum(grad * second[rows], axis=1, keepdims=True)


def mix(first, second, lines, grad_out, weights):
    total, width = lines.shape
    piece = width // CUT
    return call(
        mix_kernel,
        "mix",
        (
            jax.ShapeDtypeStruct(grad_out.shape, BF16),
            jax.ShapeDtypeStruct(weights.shape, F32),
        ),
        grid=(CUT,),
        in_specs=[
            whole(first.shape),
            whole(second.shape),
            pl.BlockSpec((total, piece), lambda n: (0, n)),
            whole(grad_out.shape),
            whole(weights.shape),
        ],
        out_specs=(whole(grad_out.shape), whole(weights.shape)),
    )(first, second, lines, grad_out, weights)


def unpack_kernel(either_ref, lines_ref, out_ref):
    step = pl.program_id(0)
    count, piece = out_ref.shape[0], lines_ref.shape[1]
    width = out_ref.shape[1] // CUT
    rows = dot(either_ref[...], lines_ref[...]).astype(BF16)
    for j in range(CUT):
        columns = pl.ds(pl.multiple_of(j * width + step * piece, piece), piece)
        out_ref[:, columns] = rows[j * count : (j + 1) * count]


def unpack(either, lines, count):
    total, width = lines.shape
    piece = width // CUT
    return call(
        unpack_kernel,
        "unpack",
        jax.ShapeDtypeStruct((count, CUT * width), BF16),
        grid=(CUT,),
        in_specs=[whole(either.shape), pl.BlockSpec((total, piece), lambda n: (0, n))],
        out_specs=whole((count, CUT * width)),
    )(either, lines)


def body(tokens, grad_out, router_logits, group_id, expert_ids, w_gate, w_up, w_down):
    count = tokens.shape[0]
    expert_total = lax.axis_size(NODE)
    sides = lax.axis_size("h")
    peers = expert_total * sides
    spread = jnp.asarray(order_matrix(sides))
    order = order_matrix(1)
    to_travel, in_order = jnp.asarray(order), jnp.asarray(order.T)

    tokens_out, slot = pack_tokens(group_id, expert_ids, tokens, spread, expert_total)

    inside = group_id < expert_total // GSIZE
    chosen = group_id[:, None] * GSIZE + expert_ids
    weights, pull_back = jax.vjp(
        lambda values: gate_weights(values, group_id, chosen, inside), router_logits
    )
    grads_out = pack_grads(slot, weights.T, grad_out, spread, expert_total)

    line = np.arange(peers * LINES)
    line_key = ((line // LINES // sides * CAP + line % CAP) * CUT + line // CAP % CUT)[None, :]
    chunk = jnp.arange(CUT, dtype=jnp.int32)[:, None]

    def lines_of(slots):
        key = jnp.where(slots[None] >= 0, slots[None] * CUT + chunk, -1).reshape(CUT * count, 1)
        return key == line_key.astype(np.int32)

    first, second = lines_of(slot[0]), lines_of(slot[1])
    either = (first | second).astype(BF16)
    first, second = first.astype(BF16), second.astype(BF16)

    tokens_in, grads_out, first, second, either = lax.optimization_barrier(
        (exchange(tokens_out), grads_out, first, second, either)
    )
    grads_in = exchange(grads_out)
    lines_other = swap(tokens_in)
    weights3 = (w_gate, w_up, w_down)
    rows_own, gate_own, up_own, hidden_own = forward(tokens_in, in_order, *weights3, True)
    lines_other, hidden_own = lax.optimization_barrier((lines_other, hidden_own))
    rows_other, gate_other, up_other, hidden_other, out_other = forward(
        lines_other, in_order, *weights3, False
    )
    out_lines = to_lines(product_out(hidden_own, w_down), swap(out_other), to_travel)
    out_lines, grads_in = lax.optimization_barrier((out_lines, grads_in))
    out_back = exchange(out_lines)

    lines_other = swap(grads_in)
    grads_own, dg_own, du_own = backward(
        grads_in, in_order, w_down, gate_own, up_own, w_gate, w_up, True
    )
    lines_other, dg_own, du_own = lax.optimization_barrier((lines_other, dg_own, du_own))
    grads_other, dg_other, du_other, in_other = backward(
        lines_other, in_order, w_down, gate_other, up_other, w_gate, w_up, False
    )
    in_lines = to_lines(product_in(dg_own, du_own, w_gate, w_up), swap(in_other), to_travel)
    in_lines, out_back, *halves = lax.optimization_barrier(
        (
            in_lines,
            out_back,
            (rows_own, rows_other),
            (grads_own, grads_other),
            jnp.concatenate([hidden_own, hidden_other]),
            jnp.concatenate([dg_own, dg_other]),
            jnp.concatenate([du_own, du_other]),
        )
    )
    in_back = exchange(in_lines)

    rows, grads = (jnp.concatenate(pair) for pair in halves[:2])
    hidden, dg, du = halves[2:]
    grad_gate = dot(rows, dg, ((0,), (0,))).astype(BF16)
    grad_up = dot(rows, du, ((0,), (0,))).astype(BF16)
    grad_down = dot(hidden, grads, ((0,), (0,))).astype(BF16)
    grad_down, out_back = lax.optimization_barrier((grad_down, out_back))
    mixed, scores = mix(first, second, out_back, grad_out, weights)
    d_logits = pull_back(scores)[0]
    d_tokens = unpack(either, in_back, count)
    return (mixed, d_tokens, d_logits, grad_gate[None], grad_up[None], grad_down[None])


def solution(mesh):
    fine = Mesh(mesh.devices.reshape(4, 4, 2, 2, 2), ALL)
    return jax.shard_map(
        body,
        mesh=fine,
        in_specs=(
            P(ALL, None),
            P(ALL, None),
            P(ALL, None),
            P(ALL),
            P(ALL, None),
            P(NODE, None, LOCAL),
            P(NODE, None, LOCAL),
            P(NODE, LOCAL, None),
        ),
        out_specs=(
            P(ALL, None),
            P(ALL, None),
            P(ALL, None),
            P(NODE, None, LOCAL),
            P(NODE, None, LOCAL),
            P(NODE, LOCAL, None),
        ),
        check_vma=False,
    )
```

profile of v0, /device:TPU:0, one launch (start us, length us, event | category | flops | bytes accessed | tf_op | source)
XLA Modules:
  0.0 223.0 jit_solution(9520352629284602257)
XLA Ops:
  0.6 0.8 copy.27.expert_ref
  1.4 1.2 copy-done.2
  2.6 0.9 copy-done.3
  3.6 0.7 copy-done.7
  4.2 3.7 %pack_tokens.1 = (bf16[1536,1024]{1,0:T(8,128)(2,1)}, s32[2,128]{1,0:T(2,128)S(1)}) custom-call(s32[1,128]{1,0:T(1,128)S(1)} %bitcast.33, s32[128,2]{1,0:T(8,128)S(1)} %copy.27.expert_ref, bf16[128,4096]{1,0:T(8,128)(2,1)S(1)} %copy-done.2, bf16[384,192]{1,0:T(8,128)(2,1)S(1)} %copy-done.3), custom_call_target="tpu_custom_call" | custom-call | flops 1 | bytes 1 | tf_op jit(solution)/shard_map/pack_tokens/pallas_call | solution.py:122
  7.9 11.9 %all-to-all-start = ((bf16[64,24,1024]{2,1,0:T(8,128)(2,1)}), bf16[64,24,1024]{2,1,0:T(8,128)(2,1)}, u32[]{:S(2)}, u32[]{:S(2)}) async-start(bf16[64,24,1024]{2,1,0:T(8,128)(2,1)} %bitcast.37), calls=%async_computation | async-start | bytes 6291456 | tf_op jit(solution)/shard_map/all_to_all | solution.py:62
  19.9 0.6 copy-done.28
  20.4 0.2 select_reduce_fusion.1
  21.0 0.2 fusion.16
  21.2 0.3 copy-done.33
  21.5 0.2 fusion.13
  21.9 3.5 %pack_grads.1 = bf16[1536,1024]{1,0:T(8,128)(2,1)} custom-call(s32[2,128]{1,0:T(2,128)S(1)} %get-tuple-element.50.slot_ref, f32[2,128]{1,0:T(2,128)S(1)} %copy.30.weight_ref, bf16[128,4096]{1,0:T(8,128)(2,1)S(1)} %copy-done, bf16[384,192]{1,0:T(8,128)(2,1)S(1)} %copy-done.4), custom_call_target="tpu_custom_call" | custom-call | flops 1 | bytes 1 | tf_op jit(solution)/shard_map/pack_grads/pallas_call | solution.py:163
  25.4 0.5 multiply_divide_fusion.1
  25.9 0.5 multiply_divide_fusion
  26.7 2.5 %fusion.9 = (bf16[512,1536]{1,0:T(8,128)(2,1)S(1)}, bf16[512,1536]{1,0:T(8,128)(2,1)}, bf16[512,1536]{1,0:T(8,128)(2,1)}) fusion(s32[1536]{0:T(1024)S(1)} %copy-done.30, s32[512]{0:T(512)S(1)} %get-tuple-element.101, s32[512]{0:T(512)S(1)} %get-tuple-element.102), kind=kLoop, calls=%fused_computation.12 | loop fusion | flops 4718592 | bytes 4728832 | tf_op jit(solution)/shard_map/convert_element_type | solution.py:475
  29.2 30.4 %all-to-all-done = bf16[64,24,1024]{2,1,0:T(8,128)(2,1)} async-done(((bf16[64,24,1024]{2,1,0:T(8,128)(2,1)}), bf16[64,24,1024]{2,1,0:T(8,128)(2,1)}, u32[]{:S(2)}, u32[]{:S(2)}) %all-to-all-start) | async-done | bytes 3145760 | tf_op jit(solution)/shard_map/all_to_all | solution.py:62
  59.5 10.1 %all-to-all-start.1 = ((bf16[64,24,1024]{2,1,0:T(8,128)(2,1)}), bf16[64,24,1024]{2,1,0:T(8,128)(2,1)}, u32[]{:S(2)}, u32[]{:S(2)}) async-start(bf16[64,24,1024]{2,1,0:T(8,128)(2,1)} %bitcast.34), calls=%async_computation.1 | async-start | bytes 6291456 | tf_op jit(solution)/shard_map/all_to_all | solution.py:62
  69.7 9.8 %forward_own.1 = (bf16[384,4096]{1,0:T(8,128)(2,1)}, f32[384,384]{1,0:T(8,128)S(1)}, f32[384,384]{1,0:T(8,128)S(1)}, bf16[384,384]{1,0:T(8,128)(2,1)S(1)}) custom-call(bf16[1536,1024]{1,0:T(8,128)(2,1)} %bitcast.2.lines_ref, bf16[192,192]{1,0:T(8,128)(2,1)S(1)} %copy-done.10, bf16[1,4096,384]{2,1,0:T(8,128)(2,1)} %gate_ref.9, bf16[1,4096,384]{2,1,0:T(8,128)(2,1)} %up_ref.9, ...), custom_call_target="tpu_custom_call" | custom-call | flops 199999995904 | bytes 1 | tf_op jit(solution)/shard_map/forward_own/pallas_call | solution.py:227
  79.5 0.8 copy-done.13
  80.3 13.5 %forward_other.1 = (bf16[384,4096]{1,0:T(8,128)(2,1)}, f32[384,384]{1,0:T(8,128)S(1)}, f32[384,384]{1,0:T(8,128)S(1)}, bf16[384,384]{1,0:T(8,128)(2,1)S(1)}, bf16[384,4096]{1,0:T(8,128)(2,1)}) custom-call(bf16[1536,1024]{1,0:T(8,128)(2,1)} %collective-permute-done.lines_ref, bf16[192,192]{1,0:T(8,128)(2,1)S(1)} %copy-done.10, ...), custom_call_target="tpu_custom_call" | custom-call | flops 199999995904 | bytes 1 | tf_op jit(solution)/shard_map/forward_other/pallas_call | solution.py:227
  93.8 0.2 collective-permute-start.1
  94.1 6.0 %product_out.1.total_ref = f32[384,4096]{1,0:T(8,128)} custom-call(bf16[384,384]{1,0:T(8,128)(2,1)S(1)} %get-tuple-element.55.hidden_ref, bf16[1,384,4096]{2,1,0:T(8,128)(2,1)} %down_ref.9), custom_call_target="tpu_custom_call" | custom-call | flops 199999995904 | bytes 1 | tf_op jit(solution)/shard_map/product_out/pallas_call | solution.py:315
  100.0 0.9 pad_maximum_fusion
  101.0 6.2 %to_lines.2 = bf16[1536,1024]{1,0:T(8,128)(2,1)} custom-call(f32[384,4096]{1,0:T(8,128)} %product_out.1.total_ref, bf16[384,4096]{1,0:T(8,128)(2,1)} %collective-permute-done.1.arrived_ref, bf16[192,192]{1,0:T(8,128)(2,1)S(1)} %copy-done.5), custom_call_target="tpu_custom_call" | custom-call | flops 1 | bytes 1 | tf_op jit(solution)/shard_map/to_lines/pallas_call | solution.py:367
  107.2 3.9 %all-to-all-done.1 = bf16[64,24,1024]{2,1,0:T(8,128)(2,1)} async-done(((bf16[64,24,1024]{2,1,0:T(8,128)(2,1)}), bf16[64,24,1024]{2,1,0:T(8,128)(2,1)}, u32[]{:S(2)}, u32[]{:S(2)}) %all-to-all-start.1) | async-done | bytes 3145760 | tf_op jit(solution)/shard_map/all_to_all | solution.py:62
  111.1 9.2 %all-to-all-start.2 = ((bf16[64,24,1024]{2,1,0:T(8,128)(2,1)}), bf16[64,24,1024]{2,1,0:T(8,128)(2,1)}, u32[]{:S(2)}, u32[]{:S(2)}) async-start(bf16[64,24,1024]{2,1,0:T(8,128)(2,1)} %bitcast.36), calls=%async_computation.2 | async-start | bytes 6291456 | tf_op jit(solution)/shard_map/all_to_all | solution.py:62
  120.3 1.1 copy-done.12
  121.3 1.1 copy-done.14
  122.4 8.2 %backward_own.1 = (bf16[384,4096]{1,0:T(8,128)(2,1)}, bf16[384,384]{1,0:T(8,128)(2,1)S(1)}, bf16[384,384]{1,0:T(8,128)(2,1)S(1)}) custom-call(bf16[1536,1024]{1,0:T(8,128)(2,1)} %bitcast.11.lines_ref, bf16[192,192]{1,0:T(8,128)(2,1)S(1)} %copy-done.10, bf16[1,384,4096]{2,1,0:T(8,128)(2,1)} %down_ref.9, f32[384,384]{1,0:T(8,128)S(1)} %copy-done.12, ...), custom_call_target="tpu_custom_call" | custom-call | flops 199999995904 | bytes 1 | tf_op jit(solution)/shard_map/backward_own/pallas_call | solution.py:287
  130.6 14.2 %backward_other.1 = (bf16[384,4096]{1,0:T(8,128)(2,1)}, bf16[384,384]{1,0:T(8,128)(2,1)S(1)}, bf16[384,384]{1,0:T(8,128)(2,1)S(1)}, bf16[384,4096]{1,0:T(8,128)(2,1)}) custom-call(bf16[1536,1024]{1,0:T(8,128)(2,1)} %collective-permute-done.2.lines_ref, bf16[192,192]{1,0:T(8,128)(2,1)S(1)} %copy-done.10, bf16[1,384,4096]{2,1,0:T(8,128)(2,1)} %down_ref.9, ...), custom_call_target="tpu_custom_call" | custom-call | flops 199999995904 | bytes 1 | tf_op jit(solution)/shard_map/backward_other/pallas_call | solution.py:287
  144.8 0.2 collective-permute-start.3
  145.0 7.6 %product_in.1.total_ref = f32[384,4096]{1,0:T(8,128)} custom-call(bf16[384,384]{1,0:T(8,128)(2,1)S(1)} %get-tuple-element.64.dg_ref, bf16[384,384]{1,0:T(8,128)(2,1)S(1)} %get-tuple-element.65.du_ref, bf16[1,4096,384]{2,1,0:T(8,128)(2,1)} %gate_ref.9, bf16[1,4096,384]{2,1,0:T(8,128)(2,1)} %up_ref.9), custom_call_target="tpu_custom_call" | custom-call | flops 199999995904 | bytes 1 | tf_op jit(solution)/shard_map/product_in/pallas_call | solution.py:338
  152.7 0.9 pad_maximum_fusion.1
  153.6 6.3 %to_lines.3 = bf16[1536,1024]{1,0:T(8,128)(2,1)} custom-call(f32[384,4096]{1,0:T(8,128)} %product_in.1.total_ref, bf16[384,4096]{1,0:T(8,128)(2,1)} %collective-permute-done.3.arrived_ref, bf16[192,192]{1,0:T(8,128)(2,1)S(1)} %copy-done.6), custom_call_target="tpu_custom_call" | custom-call | flops 1 | bytes 1 | tf_op jit(solution)/shard_map/to_lines/pallas_call | solution.py:367
  159.9 1.8 all-to-all-done.2
  161.7 7.2 %fusion.4 = bf16[384,4096]{1,0:T(8,128)(2,1)} fusion(bf16[768,384]{1,0:T(8,128)(2,1)S(1)} %copy-done.21, bf16[384,4096]{1,0:T(8,128)(2,1)} %get-tuple-element.80, bf16[384,4096]{1,0:T(8,128)(2,1)} %get-tuple-element.79), kind=kOutput, calls=%fused_computation.4 | convolution fusion | flops 2430074880 | bytes 10027008 | tf_op jit(solution)/shard_map/dot_general | solution.py:26
  168.8 9.5 %all-to-all-start.3 = ((bf16[64,24,1024]{2,1,0:T(8,128)(2,1)}), bf16[64,24,1024]{2,1,0:T(8,128)(2,1)}, u32[]{:S(2)}, u32[]{:S(2)}) async-start(bf16[64,24,1024]{2,1,0:T(8,128)(2,1)} %bitcast.35), calls=%async_computation.3 | async-start | bytes 6291456 | tf_op jit(solution)/shard_map/all_to_all | solution.py:62
  178.5 7.9 %mix.1 = (bf16[128,4096]{1,0:T(8,128)(2,1)}, f32[128,2]{1,0:T(8,128)S(1)}) custom-call(bf16[512,1536]{1,0:T(8,128)(2,1)} %get-tuple-element.51.first_ref, bf16[512,1536]{1,0:T(8,128)(2,1)} %get-tuple-element.52.second_ref, bf16[1536,1024]{1,0:T(8,128)(2,1)} %bitcast.13.lines_ref, bf16[128,4096]{1,0:T(8,128)(2,1)S(1)} %copy-done.1, ...), custom_call_target="tpu_custom_call" | custom-call | flops 1 | bytes 1 | tf_op jit(solution)/shard_map/mix/pallas_call | solution.py:406
  186.5 0.2 multiply_reduce_fusion
  187.0 0.2 fusion.15
  187.3 0.8 fusion.12
  188.1 2.4 %constant_dynamic-update-slice_fusion.1 = bf16[768,4096]{1,0:T(8,128)(2,1)S(1)} fusion(bf16[384,4096]{1,0:T(8,128)(2,1)} %get-tuple-element.87), kind=kLoop, calls=%fused_computation.37 | loop fusion | bytes 6291456
  190.5 0.4 copy-done.15
  191.0 0.3 constant_dynamic-update-slice_fusion
  191.3 4.9 %fusion.8 = bf16[1,4096,384]{2,1,0:T(8,128)(2,1)} fusion(bf16[768,4096]{1,0:T(8,128)(2,1)S(1)} %constant_dynamic-update-slice_fusion, bf16[768,384]{1,0:T(8,128)(2,1)S(1)} %pad_maximum_fusion.2), kind=kOutput, calls=%fused_computation.8 | convolution fusion | flops 2417491968 | bytes 10027008 | tf_op jit(solution)/shard_map/dot_general | solution.py:26
  196.2 4.8 %fusion.7 = bf16[1,4096,384]{2,1,0:T(8,128)(2,1)} fusion(bf16[768,4096]{1,0:T(8,128)(2,1)S(1)} %constant_dynamic-update-slice_fusion, bf16[768,384]{1,0:T(8,128)(2,1)S(1)} %copy-done.20), kind=kOutput, calls=%fused_computation.7 | convolution fusion | flops 2417491968 | bytes 10027008 | tf_op jit(solution)/shard_map/dot_general | solution.py:26
  201.0 16.9 %all-to-all-done.3 = bf16[64,24,1024]{2,1,0:T(8,128)(2,1)} async-done(((bf16[64,24,1024]{2,1,0:T(8,128)(2,1)}), bf16[64,24,1024]{2,1,0:T(8,128)(2,1)}, u32[]{:S(2)}, u32[]{:S(2)}) %all-to-all-start.3) | async-done | bytes 3145760 | tf_op jit(solution)/shard_map/all_to_all | solution.py:62
  217.9 5.0 %unpack.1 = bf16[128,4096]{1,0:T(8,128)(2,1)} custom-call(bf16[512,1536]{1,0:T(8,128)(2,1)S(1)} %get-tuple-element.84.either_ref, bf16[1536,1024]{1,0:T(8,128)(2,1)} %bitcast.15.lines_ref), custom_call_target="tpu_custom_call" | custom-call | flops 1 | bytes 1 | tf_op jit(solution)/shard_map/unpack/pallas_call | solution.py:438
  (98 shorter events, 1.3 us)
Async XLA Ops:
  1.4 1.2 copy-start.2
  2.6 0.9 copy-start.3
  3.6 0.7 copy-start.7
  7.9 11.9 %copy-start.8 = (s32[128]{0:T(128)S(1)}, s32[128]{0:T(128)}, u32[]{:S(2)}) copy-start(s32[128]{0:T(128)} %param.16) | copy-start | bytes 1540
  7.9 11.9 %copy-start.37 = (s32[128,2]{0,1:T(2,128)S(1)}, s32[128,2]{0,1:T(2,128)}, u32[]{:S(2)}) copy-start(s32[128,2]{0,1:T(2,128)} %param.17) | copy-start | bytes 3076
  7.9 12.5 %copy-start.16 = (f32[128,128]{1,0:T(8,128)S(1)}, f32[128,128]{1,0:T(8,128)}, u32[]{:S(2)}) copy-start(f32[128,128]{1,0:T(8,128)} %param.15) | copy-start | bytes 196612
  7.9 14.0 %copy-start = (bf16[128,4096]{1,0:T(8,128)(2,1)S(1)}, bf16[128,4096]{1,0:T(8,128)(2,1)}, u32[]{:S(2)}) copy-start(bf16[128,4096]{1,0:T(8,128)(2,1)} %grad_ref.1) | copy-start | bytes 3145732
  7.9 14.0 %copy-start.4 = (bf16[384,192]{1,0:T(8,128)(2,1)S(1)}, bf16[384,192]{1,0:T(8,128)(2,1)}, u32[]{:S(2)}) copy-start(bf16[384,192]{1,0:T(8,128)(2,1)} %constant.48.clone.spread_ref) | copy-start | bytes 442372
  7.9 51.6 %all-to-all-start = ((bf16[64,24,1024]{2,1,0:T(8,128)(2,1)}), bf16[64,24,1024]{2,1,0:T(8,128)(2,1)}, u32[]{:S(2)}, u32[]{:S(2)}) async-start(bf16[64,24,1024]{2,1,0:T(8,128)(2,1)} %bitcast.37), calls=%async_computation | async-start | bytes 6291456 | tf_op jit(solution)/shard_map/all_to_all | solution.py:62
  19.8 6.9 %copy-start.30 = (s32[1536]{0:T(1024)S(1)}, s32[1536]{0:T(1024)}, u32[]{:S(2)}) copy-start(s32[1536]{0:T(1024)} %constant.55) | copy-start | bytes 18436
  19.8 0.6 copy-start.28
  20.7 5.9 %copy-start.22 = (f32[128]{0:T(128)}, f32[128]{0:T(128)S(1)}, u32[]{:S(2)}) copy-start(f32[128]{0:T(128)S(1)} %reduce_max.18) | copy-start | bytes 1540
  20.9 5.8 %copy-start.18 = (f32[128,2]{1,0:T(8,128)}, f32[128,2]{1,0:T(8,128)S(1)}, u32[]{:S(2)}) copy-start(f32[128,2]{1,0:T(8,128)S(1)} %copy.28) | copy-start | bytes 3076
  20.9 0.6 copy-start.33
  21.0 5.6 %copy-start.24 = (f32[128]{0:T(128)}, f32[128]{0:T(128)S(1)}, u32[]{:S(2)}) copy-start(f32[128]{0:T(128)S(1)} %exponential_reduce_fusion) | copy-start | bytes 1540
  21.5 5.2 %copy-start.35 = (f32[128]{0:T(128)}, f32[128]{0:T(128)S(1)}, u32[]{:S(2)}) copy-start(f32[128]{0:T(128)S(1)} %fusion.16) | copy-start | bytes 1540
  21.7 5.0 %copy-start.26 = (f32[128]{0:T(128)}, f32[128]{0:T(128)S(1)}, u32[]{:S(2)}) copy-start(f32[128]{0:T(128)S(1)} %fusion.13) | copy-start | bytes 1540
  21.7 5.0 %copy-start.31 = (pred[128]{0:T(512)(128)(4,1)}, pred[128]{0:T(512)(128)(4,1)S(1)}, u32[]{:S(2)}) copy-start(pred[128]{0:T(512)(128)(4,1)S(1)} %broadcast_compare_fusion) | copy-start | bytes 388
  59.5 20.8 %collective-permute-start = (bf16[1536,1024]{1,0:T(8,128)(2,1)}, bf16[1536,1024]{1,0:T(8,128)(2,1)}, u32[]{:S(2)}, u32[]{:S(2)}) collective-permute-start(bf16[1536,1024]{1,0:T(8,128)(2,1)} %bitcast.2.lines_ref), channel_id=1, source_target_pairs={{0,1},{1,0},{2,3},{3,2},{4,5},{5,4},{6,7},{7,6},{8,9},{9,8},{10,11... | collective-permute-start | bytes 9437192 | tf_op jit(solution)/shard_map/ppermute | solution.py:67
  59.5 10.2 %copy-start.10 = (bf16[192,192]{1,0:T(8,128)(2,1)S(1)}, bf16[192,192]{1,0:T(8,128)(2,1)}, u32[]{:S(2)}) copy-start(bf16[192,192]{1,0:T(8,128)(2,1)} %constant.50.clone.order_ref) | copy-start | bytes 221188
  59.5 51.5 %all-to-all-start.1 = ((bf16[64,24,1024]{2,1,0:T(8,128)(2,1)}), bf16[64,24,1024]{2,1,0:T(8,128)(2,1)}, u32[]{:S(2)}, u32[]{:S(2)}) async-start(bf16[64,24,1024]{2,1,0:T(8,128)(2,1)} %bitcast.34), calls=%async_computation.1 | async-start | bytes 6291456 | tf_op jit(solution)/shard_map/all_to_all | solution.py:62
  79.5 0.8 copy-start.13
  80.3 13.5 %copy-start.11 = (f32[384,384]{1,0:T(8,128)}, f32[384,384]{1,0:T(8,128)S(1)}, u32[]{:S(2)}) copy-start(f32[384,384]{1,0:T(8,128)S(1)} %get-tuple-element.60.g_ref) | copy-start | bytes 1769476
  93.8 7.1 %collective-permute-start.1 = (bf16[384,4096]{1,0:T(8,128)(2,1)}, bf16[384,4096]{1,0:T(8,128)(2,1)}, u32[]{:S(2)}, u32[]{:S(2)}) collective-permute-start(bf16[384,4096]{1,0:T(8,128)(2,1)} %get-tuple-element.57), channel_id=1, source_target_pairs={{0,1},{1,0},{2,3},{3,2},{4,5},{5,4},{6,7},{7,6},{8,9},{9,8},{10,11... | collective-permute-start | bytes 9437192 | tf_op jit(solution)/shard_map/ppermute | solution.py:67
  94.1 6.9 %copy-start.5 = (bf16[192,192]{1,0:T(8,128)(2,1)S(1)}, bf16[192,192]{1,0:T(8,128)(2,1)}, u32[]{:S(2)}) copy-start(bf16[192,192]{1,0:T(8,128)(2,1)} %constant.49.clone.order_ref) | copy-start | bytes 221188
  111.1 19.5 %collective-permute-start.2 = (bf16[1536,1024]{1,0:T(8,128)(2,1)}, bf16[1536,1024]{1,0:T(8,128)(2,1)}, u32[]{:S(2)}, u32[]{:S(2)}) collective-permute-start(bf16[1536,1024]{1,0:T(8,128)(2,1)} %bitcast.11.lines_ref), channel_id=1, source_target_pairs={{0,1},{1,0},{2,3},{3,2},{4,5},{5,4},{6,7},{7,6},{8,9},{9,8},{10,11... | collective-permute-start | bytes 9437192 | tf_op jit(solution)/shard_map/ppermute | solution.py:67
  111.1 50.6 %all-to-all-start.2 = ((bf16[64,24,1024]{2,1,0:T(8,128)(2,1)}), bf16[64,24,1024]{2,1,0:T(8,128)(2,1)}, u32[]{:S(2)}, u32[]{:S(2)}) async-start(bf16[64,24,1024]{2,1,0:T(8,128)(2,1)} %bitcast.36), calls=%async_computation.2 | async-start | bytes 6291456 | tf_op jit(solution)/shard_map/all_to_all | solution.py:62
  120.3 1.1 copy-start.12
  121.3 1.1 copy-start.14
  144.8 8.8 %collective-permute-start.3 = (bf16[384,4096]{1,0:T(8,128)(2,1)}, bf16[384,4096]{1,0:T(8,128)(2,1)}, u32[]{:S(2)}, u32[]{:S(2)}) collective-permute-start(bf16[384,4096]{1,0:T(8,128)(2,1)} %get-tuple-element.69), channel_id=1, source_target_pairs={{0,1},{1,0},{2,3},{3,2},{4,5},{5,4},{6,7},{7,6},{8,9},{9,8},{10,11... | collective-permute-start | bytes 9437192 | tf_op jit(solution)/shard_map/ppermute | solution.py:67
  145.0 8.6 %copy-start.6 = (bf16[192,192]{1,0:T(8,128)(2,1)S(1)}, bf16[192,192]{1,0:T(8,128)(2,1)}, u32[]{:S(2)}) copy-start(bf16[192,192]{1,0:T(8,128)(2,1)} %constant.49.clone.order_ref) | copy-start | bytes 221188
  153.6 8.1 %copy-start.21 = (bf16[768,384]{1,0:T(8,128)(2,1)S(1)}, bf16[768,384]{1,0:T(8,128)(2,1)}, u32[]{:S(2)}) copy-start(bf16[768,384]{1,0:T(8,128)(2,1)} %pad_maximum_fusion) | copy-start | bytes 1769476
  168.8 9.6 %copy-start.1 = (bf16[128,4096]{1,0:T(8,128)(2,1)S(1)}, bf16[128,4096]{1,0:T(8,128)(2,1)}, u32[]{:S(2)}) copy-start(bf16[128,4096]{1,0:T(8,128)(2,1)} %grad_ref.1) | copy-start | bytes 3145732
  168.8 49.1 %all-to-all-start.3 = ((bf16[64,24,1024]{2,1,0:T(8,128)(2,1)}), bf16[64,24,1024]{2,1,0:T(8,128)(2,1)}, u32[]{:S(2)}, u32[]{:S(2)}) async-start(bf16[64,24,1024]{2,1,0:T(8,128)(2,1)} %bitcast.35), calls=%async_computation.3 | async-start | bytes 6291456 | tf_op jit(solution)/shard_map/all_to_all | solution.py:62
  178.4 8.1 %copy-start.19 = (f32[128,2]{1,0:T(8,128)S(1)}, f32[128,2]{1,0:T(8,128)}, u32[]{:S(2)}) copy-start(f32[128,2]{1,0:T(8,128)} %copy-done.18) | copy-start | bytes 3076
  178.4 8.1 %copy-start.25 = (f32[128]{0:T(128)S(1)}, f32[128]{0:T(128)}, u32[]{:S(2)}) copy-start(f32[128]{0:T(128)} %copy-done.24) | copy-start | bytes 1540
  178.4 8.1 %copy-start.27 = (f32[128]{0:T(128)S(1)}, f32[128]{0:T(128)}, u32[]{:S(2)}) copy-start(f32[128]{0:T(128)} %copy-done.26) | copy-start | bytes 1540
  178.4 8.0 %copy-start.32 = (pred[128]{0:T(512)(128)(4,1)S(1)}, pred[128]{0:T(512)(128)(4,1)}, u32[]{:S(2)}) copy-start(pred[128]{0:T(512)(128)(4,1)} %copy-done.31) | copy-start | bytes 388
  178.4 8.0 %copy-start.39 = (f32[128]{0:T(128)S(1)}, f32[128]{0:T(128)}, u32[]{:S(2)}) copy-start(f32[128]{0:T(128)} %multiply_divide_fusion.1) | copy-start | bytes 1540
  178.4 8.5 %copy-start.9 = (s32[128]{0:T(128)S(1)}, s32[128]{0:T(128)}, u32[]{:S(2)}) copy-start(s32[128]{0:T(128)} %param.16) | copy-start | bytes 1540
  178.5 8.5 %copy-start.17 = (f32[128,128]{1,0:T(8,128)S(1)}, f32[128,128]{1,0:T(8,128)}, u32[]{:S(2)}) copy-start(f32[128,128]{1,0:T(8,128)} %param.15) | copy-start | bytes 196612
  178.5 8.5 %copy-start.23 = (f32[128]{0:T(128)S(1)}, f32[128]{0:T(128)}, u32[]{:S(2)}) copy-start(f32[128]{0:T(128)} %copy-done.22) | copy-start | bytes 1540
  178.5 8.5 %copy-start.34 = (s32[128]{0:T(128)S(1)}, s32[128]{0:T(128)}, u32[]{:S(2)}) copy-start(s32[128]{0:T(128)} %copy-done.33) | copy-start | bytes 1540
  178.5 8.5 %copy-start.38 = (f32[128]{0:T(128)S(1)}, f32[128]{0:T(128)}, u32[]{:S(2)}) copy-start(f32[128]{0:T(128)} %multiply_divide_fusion) | copy-start | bytes 1540
  178.5 8.7 %copy-start.29 = (s32[128,2]{0,1:T(2,128)S(1)}, s32[128,2]{0,1:T(2,128)}, u32[]{:S(2)}) copy-start(s32[128,2]{0,1:T(2,128)} %copy-done.28) | copy-start | bytes 3076
  178.5 8.8 %copy-start.36 = (f32[128]{0:T(128)S(1)}, f32[128]{0:T(128)}, u32[]{:S(2)}) copy-start(f32[128]{0:T(128)} %copy-done.35) | copy-start | bytes 1540
  188.1 2.8 %copy-start.15 = (bf16[384,4096]{1,0:T(8,128)(2,1)S(1)}, bf16[384,4096]{1,0:T(8,128)(2,1)}, u32[]{:S(2)}) copy-start(bf16[384,4096]{1,0:T(8,128)(2,1)} %get-tuple-element.88) | copy-start | bytes 9437188
  191.3 4.9 %copy-start.20 = (bf16[768,384]{1,0:T(8,128)(2,1)S(1)}, bf16[768,384]{1,0:T(8,128)(2,1)}, u32[]{:S(2)}) copy-start(bf16[768,384]{1,0:T(8,128)(2,1)} %pad_maximum_fusion.1) | copy-start | bytes 1769476
where the time goes:
time: 225 us; the launch traced here: 223 us
  Pallas kernels  92 us (41%)
  waiting for transfers between devices  52.9 us (24%)
  starting transfers between devices  41.2 us (18%)
  matrix products  16.9 us (8%)
  local copies, waits for them, and re-layouts  10.9 us (5%)
  other arithmetic  7.96 us (4%)
    all_to_all x4, waiting for transfers between devices, exchange(): out = lax.all_to_all(blocks, WIDE, split_axis=0, concat_axis=0, tiled=True)  52.9 us
    all_to_all x4, starting transfers between devices, exchange(): out = lax.all_to_all(blocks, WIDE, split_axis=0, concat_axis=0, tiled=True)  40.8 us
    pallas_call x2, Pallas kernels, forward(): call(forward_kernel, 'forward_own' if own else 'forward_other', outs, BUS...  23.3 us
    pallas_call x2, Pallas kernels, backward(): call(backward_kernel, 'backward_own' if own else 'backward_other', outs,...  22.4 us
    dot_general x3, matrix products, dot(): return lax.dot_general(a, b, (dims, ((), ())), preferred_element_type=F32)  16.9 us
    pallas_call x2, Pallas kernels, to_lines(): call(lines_kernel, 'to_lines', jax.ShapeDtypeStruct((half * CUT, width),...  12.5 us
    unnamed x82, local copies, waits for them, and re-layouts  10.4 us
    pallas_call x1, Pallas kernels, mix(): call(mix_kernel, 'mix', (jax.ShapeDtypeStruct(grad_out.shape, BF16), jax....  7.94 us
  transfers between devices with their start and end apart: 8, of which 4 were waited for; matrix products, arithmetic and copies ran while one was open for 9% of the time, Pallas kernels for 37%

commit v1 on v0

--- a/solution.py
+++ b/solution.py
@@ -79,7 +79,15 @@
     return jnp.concatenate([ref[team, j * width : (j + 1) * width] for j in range(CUT)], axis=0)
 
 
-def slots_kernel(expert_total, group_ref, expert_ref, rows_ref, spread_ref, out_ref, slot_ref, held):
+def spread_matrix(shape):
+    copies = shape[0] // shape[1]
+    line = lax.broadcasted_iota(jnp.int32, (shape[0], 1), 0)
+    member, chunk, slot = line // (copies * LINES), line // CAP % CUT, line % CAP
+    wanted = (chunk * TEAM + member) * CAP + slot
+    return (wanted == lax.broadcasted_iota(jnp.int32, shape, 1)).astype(F32).astype(BF16)
+
+
+def slots_kernel(expert_total, group_ref, expert_ref, rows_ref, out_ref, slot_ref, held, spread):
     team = pl.program_id(0)
     width = out_ref.shape[1]
 
@@ -110,15 +118,16 @@
             picked = match if picked is None else picked | match
         picked = picked.astype(F32).astype(BF16)
         held[...] = dot(picked, rows_ref[...]).astype(BF16)
+        spread[...] = spread_matrix(spread.shape)
 
     start = pl.multiple_of(team * (TEAM * CAP), 16)
-    out_ref[...] = dot(spread_ref[...], gathered(held, start, width)).astype(BF16)
-
-
-def pack_tokens(group_id, expert_ids, tokens, spread, expert_total):
+    out_ref[...] = dot(spread[...], gathered(held, start, width)).astype(BF16)
+
+
+def pack_tokens(group_id, expert_ids, tokens, copies, expert_total):
     count, model_width = tokens.shape
     width = model_width // CUT
-    teams, lines = expert_total // TEAM, spread.shape[0]
+    teams, lines = expert_total // TEAM, TEAM * copies * LINES
     return call(
         functools.partial(slots_kernel, expert_total),
         "pack_tokens",
@@ -131,11 +140,13 @@
             whole((1, count)),
             whole(expert_ids.shape),
             whole(tokens.shape),
-            whole(spread.shape),
         ],
         out_specs=(pl.BlockSpec((lines, width), lambda t: (t, 0)), whole((2, count))),
-        scratch_shapes=[pltpu.VMEM((expert_total * CAP, model_width), BF16)],
-    )(group_id[None], expert_ids, tokens, spread)
+        scratch_shapes=[
+            pltpu.VMEM((expert_total * CAP, model_width), BF16),
+            pltpu.VMEM((lines, TEAM * LINES), BF16),
+        ],
+    )(group_id[None], expert_ids, tokens)
 
 
 def grads_kernel(slot_ref, weight_ref, rows_ref, spread_ref, out_ref, held):
@@ -378,6 +389,49 @@
     )(total, arrived, order)
 
 
+def columns_grad_kernel(own, other, dg_own, dg_other, du_own, du_other, gate_ref, up_ref):
+    rows_own, rows_other = own[...].T, other[...].T
+    gate_ref[...] = (dot(rows_own, dg_own[...]) + dot(rows_other, dg_other[...])).astype(BF16)
+    up_ref[...] = (dot(rows_own, du_own[...]) + dot(rows_other, du_other[...])).astype(BF16)
+
+
+def columns_grad(rows, dg, du):
+    half, model_width = rows[0].shape
+    units = dg[0].shape[1]
+    piece = model_width // 8
+    rows_spec = pl.BlockSpec((half, piece), lambda k: (0, k))
+    out_spec = pl.BlockSpec((None, piece, units), lambda k: (0, k, 0))
+    return call(
+        columns_grad_kernel,
+        "columns_grad",
+        [jax.ShapeDtypeStruct((1, model_width, units), BF16)] * 2,
+        grid=(model_width // piece,),
+        in_specs=[rows_spec] * 2 + [whole((half, units))] * 4,
+        out_specs=[out_spec] * 2,
+    )(*rows, *dg, *du)
+
+
+def rows_grad_kernel(hidden_own, hidden_other, own, other, down_ref):
+    down_ref[...] = (
+        dot(hidden_own[...].T, own[...]) + dot(hidden_other[...].T, other[...])
+    ).astype(BF16)
+
+
+def rows_grad(hidden, grads):
+    half, model_width = grads[0].shape
+    units = hidden[0].shape[1]
+    piece = model_width // CUT
+    rows_spec = pl.BlockSpec((half, piece), lambda k: (0, k))
+    return call(
+        rows_grad_kernel,
+        "rows_grad",
+        jax.ShapeDtypeStruct((1, units, model_width), BF16),
+        grid=(CUT,),
+        in_specs=[whole((half, units))] * 2 + [rows_spec] * 2,
+        out_specs=pl.BlockSpec((None, units, piece), lambda k: (0, 0, k)),
+    )(*hidden, *grads)
+
+
 def mix_kernel(first_ref, second_ref, lines_ref, grad_ref, weight_ref, mixed_ref, score_ref):
     step = pl.program_id(0)
     count, piece = grad_ref.shape[0], lines_ref.shape[1]
@@ -454,7 +508,7 @@
     order = order_matrix(1)
     to_travel, in_order = jnp.asarray(order), jnp.asarray(order.T)
 
-    tokens_out, slot = pack_tokens(group_id, expert_ids, tokens, spread, expert_total)
+    tokens_out, slot = pack_tokens(group_id, expert_ids, tokens, sides, expert_total)
 
     inside = group_id < expert_total // GSIZE
     chosen = group_id[:, None] * GSIZE + expert_ids
@@ -499,29 +553,25 @@
         lines_other, in_order, w_down, gate_other, up_other, w_gate, w_up, False
     )
     in_lines = to_lines(product_in(dg_own, du_own, w_gate, w_up), swap(in_other), to_travel)
-    in_lines, out_back, *halves = lax.optimization_barrier(
+    in_lines, out_back, rows, grads, hidden, dg, du = lax.optimization_barrier(
         (
             in_lines,
             out_back,
             (rows_own, rows_other),
             (grads_own, grads_other),
-            jnp.concatenate([hidden_own, hidden_other]),
-            jnp.concatenate([dg_own, dg_other]),
-            jnp.concatenate([du_own, du_other]),
+            (hidden_own, hidden_other),
+            (dg_own, dg_other),
+            (du_own, du_other),
         )
     )
     in_back = exchange(in_lines)
 
-    rows, grads = (jnp.concatenate(pair) for pair in halves[:2])
-    hidden, dg, du = halves[2:]
-    grad_gate = dot(rows, dg, ((0,), (0,))).astype(BF16)
-    grad_up = dot(rows, du, ((0,), (0,))).astype(BF16)
-    grad_down = dot(hidden, grads, ((0,), (0,))).astype(BF16)
-    grad_down, out_back = lax.optimization_barrier((grad_down, out_back))
+    grad_gate, grad_up = columns_grad(rows, dg, du)
+    grad_down = rows_grad(hidden, grads)
     mixed, scores = mix(first, second, out_back, grad_out, weights)
     d_logits = pull_back(scores)[0]
     d_tokens = unpack(either, in_back, count)
-    return (mixed, d_tokens, d_logits, grad_gate[None], grad_up[None], grad_down[None])
+    return (mixed, d_tokens, d_logits, grad_gate, grad_up, grad_down)
 
 
 def solution(mesh):

time: 225 us -> 217 us (0.964)
  Pallas kernels: 92 us -> 111 us
  matrix products: 16.9 us -> 0 us
  local copies, waits for them, and re-layouts: 10.9 us -> 6.3 us
  other arithmetic: 7.96 us -> 5.02 us
    pallas_call x0 -> x2, Pallas kernels: none -> 18.7 us  [the longest x1 11.5 us: columns_grad(): call(columns_grad_kernel, 'columns_grad', [jax.ShapeDtypeStruct((1, model...]
    dot_general x3 -> x0, matrix products: 16.9 us -> none  [dot(): return lax.dot_general(a, b, (dims, ((), ())), preferred_element_type=F32)]
    unnamed x82 -> x77, local copies, waits for them, and re-layouts: 10.4 us -> 6.06 us
  transfers between devices with their start and end apart: 8 -> 8, of which waited for: 4 -> 4; matrix products, arithmetic and copies ran while one was open for 9% -> 2% of each run, Pallas kernels for 37% -> 47%
where the time goes in v1:
time: 217 us; the launch traced here: 216 us
  Pallas kernels  111 us (51%)
  waiting for transfers between devices  50.9 us (23%)
  starting transfers between devices  41.2 us (19%)
  local copies, waits for them, and re-layouts  6.3 us (3%)
  other arithmetic  5.02 us (2%)
    all_to_all x4, waiting for transfers between devices, exchange(): out = lax.all_to_all(blocks, WIDE, split_axis=0, concat_axis=0, tiled=True)  50.9 us
    all_to_all x4, starting transfers between devices, exchange(): out = lax.all_to_all(blocks, WIDE, split_axis=0, concat_axis=0, tiled=True)  40.8 us
    pallas_call x2, Pallas kernels, forward(): call(forward_kernel, 'forward_own' if own else 'forward_other', outs, BUS...  23.2 us
    pallas_call x2, Pallas kernels, backward(): call(backward_kernel, 'backward_own' if own else 'backward_other', outs,...  22.5 us
    pallas_call x2, Pallas kernels, to_lines(): call(lines_kernel, 'to_lines', jax.ShapeDtypeStruct((half * CUT, width),...  12.5 us
    pallas_call x1, Pallas kernels, columns_grad(): call(columns_grad_kernel, 'columns_grad', [jax.ShapeDtypeStruct((1, model...  11.5 us
    pallas_call x1, Pallas kernels, mix(): call(mix_kernel, 'mix', (jax.ShapeDtypeStruct(grad_out.shape, BF16), jax....  7.93 us
    pallas_call x1, Pallas kernels, product_in(): call(in_kernel, 'product_in', jax.ShapeDtypeStruct((half, model_width), F...  7.77 us
  transfers between devices with their start and end apart: 8, of which 4 were waited for; matrix products, arithmetic and copies ran while one was open for 2% of the time, Pallas kernels for 47%

profile of v1, /device:TPU:0, one launch (start us, length us, event | category | flops | bytes accessed | tf_op | source)
XLA Modules:
  0.0 215.6 jit_solution(9917766127304765933)
XLA Ops:
  0.6 0.8 copy.27.expert_ref
  1.4 1.2 copy-done.2
  2.6 0.7 copy-done.8
  3.3 3.8 %pack_tokens.1 = (bf16[1536,1024]{1,0:T(8,128)(2,1)}, s32[2,128]{1,0:T(2,128)S(1)}) custom-call(s32[1,128]{1,0:T(1,128)S(1)} %bitcast.23, s32[128,2]{1,0:T(8,128)S(1)} %copy.27.expert_ref, bf16[128,4096]{1,0:T(8,128)(2,1)S(1)} %copy-done.2), custom_call_target="tpu_custom_call" | custom-call | flops 1 | bytes 1 | tf_op jit(solution)/shard_map/pack_tokens/pallas_call | solution.py:131
  7.1 11.9 %all-to-all-start = ((bf16[64,24,1024]{2,1,0:T(8,128)(2,1)}), bf16[64,24,1024]{2,1,0:T(8,128)(2,1)}, u32[]{:S(2)}, u32[]{:S(2)}) async-start(bf16[64,24,1024]{2,1,0:T(8,128)(2,1)} %bitcast.27), calls=%async_computation | async-start | bytes 6291456 | tf_op jit(solution)/shard_map/all_to_all | solution.py:62
  19.0 0.1 reduce_max.18
  19.2 0.2 select_reduce_fusion.1
  19.4 0.4 copy-done.28
  19.8 0.1 copy.28
  19.9 0.1 exponential_reduce_fusion
  20.0 0.2 fusion.7
  20.2 0.2 copy-done.33
  20.4 0.2 fusion.4
  20.6 0.1 fusion.8
  20.7 0.1 copy.30.weight_ref
  20.8 3.5 %pack_grads.1 = bf16[1536,1024]{1,0:T(8,128)(2,1)} custom-call(s32[2,128]{1,0:T(2,128)S(1)} %get-tuple-element.53.slot_ref, f32[2,128]{1,0:T(2,128)S(1)} %copy.30.weight_ref, bf16[128,4096]{1,0:T(8,128)(2,1)S(1)} %copy-done, bf16[384,192]{1,0:T(8,128)(2,1)S(1)} %copy-done.7), custom_call_target="tpu_custom_call" | custom-call | flops 1 | bytes 1 | tf_op jit(solution)/shard_map/pack_grads/pallas_call | solution.py:174
  24.4 2.5 %fusion = (bf16[512,1536]{1,0:T(8,128)(2,1)S(1)}, bf16[512,1536]{1,0:T(8,128)(2,1)}, bf16[512,1536]{1,0:T(8,128)(2,1)}) fusion(s32[1536]{0:T(1024)S(1)} %copy-done.30, s32[512]{0:T(512)S(1)} %get-tuple-element.107, s32[512]{0:T(512)S(1)} %get-tuple-element.108), kind=kLoop, calls=%fused_computation.3 | loop fusion | flops 4718592 | bytes 4728832 | tf_op jit(solution)/shard_map/convert_element_type | solution.py:529
  26.8 31.9 %all-to-all-done = bf16[64,24,1024]{2,1,0:T(8,128)(2,1)} async-done(((bf16[64,24,1024]{2,1,0:T(8,128)(2,1)}), bf16[64,24,1024]{2,1,0:T(8,128)(2,1)}, u32[]{:S(2)}, u32[]{:S(2)}) %all-to-all-start) | async-done | bytes 3145760 | tf_op jit(solution)/shard_map/all_to_all | solution.py:62
  58.7 10.2 %all-to-all-start.1 = ((bf16[64,24,1024]{2,1,0:T(8,128)(2,1)}), bf16[64,24,1024]{2,1,0:T(8,128)(2,1)}, u32[]{:S(2)}, u32[]{:S(2)}) async-start(bf16[64,24,1024]{2,1,0:T(8,128)(2,1)} %bitcast.25), calls=%async_computation.1 | async-start | bytes 6291456 | tf_op jit(solution)/shard_map/all_to_all | solution.py:62
  68.9 9.8 %forward_own.1 = (bf16[384,4096]{1,0:T(8,128)(2,1)}, f32[384,384]{1,0:T(8,128)S(1)}, f32[384,384]{1,0:T(8,128)S(1)}, bf16[384,384]{1,0:T(8,128)(2,1)S(1)}) custom-call(bf16[1536,1024]{1,0:T(8,128)(2,1)} %bitcast.2.lines_ref, bf16[192,192]{1,0:T(8,128)(2,1)S(1)} %copy-done.11, bf16[1,4096,384]{2,1,0:T(8,128)(2,1)} %gate_ref.9, bf16[1,4096,384]{2,1,0:T(8,128)(2,1)} %up_ref.9, ...), custom_call_target="tpu_custom_call" | custom-call | flops 199999995904 | bytes 1 | tf_op jit(solution)/shard_map/forward_own/pallas_call | solution.py:238
  78.8 0.8 copy-done.16
  79.6 13.4 %forward_other.1 = (bf16[384,4096]{1,0:T(8,128)(2,1)}, f32[384,384]{1,0:T(8,128)S(1)}, f32[384,384]{1,0:T(8,128)S(1)}, bf16[384,384]{1,0:T(8,128)(2,1)S(1)}, bf16[384,4096]{1,0:T(8,128)(2,1)}) custom-call(bf16[1536,1024]{1,0:T(8,128)(2,1)} %collective-permute-done.lines_ref, bf16[192,192]{1,0:T(8,128)(2,1)S(1)} %copy-done.11, ...), custom_call_target="tpu_custom_call" | custom-call | flops 199999995904 | bytes 1 | tf_op jit(solution)/shard_map/forward_other/pallas_call | solution.py:238
  93.0 0.8 copy-done.12
  93.8 0.2 collective-permute-start.1
  94.0 6.1 %product_out.1.total_ref = f32[384,4096]{1,0:T(8,128)} custom-call(bf16[384,384]{1,0:T(8,128)(2,1)S(1)} %get-tuple-element.94.hidden_ref.hidden_own, bf16[1,384,4096]{2,1,0:T(8,128)(2,1)} %down_ref.9), custom_call_target="tpu_custom_call" | custom-call | flops 199999995904 | bytes 1 | tf_op jit(solution)/shard_map/product_out/pallas_call | solution.py:326
  100.1 6.2 %to_lines.2 = bf16[1536,1024]{1,0:T(8,128)(2,1)} custom-call(f32[384,4096]{1,0:T(8,128)} %product_out.1.total_ref, bf16[384,4096]{1,0:T(8,128)(2,1)} %collective-permute-done.1.arrived_ref, bf16[192,192]{1,0:T(8,128)(2,1)S(1)} %copy-done.3), custom_call_target="tpu_custom_call" | custom-call | flops 1 | bytes 1 | tf_op jit(solution)/shard_map/to_lines/pallas_call | solution.py:378
  106.4 3.9 %all-to-all-done.1 = bf16[64,24,1024]{2,1,0:T(8,128)(2,1)} async-done(((bf16[64,24,1024]{2,1,0:T(8,128)(2,1)}), bf16[64,24,1024]{2,1,0:T(8,128)(2,1)}, u32[]{:S(2)}, u32[]{:S(2)}) %all-to-all-start.1) | async-done | bytes 3145760 | tf_op jit(solution)/shard_map/all_to_all | solution.py:62
  110.3 9.2 %all-to-all-start.2 = ((bf16[64,24,1024]{2,1,0:T(8,128)(2,1)}), bf16[64,24,1024]{2,1,0:T(8,128)(2,1)}, u32[]{:S(2)}, u32[]{:S(2)}) async-start(bf16[64,24,1024]{2,1,0:T(8,128)(2,1)} %bitcast.26), calls=%async_computation.2 | async-start | bytes 6291456 | tf_op jit(solution)/shard_map/all_to_all | solution.py:62
  119.5 1.1 copy-done.17
  120.6 8.3 %backward_own.1 = (bf16[384,4096]{1,0:T(8,128)(2,1)}, bf16[384,384]{1,0:T(8,128)(2,1)S(1)}, bf16[384,384]{1,0:T(8,128)(2,1)S(1)}) custom-call(bf16[1536,1024]{1,0:T(8,128)(2,1)} %bitcast.11.lines_ref, bf16[192,192]{1,0:T(8,128)(2,1)S(1)} %copy-done.11, bf16[1,384,4096]{2,1,0:T(8,128)(2,1)} %down_ref.9, f32[384,384]{1,0:T(8,128)S(1)} %get-tuple-element.63.g_ref, ...), custom_call_target="tpu_custom_call" | custom-call | flops 199999995904 | bytes 1 | tf_op jit(solution)/shard_map/backward_own/pallas_call | solution.py:298
  128.8 14.2 %backward_other.1 = (bf16[384,4096]{1,0:T(8,128)(2,1)}, bf16[384,384]{1,0:T(8,128)(2,1)S(1)}, bf16[384,384]{1,0:T(8,128)(2,1)S(1)}, bf16[384,4096]{1,0:T(8,128)(2,1)}) custom-call(bf16[1536,1024]{1,0:T(8,128)(2,1)} %collective-permute-done.2.lines_ref, bf16[192,192]{1,0:T(8,128)(2,1)S(1)} %copy-done.11, bf16[1,384,4096]{2,1,0:T(8,128)(2,1)} %down_ref.9, ...), custom_call_target="tpu_custom_call" | custom-call | flops 199999995904 | bytes 1 | tf_op jit(solution)/shard_map/backward_other/pallas_call | solution.py:298
  143.1 0.2 collective-permute-start.3
  143.3 7.8 %product_in.1.total_ref = f32[384,4096]{1,0:T(8,128)} custom-call(bf16[384,384]{1,0:T(8,128)(2,1)S(1)} %get-tuple-element.88.dg_ref.dg_own, bf16[384,384]{1,0:T(8,128)(2,1)S(1)} %get-tuple-element.90.du_ref.du_own, bf16[1,4096,384]{2,1,0:T(8,128)(2,1)} %gate_ref.9, bf16[1,4096,384]{2,1,0:T(8,128)(2,1)} %up_ref.9), custom_call_target="tpu_custom_call" | custom-call | flops 199999995904 | bytes 1 | tf_op jit(solution)/shard_map/product_in/pallas_call | solution.py:349
  151.1 6.3 %to_lines.3 = bf16[1536,1024]{1,0:T(8,128)(2,1)} custom-call(f32[384,4096]{1,0:T(8,128)} %product_in.1.total_ref, bf16[384,4096]{1,0:T(8,128)(2,1)} %collective-permute-done.3.arrived_ref, bf16[192,192]{1,0:T(8,128)(2,1)S(1)} %copy-done.4), custom_call_target="tpu_custom_call" | custom-call | flops 1 | bytes 1 | tf_op jit(solution)/shard_map/to_lines/pallas_call | solution.py:378
  157.3 3.5 %all-to-all-done.2 = bf16[64,24,1024]{2,1,0:T(8,128)(2,1)} async-done(((bf16[64,24,1024]{2,1,0:T(8,128)(2,1)}), bf16[64,24,1024]{2,1,0:T(8,128)(2,1)}, u32[]{:S(2)}, u32[]{:S(2)}) %all-to-all-start.2) | async-done | bytes 3145760 | tf_op jit(solution)/shard_map/all_to_all | solution.py:62
  160.9 9.6 %all-to-all-start.3 = ((bf16[64,24,1024]{2,1,0:T(8,128)(2,1)}), bf16[64,24,1024]{2,1,0:T(8,128)(2,1)}, u32[]{:S(2)}, u32[]{:S(2)}) async-start(bf16[64,24,1024]{2,1,0:T(8,128)(2,1)} %bitcast.24), calls=%async_computation.3 | async-start | bytes 6291456 | tf_op jit(solution)/shard_map/all_to_all | solution.py:62
  170.5 0.1 multiply_select_fusion.weight_ref
  170.7 7.1 %rows_grad.1 = bf16[1,384,4096]{2,1,0:T(8,128)(2,1)} custom-call(bf16[384,384]{1,0:T(8,128)(2,1)S(1)} %copy-done.6, bf16[384,384]{1,0:T(8,128)(2,1)S(1)} %get-tuple-element.95.hidden_other, bf16[384,4096]{1,0:T(8,128)(2,1)} %get-tuple-element.96.own, bf16[384,4096]{1,0:T(8,128)(2,1)} %get-tuple-element.97.other), custom_call_target="tpu_custom_call" | custom-call | flops 1 | bytes 1 | tf_op jit(solution)/shard_map/rows_grad/pallas_call | solution.py:425
  177.8 7.9 %mix.1 = (bf16[128,4096]{1,0:T(8,128)(2,1)}, f32[128,2]{1,0:T(8,128)S(1)}) custom-call(bf16[512,1536]{1,0:T(8,128)(2,1)} %get-tuple-element.54.first_ref, bf16[512,1536]{1,0:T(8,128)(2,1)} %get-tuple-element.55.second_ref, bf16[1536,1024]{1,0:T(8,128)(2,1)} %bitcast.13.lines_ref, bf16[128,4096]{1,0:T(8,128)(2,1)S(1)} %copy-done.1, ...), custom_call_target="tpu_custom_call" | custom-call | flops 1 | bytes 1 | tf_op jit(solution)/shard_map/mix/pallas_call | solution.py:460
  185.8 11.5 %columns_grad.1 = (bf16[1,4096,384]{2,1,0:T(8,128)(2,1)}, bf16[1,4096,384]{2,1,0:T(8,128)(2,1)}) custom-call(bf16[384,4096]{1,0:T(8,128)(2,1)} %get-tuple-element.86.own, bf16[384,4096]{1,0:T(8,128)(2,1)} %get-tuple-element.87.other, bf16[384,384]{1,0:T(8,128)(2,1)S(1)} %get-tuple-element.88.dg_ref.dg_own, bf16[384,384]{1,0:T(8,128)(2,1)S(1)} %get-tuple-element.89.dg_other, ...), custom_call_target="tpu_custom_call" | custom-call | flops 1 | bytes 1 | tf_op jit(solution)/shard_map/columns_grad/pallas_call | solution.py:404
  197.3 0.2 multiply_reduce_fusion
  197.6 0.1 add_multiply_fusion
  197.7 0.1 copy.32
  197.8 0.2 fusion.6
  198.0 0.1 select_reduce_fusion
  198.2 0.8 fusion.3
  199.0 11.6 %all-to-all-done.3 = bf16[64,24,1024]{2,1,0:T(8,128)(2,1)} async-done(((bf16[64,24,1024]{2,1,0:T(8,128)(2,1)}), bf16[64,24,1024]{2,1,0:T(8,128)(2,1)}, u32[]{:S(2)}, u32[]{:S(2)}) %all-to-all-start.3) | async-done | bytes 3145760 | tf_op jit(solution)/shard_map/all_to_all | solution.py:62
  210.6 5.0 %unpack.1 = bf16[128,4096]{1,0:T(8,128)(2,1)} custom-call(bf16[512,1536]{1,0:T(8,128)(2,1)S(1)} %get-tuple-element.83.either_ref, bf16[1536,1024]{1,0:T(8,128)(2,1)} %bitcast.15.lines_ref), custom_call_target="tpu_custom_call" | custom-call | flops 1 | bytes 1 | tf_op jit(solution)/shard_map/unpack/pallas_call | solution.py:492
  (88 shorter events, 0.3 us)
Async XLA Ops:
  1.4 1.2 copy-start.2
  2.6 0.7 copy-start.8
  7.1 11.9 %copy-start.18 = (f32[128,128]{1,0:T(8,128)S(1)}, f32[128,128]{1,0:T(8,128)}, u32[]{:S(2)}) copy-start(f32[128,128]{1,0:T(8,128)} %param.15) | copy-start | bytes 196612
  7.1 12.0 %copy-start.9 = (s32[128]{0:T(128)S(1)}, s32[128]{0:T(128)}, u32[]{:S(2)}) copy-start(s32[128]{0:T(128)} %param.16) | copy-start | bytes 1540
  7.1 12.1 %copy-start.37 = (s32[128,2]{0,1:T(2,128)S(1)}, s32[128,2]{0,1:T(2,128)}, u32[]{:S(2)}) copy-start(s32[128,2]{0,1:T(2,128)} %param.17) | copy-start | bytes 3076
  7.1 13.7 %copy-start = (bf16[128,4096]{1,0:T(8,128)(2,1)S(1)}, bf16[128,4096]{1,0:T(8,128)(2,1)}, u32[]{:S(2)}) copy-start(bf16[128,4096]{1,0:T(8,128)(2,1)} %grad_ref.1) | copy-start | bytes 3145732
  7.1 13.7 %copy-start.7 = (bf16[384,192]{1,0:T(8,128)(2,1)S(1)}, bf16[384,192]{1,0:T(8,128)(2,1)}, u32[]{:S(2)}) copy-start(bf16[384,192]{1,0:T(8,128)(2,1)} %constant.48.clone.spread_ref) | copy-start | bytes 442372
  7.1 51.6 %all-to-all-start = ((bf16[64,24,1024]{2,1,0:T(8,128)(2,1)}), bf16[64,24,1024]{2,1,0:T(8,128)(2,1)}, u32[]{:S(2)}, u32[]{:S(2)}) async-start(bf16[64,24,1024]{2,1,0:T(8,128)(2,1)} %bitcast.27), calls=%async_computation | async-start | bytes 6291456 | tf_op jit(solution)/shard_map/all_to_all | solution.py:62
  19.0 5.4 %copy-start.30 = (s32[1536]{0:T(1024)S(1)}, s32[1536]{0:T(1024)}, u32[]{:S(2)}) copy-start(s32[1536]{0:T(1024)} %constant.55) | copy-start | bytes 18436
  19.1 5.2 %copy-start.22 = (f32[128]{0:T(128)}, f32[128]{0:T(128)S(1)}, u32[]{:S(2)}) copy-start(f32[128]{0:T(128)S(1)} %reduce_max.18) | copy-start | bytes 1540
  19.2 0.6 copy-start.28
  19.9 4.5 %copy-start.20 = (f32[128,2]{1,0:T(8,128)}, f32[128,2]{1,0:T(8,128)S(1)}, u32[]{:S(2)}) copy-start(f32[128,2]{1,0:T(8,128)S(1)} %copy.28) | copy-start | bytes 3076
  19.9 0.5 copy-start.33
  20.0 4.3 %copy-start.24 = (f32[128]{0:T(128)}, f32[128]{0:T(128)S(1)}, u32[]{:S(2)}) copy-start(f32[128]{0:T(128)S(1)} %exponential_reduce_fusion) | copy-start | bytes 1540
  20.4 3.9 %copy-start.35 = (f32[128]{0:T(128)}, f32[128]{0:T(128)S(1)}, u32[]{:S(2)}) copy-start(f32[128]{0:T(128)S(1)} %fusion.7) | copy-start | bytes 1540
  20.6 3.8 %copy-start.26 = (f32[128]{0:T(128)}, f32[128]{0:T(128)S(1)}, u32[]{:S(2)}) copy-start(f32[128]{0:T(128)S(1)} %fusion.4) | copy-start | bytes 1540
  20.6 3.7 %copy-start.31 = (pred[128]{0:T(512)(128)(4,1)}, pred[128]{0:T(512)(128)(4,1)S(1)}, u32[]{:S(2)}) copy-start(pred[128]{0:T(512)(128)(4,1)S(1)} %broadcast_compare_fusion) | copy-start | bytes 388
  58.7 20.8 %collective-permute-start = (bf16[1536,1024]{1,0:T(8,128)(2,1)}, bf16[1536,1024]{1,0:T(8,128)(2,1)}, u32[]{:S(2)}, u32[]{:S(2)}) collective-permute-start(bf16[1536,1024]{1,0:T(8,128)(2,1)} %bitcast.2.lines_ref), channel_id=1, source_target_pairs={{0,1},{1,0},{2,3},{3,2},{4,5},{5,4},{6,7},{7,6},{8,9},{9,8},{10,11... | collective-permute-start | bytes 9437192 | tf_op jit(solution)/shard_map/ppermute | solution.py:67
  58.7 10.2 %copy-start.11 = (bf16[192,192]{1,0:T(8,128)(2,1)S(1)}, bf16[192,192]{1,0:T(8,128)(2,1)}, u32[]{:S(2)}) copy-start(bf16[192,192]{1,0:T(8,128)(2,1)} %constant.50.clone.order_ref) | copy-start | bytes 221188
  58.7 51.5 %all-to-all-start.1 = ((bf16[64,24,1024]{2,1,0:T(8,128)(2,1)}), bf16[64,24,1024]{2,1,0:T(8,128)(2,1)}, u32[]{:S(2)}, u32[]{:S(2)}) async-start(bf16[64,24,1024]{2,1,0:T(8,128)(2,1)} %bitcast.25), calls=%async_computation.1 | async-start | bytes 6291456 | tf_op jit(solution)/shard_map/all_to_all | solution.py:62
  78.8 0.8 copy-start.16
  79.6 14.4 %copy-start.5 = (bf16[384,384]{1,0:T(8,128)(2,1)}, bf16[384,384]{1,0:T(8,128)(2,1)S(1)}, u32[]{:S(2)}) copy-start(bf16[384,384]{1,0:T(8,128)(2,1)S(1)} %get-tuple-element.94.hidden_ref.hidden_own) | copy-start | bytes 884740
  93.0 0.8 copy-start.12
  93.8 6.3 %copy-start.14 = (f32[384,384]{1,0:T(8,128)}, f32[384,384]{1,0:T(8,128)S(1)}, u32[]{:S(2)}) copy-start(f32[384,384]{1,0:T(8,128)S(1)} %get-tuple-element.71.u_ref) | copy-start | bytes 1769476
  93.8 6.3 %collective-permute-start.1 = (bf16[384,4096]{1,0:T(8,128)(2,1)}, bf16[384,4096]{1,0:T(8,128)(2,1)}, u32[]{:S(2)}, u32[]{:S(2)}) collective-permute-start(bf16[384,4096]{1,0:T(8,128)(2,1)} %get-tuple-element.60), channel_id=1, source_target_pairs={{0,1},{1,0},{2,3},{3,2},{4,5},{5,4},{6,7},{7,6},{8,9},{9,8},{10,11... | collective-permute-start | bytes 9437192 | tf_op jit(solution)/shard_map/ppermute | solution.py:67
  94.0 6.1 %copy-start.3 = (bf16[192,192]{1,0:T(8,128)(2,1)S(1)}, bf16[192,192]{1,0:T(8,128)(2,1)}, u32[]{:S(2)}) copy-start(bf16[192,192]{1,0:T(8,128)(2,1)} %constant.49.clone.order_ref) | copy-start | bytes 221188
  110.3 18.5 %collective-permute-start.2 = (bf16[1536,1024]{1,0:T(8,128)(2,1)}, bf16[1536,1024]{1,0:T(8,128)(2,1)}, u32[]{:S(2)}, u32[]{:S(2)}) collective-permute-start(bf16[1536,1024]{1,0:T(8,128)(2,1)} %bitcast.11.lines_ref), channel_id=1, source_target_pairs={{0,1},{1,0},{2,3},{3,2},{4,5},{5,4},{6,7},{7,6},{8,9},{9,8},{10,11... | collective-permute-start | bytes 9437192 | tf_op jit(solution)/shard_map/ppermute | solution.py:67
  110.3 50.6 %all-to-all-start.2 = ((bf16[64,24,1024]{2,1,0:T(8,128)(2,1)}), bf16[64,24,1024]{2,1,0:T(8,128)(2,1)}, u32[]{:S(2)}, u32[]{:S(2)}) async-start(bf16[64,24,1024]{2,1,0:T(8,128)(2,1)} %bitcast.26), calls=%async_computation.2 | async-start | bytes 6291456 | tf_op jit(solution)/shard_map/all_to_all | solution.py:62
  119.5 1.1 copy-start.17
  120.6 8.3 %copy-start.13 = (f32[384,384]{1,0:T(8,128)S(1)}, f32[384,384]{1,0:T(8,128)}, u32[]{:S(2)}) copy-start(f32[384,384]{1,0:T(8,128)} %copy-done.12) | copy-start | bytes 1769476
  120.6 8.3 %copy-start.15 = (f32[384,384]{1,0:T(8,128)S(1)}, f32[384,384]{1,0:T(8,128)}, u32[]{:S(2)}) copy-start(f32[384,384]{1,0:T(8,128)} %copy-done.14) | copy-start | bytes 1769476
  143.1 8.0 %collective-permute-start.3 = (bf16[384,4096]{1,0:T(8,128)(2,1)}, bf16[384,4096]{1,0:T(8,128)(2,1)}, u32[]{:S(2)}, u32[]{:S(2)}) collective-permute-start(bf16[384,4096]{1,0:T(8,128)(2,1)} %get-tuple-element.72), channel_id=1, source_target_pairs={{0,1},{1,0},{2,3},{3,2},{4,5},{5,4},{6,7},{7,6},{8,9},{9,8},{10,11... | collective-permute-start | bytes 9437192 | tf_op jit(solution)/shard_map/ppermute | solution.py:67
  143.3 7.8 %copy-start.4 = (bf16[192,192]{1,0:T(8,128)(2,1)S(1)}, bf16[192,192]{1,0:T(8,128)(2,1)}, u32[]{:S(2)}) copy-start(bf16[192,192]{1,0:T(8,128)(2,1)} %constant.49.clone.order_ref) | copy-start | bytes 221188
  160.9 9.6 %copy-start.25 = (f32[128]{0:T(128)S(1)}, f32[128]{0:T(128)}, u32[]{:S(2)}) copy-start(f32[128]{0:T(128)} %copy-done.24) | copy-start | bytes 1540
  160.9 9.6 %copy-start.36 = (f32[128]{0:T(128)S(1)}, f32[128]{0:T(128)}, u32[]{:S(2)}) copy-start(f32[128]{0:T(128)} %copy-done.35) | copy-start | bytes 1540
  160.9 9.6 %copy-start.21 = (f32[128,2]{1,0:T(8,128)S(1)}, f32[128,2]{1,0:T(8,128)}, u32[]{:S(2)}) copy-start(f32[128,2]{1,0:T(8,128)} %copy-done.20) | copy-start | bytes 3076
  160.9 9.6 %copy-start.27 = (f32[128]{0:T(128)S(1)}, f32[128]{0:T(128)}, u32[]{:S(2)}) copy-start(f32[128]{0:T(128)} %copy-done.26) | copy-start | bytes 1540
  160.9 9.7 %copy-start.32 = (pred[128]{0:T(512)(128)(4,1)S(1)}, pred[128]{0:T(512)(128)(4,1)}, u32[]{:S(2)}) copy-start(pred[128]{0:T(512)(128)(4,1)} %copy-done.31) | copy-start | bytes 388
  160.9 9.8 %copy-start.6 = (bf16[384,384]{1,0:T(8,128)(2,1)S(1)}, bf16[384,384]{1,0:T(8,128)(2,1)}, u32[]{:S(2)}) copy-start(bf16[384,384]{1,0:T(8,128)(2,1)} %copy-done.5) | copy-start | bytes 884740
  160.9 49.7 %all-to-all-start.3 = ((bf16[64,24,1024]{2,1,0:T(8,128)(2,1)}), bf16[64,24,1024]{2,1,0:T(8,128)(2,1)}, u32[]{:S(2)}, u32[]{:S(2)}) async-start(bf16[64,24,1024]{2,1,0:T(8,128)(2,1)} %bitcast.24), calls=%async_computation.3 | async-start | bytes 6291456 | tf_op jit(solution)/shard_map/all_to_all | solution.py:62
  170.7 7.2 %copy-start.1 = (bf16[128,4096]{1,0:T(8,128)(2,1)S(1)}, bf16[128,4096]{1,0:T(8,128)(2,1)}, u32[]{:S(2)}) copy-start(bf16[128,4096]{1,0:T(8,128)(2,1)} %grad_ref.1) | copy-start | bytes 3145732
  185.8 12.0 %copy-start.10 = (s32[128]{0:T(128)S(1)}, s32[128]{0:T(128)}, u32[]{:S(2)}) copy-start(s32[128]{0:T(128)} %param.16) | copy-start | bytes 1540
  185.8 12.0 %copy-start.19 = (f32[128,128]{1,0:T(8,128)S(1)}, f32[128,128]{1,0:T(8,128)}, u32[]{:S(2)}) copy-start(f32[128,128]{1,0:T(8,128)} %param.15) | copy-start | bytes 196612
  185.8 12.0 %copy-start.23 = (f32[128]{0:T(128)S(1)}, f32[128]{0:T(128)}, u32[]{:S(2)}) copy-start(f32[128]{0:T(128)} %copy-done.22) | copy-start | bytes 1540
  185.8 12.0 %copy-start.34 = (s32[128]{0:T(128)S(1)}, s32[128]{0:T(128)}, u32[]{:S(2)}) copy-start(s32[128]{0:T(128)} %copy-done.33) | copy-start | bytes 1540
  185.8 12.3 %copy-start.29 = (s32[128,2]{0,1:T(2,128)S(1)}, s32[128,2]{0,1:T(2,128)}, u32[]{:S(2)}) copy-start(s32[128,2]{0,1:T(2,128)} %copy-done.28) | copy-start | bytes 3076

commit v2 on v1

--- a/solution.py
+++ b/solution.py
@@ -14,7 +14,7 @@
 TEAM = 8
 LINES = CUT * CAP
 BUSY = 200_000_000_000
-WIDE = ("y", "x", "l", "h")
+WIDE = ("h", "y", "x", "l")
 ALL = ("y", "x", "l", "h", "c")
 NODE = ("y", "x", "l")
 LOCAL = ("h", "c")
@@ -41,6 +41,10 @@
     )
 
 
+def in_hbm(value):
+    return pltpu.with_memory_space_constraint(value, pltpu.HBM)
+
+
 def whole(shape):
     return pl.BlockSpec(shape, lambda *_: (0,) * len(shape))
 
@@ -60,18 +64,18 @@
 def exchange(value):
     blocks = value.reshape(-1, LINES, value.shape[-1])
     out = lax.all_to_all(blocks, WIDE, split_axis=0, concat_axis=0, tiled=True)
-    return out.reshape(value.shape)
+    return out.reshape(-1, value.shape[-1])
 
 
 def swap(value):
     return lax.ppermute(value, "c", [(0, 1), (1, 0)])
 
 
-def order_matrix(copies):
-    line = np.arange(TEAM * copies * LINES)
-    member, chunk, slot = line // (copies * LINES), line // CAP % CUT, line % CAP
+def order_matrix():
+    line = np.arange(TEAM * LINES)
+    member, chunk, slot = line // LINES, line // CAP % CUT, line % CAP
     wanted = (chunk * TEAM + member) * CAP + slot
-    return (wanted[:, None] == np.arange(TEAM * LINES)[None, :]).astype(BF16)
+    return (wanted[:, None] == line[None, :]).astype(BF16)
 
 
 def gathered(ref, start, width):
@@ -79,20 +83,35 @@
     return jnp.concatenate([ref[team, j * width : (j + 1) * width] for j in range(CUT)], axis=0)
 
 
-def spread_matrix(shape):
-    copies = shape[0] // shape[1]
+def order_in_kernel(shape):
     line = lax.broadcasted_iota(jnp.int32, (shape[0], 1), 0)
-    member, chunk, slot = line // (copies * LINES), line // CAP % CUT, line % CAP
+    member, chunk, slot = line // LINES, line // CAP % CUT, line % CAP
     wanted = (chunk * TEAM + member) * CAP + slot
     return (wanted == lax.broadcasted_iota(jnp.int32, shape, 1)).astype(F32).astype(BF16)
 
 
-def slots_kernel(expert_total, group_ref, expert_ref, rows_ref, out_ref, slot_ref, held, spread):
-    team = pl.program_id(0)
-    width = out_ref.shape[1]
-
-    @pl.when(team == 0)
+def send_team(held, order, out_ref):
+    team, width = pl.program_id(0), out_ref.shape[2]
+    start = pl.multiple_of(team * (TEAM * CAP), 16)
+    lines = dot(order, gathered(held, start, width)).astype(BF16)
+    for side in range(out_ref.shape[0]):
+        out_ref[side] = lines
+
+
+def slots_kernel(expert_total, group_in, expert_in, rows_in, out_ref, slot_ref, held, order, *own):
+    group_ref, expert_ref, rows_ref, sems = own
+
+    @pl.when(pl.program_id(0) == 0)
     def _():
+        pairs = ((group_in, group_ref), (expert_in, expert_ref), (rows_in, rows_ref))
+        copies = [
+            pltpu.make_async_copy(src, dst, sems.at[k]) for k, (src, dst) in enumerate(pairs)
+        ]
+        for copy in copies:
+            copy.start()
+        order[...] = order_in_kernel(order.shape)
+        copies[0].wait()
+        copies[1].wait()
         count = group_ref.shape[1]
         group = group_ref[...]
         inside = group < expert_total // GSIZE
@@ -101,9 +120,7 @@
         expert = lax.broadcasted_iota(jnp.int32, (expert_total, count), 0)
         targets, hots = [], []
         for k in range(2):
-            column = expert_ref[:, k : k + 1].astype(F32)
-            row = jnp.sum(jnp.where(down == along, column, 0.0), axis=0, keepdims=True)
-            target = jnp.where(inside, group * GSIZE + row.astype(jnp.int32), expert_total)
+            target = jnp.where(inside, group * GSIZE + expert_ref[k : k + 1, :], expert_total)
             targets.append(target)
             hots.append((expert == target).astype(F32))
         before = (down < along).astype(F32).astype(BF16)
@@ -117,43 +134,41 @@
             match = place == slot
             picked = match if picked is None else picked | match
         picked = picked.astype(F32).astype(BF16)
+        copies[2].wait()
         held[...] = dot(picked, rows_ref[...]).astype(BF16)
-        spread[...] = spread_matrix(spread.shape)
-
-    start = pl.multiple_of(team * (TEAM * CAP), 16)
-    out_ref[...] = dot(spread[...], gathered(held, start, width)).astype(BF16)
-
-
-def pack_tokens(group_id, expert_ids, tokens, copies, expert_total):
+
+    send_team(held, order[...], out_ref)
+
+
+def lines_out(sides, teams, width):
+    shape = jax.ShapeDtypeStruct((sides, teams * TEAM * LINES, width), BF16)
+    return shape, pl.BlockSpec((sides, TEAM * LINES, width), lambda t: (0, t, 0))
+
+
+def pack_tokens(group_id, expert_ids, tokens, sides, expert_total):
     count, model_width = tokens.shape
-    width = model_width // CUT
-    teams, lines = expert_total // TEAM, TEAM * copies * LINES
+    teams = expert_total // TEAM
+    shape, spec = lines_out(sides, teams, model_width // CUT)
     return call(
         functools.partial(slots_kernel, expert_total),
         "pack_tokens",
-        (
-            jax.ShapeDtypeStruct((teams * lines, width), BF16),
-            jax.ShapeDtypeStruct((2, count), jnp.int32),
-        ),
+        (shape, jax.ShapeDtypeStruct((2, count), jnp.int32)),
         grid=(teams,),
-        in_specs=[
-            whole((1, count)),
-            whole(expert_ids.shape),
-            whole(tokens.shape),
-        ],
-        out_specs=(pl.BlockSpec((lines, width), lambda t: (t, 0)), whole((2, count))),
+        in_specs=[pl.BlockSpec(memory_space=pltpu.HBM)] * 3,
+        out_specs=(spec, whole((2, count))),
         scratch_shapes=[
             pltpu.VMEM((expert_total * CAP, model_width), BF16),
-            pltpu.VMEM((lines, TEAM * LINES), BF16),
+            pltpu.VMEM((TEAM * LINES, TEAM * LINES), BF16),
+            pltpu.VMEM((1, count), jnp.int32),
+            pltpu.VMEM((2, count), jnp.int32),
+            pltpu.VMEM((count, model_width), BF16),
+            pltpu.SemaphoreType.DMA((3,)),
         ],
-    )(group_id[None], expert_ids, tokens)
-
-
-def grads_kernel(slot_ref, weight_ref, rows_ref, spread_ref, out_ref, held):
-    team = pl.program_id(0)
-    width = out_ref.shape[1]
-
-    @pl.when(team == 0)
+    )(*(in_hbm(value) for value in (group_id[None], expert_ids.T, tokens)))
+
+
+def grads_kernel(slot_ref, weight_ref, rows_ref, order_ref, out_ref, held):
+    @pl.when(pl.program_id(0) == 0)
     def _():
         place = lax.broadcasted_iota(jnp.int32, (held.shape[0], slot_ref.shape[1]), 0)
         first, second = place == slot_ref[0:1, :], place == slot_ref[1:2, :]
@@ -163,28 +178,27 @@
         picked = (first | second).astype(F32).astype(BF16)
         held[...] = (dot(picked, rows_ref[...]) * weight).astype(BF16)
 
-    start = pl.multiple_of(team * (TEAM * CAP), 16)
-    out_ref[...] = dot(spread_ref[...], gathered(held, start, width)).astype(BF16)
-
-
-def pack_grads(slot, weights, grad_out, spread, expert_total):
+    send_team(held, order_ref[...], out_ref)
+
+
+def pack_grads(slot, weights, grad_out, order, sides, expert_total):
     count, model_width = grad_out.shape
-    width = model_width // CUT
-    teams, lines = expert_total // TEAM, spread.shape[0]
+    teams = expert_total // TEAM
+    shape, spec = lines_out(sides, teams, model_width // CUT)
     return call(
         grads_kernel,
         "pack_grads",
-        jax.ShapeDtypeStruct((teams * lines, width), BF16),
+        shape,
         grid=(teams,),
         in_specs=[
             whole((2, count)),
             whole((2, count)),
             whole(grad_out.shape),
-            whole(spread.shape),
+            whole(order.shape),
         ],
-        out_specs=pl.BlockSpec((lines, width), lambda t: (t, 0)),
+        out_specs=spec,
         scratch_shapes=[pltpu.VMEM((expert_total * CAP, model_width), BF16)],
-    )(slot, weights, grad_out, spread)
+    )(slot, weights, grad_out, order)
 
 
 def put_in_order(lines_ref, order_ref, rows_ref):
@@ -432,6 +446,11 @@
     )(*hidden, *grads)
 
 
+def both_chips(lines_ref):
+    half = lines_ref.shape[0] // 2
+    return (lines_ref[:half].astype(F32) + lines_ref[half:].astype(F32)).astype(BF16)
+
+
 def mix_kernel(first_ref, second_ref, lines_ref, grad_ref, weight_ref, mixed_ref, score_ref):
     step = pl.program_id(0)
     count, piece = grad_ref.shape[0], lines_ref.shape[1]
@@ -441,8 +460,9 @@
     def _():
         score_ref[...] = jnp.zeros_like(score_ref)
 
-    first = dot(first_ref[...], lines_ref[...])
-    second = dot(second_ref[...], lines_ref[...])
+    lines = both_chips(lines_ref)
+    first = dot(first_ref[...], lines)
+    second = dot(second_ref[...], lines)
     for j in range(CUT):
         rows = slice(j * count, (j + 1) * count)
         columns = pl.ds(pl.multiple_of(j * width + step * piece, piece), piece)
@@ -480,7 +500,7 @@
     step = pl.program_id(0)
     count, piece = out_ref.shape[0], lines_ref.shape[1]
     width = out_ref.shape[1] // CUT
-    rows = dot(either_ref[...], lines_ref[...]).astype(BF16)
+    rows = dot(either_ref[...], both_chips(lines_ref)).astype(BF16)
     for j in range(CUT):
         columns = pl.ds(pl.multiple_of(j * width + step * piece, piece), piece)
         out_ref[:, columns] = rows[j * count : (j + 1) * count]
@@ -503,9 +523,7 @@
     count = tokens.shape[0]
     expert_total = lax.axis_size(NODE)
     sides = lax.axis_size("h")
-    peers = expert_total * sides
-    spread = jnp.asarray(order_matrix(sides))
-    order = order_matrix(1)
+    order = order_matrix()
     to_travel, in_order = jnp.asarray(order), jnp.asarray(order.T)
 
     tokens_out, slot = pack_tokens(group_id, expert_ids, tokens, sides, expert_total)
@@ -515,10 +533,10 @@
     weights, pull_back = jax.vjp(
         lambda values: gate_weights(values, group_id, chosen, inside), router_logits
     )
-    grads_out = pack_grads(slot, weights.T, grad_out, spread, expert_total)
-
-    line = np.arange(peers * LINES)
-    line_key = ((line // LINES // sides * CAP + line % CAP) * CUT + line // CAP % CUT)[None, :]
+    grads_out = pack_grads(slot, weights.T, grad_out, to_travel, sides, expert_total)
+
+    line = np.arange(expert_total * LINES)
+    line_key = ((line // LINES * CAP + line % CAP) * CUT + line // CAP % CUT)[None, :]
     chunk = jnp.arange(CUT, dtype=jnp.int32)[:, None]
 
     def lines_of(slots):

time: 217 us -> 215 us (level)
  waiting for transfers between devices: 50.9 us -> 57.6 us
  starting transfers between devices: 41.2 us -> 35.8 us
    all_to_all x4, waiting for transfers between devices: 50.9 us -> 57.6 us  [exchange(): out = lax.all_to_all(blocks, WIDE, split_axis=0, concat_axis=0, tiled=True)]
    all_to_all x4, starting transfers between devices: 40.8 us -> 35.3 us  [exchange(): out = lax.all_to_all(blocks, WIDE, split_axis=0, concat_axis=0, tiled=True)]
    unnamed x77 -> x86, local copies, waits for them, and re-layouts: 6.06 us -> 5.93 us
where the time goes in v2:
time: 215 us; the launch traced here: 214 us
  Pallas kernels  109 us (51%)
  waiting for transfers between devices  57.6 us (27%)
  starting transfers between devices  35.8 us (17%)
  local copies, waits for them, and re-layouts  6.16 us (3%)
  other arithmetic  4.27 us (2%)
    all_to_all x4, waiting for transfers between devices, exchange(): out = lax.all_to_all(blocks, WIDE, split_axis=0, concat_axis=0, tiled=True)  57.6 us
    all_to_all x4, starting transfers between devices, exchange(): out = lax.all_to_all(blocks, WIDE, split_axis=0, concat_axis=0, tiled=True)  35.3 us
    pallas_call x2, Pallas kernels, forward(): call(forward_kernel, 'forward_own' if own else 'forward_other', outs, BUS...  23.2 us
    pallas_call x2, Pallas kernels, backward(): call(backward_kernel, 'backward_own' if own else 'backward_other', outs,...  22.5 us
    pallas_call x2, Pallas kernels, to_lines(): call(lines_kernel, 'to_lines', jax.ShapeDtypeStruct((half * CUT, width),...  12.5 us
    pallas_call x1, Pallas kernels, columns_grad(): call(columns_grad_kernel, 'columns_grad', [jax.ShapeDtypeStruct((1, model...  11.5 us
    pallas_call x1, Pallas kernels, product_in(): call(in_kernel, 'product_in', jax.ShapeDtypeStruct((half, model_width), F...  7.67 us
    pallas_call x1, Pallas kernels, rows_grad(): call(rows_grad_kernel, 'rows_grad', jax.ShapeDtypeStruct((1, units, model...  7.06 us
  transfers between devices with their start and end apart: 8, of which 4 were waited for; matrix products, arithmetic and copies ran while one was open for 2% of the time, Pallas kernels for 47%

profile of v2, /device:TPU:0, one launch (start us, length us, event | category | flops | bytes accessed | tf_op | source)
XLA Modules:
  0.0 213.6 jit_solution(15525141915377207147)
XLA Ops:
  0.6 4.4 %pack_tokens.1 = (bf16[2,768,1024]{2,1,0:T(8,128)(2,1)}, s32[2,128]{1,0:T(2,128)S(1)}) custom-call(s32[1,128]{1,0:T(1,128)} %bitcast.28, s32[2,128]{1,0:T(2,128)} %bitcast.29, bf16[128,4096]{1,0:T(8,128)(2,1)} %rows_in.1), custom_call_target="tpu_custom_call" | custom-call | flops 1 | bytes 1 | tf_op jit(solution)/shard_map/pack_tokens/pallas_call | solution.py:152
  5.1 11.9 %all-to-all-start = ((bf16[64,24,1024]{2,1,0:T(8,128)(2,1)}), bf16[64,24,1024]{2,1,0:T(8,128)(2,1)}, u32[]{:S(2)}, u32[]{:S(2)}) async-start(bf16[64,24,1024]{2,1,0:T(8,128)(2,1)} %bitcast.27), calls=%async_computation | async-start | bytes 6291456 | tf_op jit(solution)/shard_map/all_to_all | solution.py:66
  17.0 0.1 reduce_max.18
  17.2 0.2 select_reduce_fusion.1
  17.4 0.4 copy-done.30
  17.7 0.1 copy.24
  17.9 0.1 exponential_reduce_fusion
  18.0 0.2 fusion.7
  18.2 0.2 fusion.4
  18.4 0.3 copy-done.38
  18.8 0.5 copy-done.34
  19.3 0.1 fusion.8
  19.4 0.1 copy.26.weight_ref
  19.4 3.2 %pack_grads.1 = bf16[2,768,1024]{2,1,0:T(8,128)(2,1)} custom-call(s32[2,128]{1,0:T(2,128)S(1)} %get-tuple-element.53.slot_ref, f32[2,128]{1,0:T(2,128)S(1)} %copy.26.weight_ref, bf16[128,4096]{1,0:T(8,128)(2,1)S(1)} %copy-done, bf16[192,192]{1,0:T(8,128)(2,1)S(1)} %copy-done.1), custom_call_target="tpu_custom_call" | custom-call | flops 1 | bytes 1 | tf_op jit(solution)/shard_map/pack_grads/pallas_call | solution.py:188
  22.7 0.4 fusion
  23.1 36.0 %all-to-all-done = bf16[64,24,1024]{2,1,0:T(8,128)(2,1)} async-done(((bf16[64,24,1024]{2,1,0:T(8,128)(2,1)}), bf16[64,24,1024]{2,1,0:T(8,128)(2,1)}, u32[]{:S(2)}, u32[]{:S(2)}) %all-to-all-start) | async-done | bytes 3145760 | tf_op jit(solution)/shard_map/all_to_all | solution.py:66
  59.1 7.3 %all-to-all-start.1 = ((bf16[64,24,1024]{2,1,0:T(8,128)(2,1)}), bf16[64,24,1024]{2,1,0:T(8,128)(2,1)}, u32[]{:S(2)}, u32[]{:S(2)}) async-start(bf16[64,24,1024]{2,1,0:T(8,128)(2,1)} %bitcast.25), calls=%async_computation.1 | async-start | bytes 6291456 | tf_op jit(solution)/shard_map/all_to_all | solution.py:66
  66.3 9.8 %forward_own.1 = (bf16[384,4096]{1,0:T(8,128)(2,1)}, f32[384,384]{1,0:T(8,128)S(1)}, f32[384,384]{1,0:T(8,128)S(1)}, bf16[384,384]{1,0:T(8,128)(2,1)S(1)}) custom-call(bf16[1536,1024]{1,0:T(8,128)(2,1)} %bitcast.3.lines_ref, bf16[192,192]{1,0:T(8,128)(2,1)S(1)} %copy-done.10, bf16[1,4096,384]{2,1,0:T(8,128)(2,1)} %gate_ref.9, bf16[1,4096,384]{2,1,0:T(8,128)(2,1)} %up_ref.9, ...), custom_call_target="tpu_custom_call" | custom-call | flops 199999995904 | bytes 1 | tf_op jit(solution)/shard_map/forward_own/pallas_call | solution.py:252
  76.2 0.8 copy-done.16
  77.0 0.8 copy-done.18
  77.8 13.4 %forward_other.1 = (bf16[384,4096]{1,0:T(8,128)(2,1)}, f32[384,384]{1,0:T(8,128)S(1)}, f32[384,384]{1,0:T(8,128)S(1)}, bf16[384,384]{1,0:T(8,128)(2,1)S(1)}, bf16[384,4096]{1,0:T(8,128)(2,1)}) custom-call(bf16[1536,1024]{1,0:T(8,128)(2,1)} %collective-permute-done.lines_ref, bf16[192,192]{1,0:T(8,128)(2,1)S(1)} %copy-done.10, ...), custom_call_target="tpu_custom_call" | custom-call | flops 199999995904 | bytes 1 | tf_op jit(solution)/shard_map/forward_other/pallas_call | solution.py:252
  91.2 0.8 copy-done.12
  92.0 0.2 collective-permute-start.1
  92.3 6.0 %product_out.1.total_ref = f32[384,4096]{1,0:T(8,128)} custom-call(bf16[384,384]{1,0:T(8,128)(2,1)S(1)} %get-tuple-element.94.hidden_ref.hidden_own, bf16[1,384,4096]{2,1,0:T(8,128)(2,1)} %down_ref.9), custom_call_target="tpu_custom_call" | custom-call | flops 199999995904 | bytes 1 | tf_op jit(solution)/shard_map/product_out/pallas_call | solution.py:340
  98.3 6.2 %to_lines.2 = bf16[1536,1024]{1,0:T(8,128)(2,1)} custom-call(f32[384,4096]{1,0:T(8,128)} %product_out.1.total_ref, bf16[384,4096]{1,0:T(8,128)(2,1)} %collective-permute-done.1.arrived_ref, bf16[192,192]{1,0:T(8,128)(2,1)S(1)} %copy-done.2), custom_call_target="tpu_custom_call" | custom-call | flops 1 | bytes 1 | tf_op jit(solution)/shard_map/to_lines/pallas_call | solution.py:392
  104.6 4.8 %all-to-all-done.1 = bf16[64,24,1024]{2,1,0:T(8,128)(2,1)} async-done(((bf16[64,24,1024]{2,1,0:T(8,128)(2,1)}), bf16[64,24,1024]{2,1,0:T(8,128)(2,1)}, u32[]{:S(2)}, u32[]{:S(2)}) %all-to-all-start.1) | async-done | bytes 3145760 | tf_op jit(solution)/shard_map/all_to_all | solution.py:66
  109.4 7.9 %all-to-all-start.2 = ((bf16[64,24,1024]{2,1,0:T(8,128)(2,1)}), bf16[64,24,1024]{2,1,0:T(8,128)(2,1)}, u32[]{:S(2)}, u32[]{:S(2)}) async-start(bf16[64,24,1024]{2,1,0:T(8,128)(2,1)} %bitcast.26), calls=%async_computation.2 | async-start | bytes 6291456 | tf_op jit(solution)/shard_map/all_to_all | solution.py:66
  117.3 1.1 copy-done.17
  118.4 1.1 copy-done.19
  119.4 8.3 %backward_own.1 = (bf16[384,4096]{1,0:T(8,128)(2,1)}, bf16[384,384]{1,0:T(8,128)(2,1)S(1)}, bf16[384,384]{1,0:T(8,128)(2,1)S(1)}) custom-call(bf16[1536,1024]{1,0:T(8,128)(2,1)} %bitcast.12.lines_ref, bf16[192,192]{1,0:T(8,128)(2,1)S(1)} %copy-done.10, bf16[1,384,4096]{2,1,0:T(8,128)(2,1)} %down_ref.9, f32[384,384]{1,0:T(8,128)S(1)} %copy-done.17, ...), custom_call_target="tpu_custom_call" | custom-call | flops 199999995904 | bytes 1 | tf_op jit(solution)/shard_map/backward_own/pallas_call | solution.py:312
  127.7 14.2 %backward_other.1 = (bf16[384,4096]{1,0:T(8,128)(2,1)}, bf16[384,384]{1,0:T(8,128)(2,1)S(1)}, bf16[384,384]{1,0:T(8,128)(2,1)S(1)}, bf16[384,4096]{1,0:T(8,128)(2,1)}) custom-call(bf16[1536,1024]{1,0:T(8,128)(2,1)} %collective-permute-done.2.lines_ref, bf16[192,192]{1,0:T(8,128)(2,1)S(1)} %copy-done.11, bf16[1,384,4096]{2,1,0:T(8,128)(2,1)} %down_ref.9, ...), custom_call_target="tpu_custom_call" | custom-call | flops 199999995904 | bytes 1 | tf_op jit(solution)/shard_map/backward_other/pallas_call | solution.py:312
  142.0 0.2 collective-permute-start.3
  142.2 7.7 %product_in.1.total_ref = f32[384,4096]{1,0:T(8,128)} custom-call(bf16[384,384]{1,0:T(8,128)(2,1)S(1)} %get-tuple-element.88.dg_ref.dg_own, bf16[384,384]{1,0:T(8,128)(2,1)S(1)} %get-tuple-element.90.du_ref.du_own, bf16[1,4096,384]{2,1,0:T(8,128)(2,1)} %gate_ref.9, bf16[1,4096,384]{2,1,0:T(8,128)(2,1)} %up_ref.9), custom_call_target="tpu_custom_call" | custom-call | flops 199999995904 | bytes 1 | tf_op jit(solution)/shard_map/product_in/pallas_call | solution.py:363
  149.9 6.2 %to_lines.3 = bf16[1536,1024]{1,0:T(8,128)(2,1)} custom-call(f32[384,4096]{1,0:T(8,128)} %product_in.1.total_ref, bf16[384,4096]{1,0:T(8,128)(2,1)} %collective-permute-done.3.arrived_ref, bf16[192,192]{1,0:T(8,128)(2,1)S(1)} %copy-done.3), custom_call_target="tpu_custom_call" | custom-call | flops 1 | bytes 1 | tf_op jit(solution)/shard_map/to_lines/pallas_call | solution.py:392
  156.1 4.2 %all-to-all-done.2 = bf16[64,24,1024]{2,1,0:T(8,128)(2,1)} async-done(((bf16[64,24,1024]{2,1,0:T(8,128)(2,1)}), bf16[64,24,1024]{2,1,0:T(8,128)(2,1)}, u32[]{:S(2)}, u32[]{:S(2)}) %all-to-all-start.2) | async-done | bytes 3145760 | tf_op jit(solution)/shard_map/all_to_all | solution.py:66
  160.4 8.3 %all-to-all-start.3 = ((bf16[64,24,1024]{2,1,0:T(8,128)(2,1)}), bf16[64,24,1024]{2,1,0:T(8,128)(2,1)}, u32[]{:S(2)}, u32[]{:S(2)}) async-start(bf16[64,24,1024]{2,1,0:T(8,128)(2,1)} %bitcast.24), calls=%async_computation.3 | async-start | bytes 6291456 | tf_op jit(solution)/shard_map/all_to_all | solution.py:66
  168.7 0.5 multiply_divide_fusion
  169.2 1.0 multiply_select_fusion.weight_ref
  170.1 7.1 %rows_grad.1 = bf16[1,384,4096]{2,1,0:T(8,128)(2,1)} custom-call(bf16[384,384]{1,0:T(8,128)(2,1)S(1)} %copy-done.5, bf16[384,384]{1,0:T(8,128)(2,1)S(1)} %get-tuple-element.95.hidden_other, bf16[384,4096]{1,0:T(8,128)(2,1)} %get-tuple-element.96.own, bf16[384,4096]{1,0:T(8,128)(2,1)} %get-tuple-element.97.other), custom_call_target="tpu_custom_call" | custom-call | flops 1 | bytes 1 | tf_op jit(solution)/shard_map/rows_grad/pallas_call | solution.py:439
  177.2 6.1 %mix.1 = (bf16[128,4096]{1,0:T(8,128)(2,1)}, f32[128,2]{1,0:T(8,128)S(1)}) custom-call(bf16[512,768]{1,0:T(8,128)(2,1)S(1)} %get-tuple-element.54.first_ref, bf16[512,768]{1,0:T(8,128)(2,1)S(1)} %get-tuple-element.55.second_ref, bf16[1536,1024]{1,0:T(8,128)(2,1)} %bitcast.14.lines_ref, bf16[128,4096]{1,0:T(8,128)(2,1)} %grad_ref.1, ...), custom_call_target="tpu_custom_call" | custom-call | flops 1 | bytes 1 | tf_op jit(solution)/shard_map/mix/pallas_call | solution.py:480
  183.4 11.5 %columns_grad.1 = (bf16[1,4096,384]{2,1,0:T(8,128)(2,1)}, bf16[1,4096,384]{2,1,0:T(8,128)(2,1)}) custom-call(bf16[384,4096]{1,0:T(8,128)(2,1)} %get-tuple-element.86.own, bf16[384,4096]{1,0:T(8,128)(2,1)} %get-tuple-element.87.other, bf16[384,384]{1,0:T(8,128)(2,1)S(1)} %get-tuple-element.88.dg_ref.dg_own, bf16[384,384]{1,0:T(8,128)(2,1)S(1)} %copy-done.7, ...), custom_call_target="tpu_custom_call" | custom-call | flops 1 | bytes 1 | tf_op jit(solution)/shard_map/columns_grad/pallas_call | solution.py:418
  194.9 0.2 multiply_reduce_fusion
  195.1 0.1 add_multiply_fusion
  195.4 0.2 fusion.6
  195.6 0.1 select_reduce_fusion
  195.8 0.8 fusion.3
  196.5 12.5 %all-to-all-done.3 = bf16[64,24,1024]{2,1,0:T(8,128)(2,1)} async-done(((bf16[64,24,1024]{2,1,0:T(8,128)(2,1)}), bf16[64,24,1024]{2,1,0:T(8,128)(2,1)}, u32[]{:S(2)}, u32[]{:S(2)}) %all-to-all-start.3) | async-done | bytes 3145760 | tf_op jit(solution)/shard_map/all_to_all | solution.py:66
  209.1 4.5 %unpack.1 = bf16[128,4096]{1,0:T(8,128)(2,1)} custom-call(bf16[512,768]{1,0:T(8,128)(2,1)S(1)} %get-tuple-element.83.either_ref, bf16[1536,1024]{1,0:T(8,128)(2,1)} %bitcast.16.lines_ref), custom_call_target="tpu_custom_call" | custom-call | flops 1 | bytes 1 | tf_op jit(solution)/shard_map/unpack/pallas_call | solution.py:512
  (97 shorter events, 0.4 us)
Async XLA Ops:
  5.1 11.9 %copy-start.20 = (f32[128,128]{1,0:T(8,128)S(1)}, f32[128,128]{1,0:T(8,128)}, u32[]{:S(2)}) copy-start(f32[128,128]{1,0:T(8,128)} %param.14) | copy-start | bytes 196612
  5.1 12.1 %copy-start.32 = (s32[128]{0:T(128)S(1)}, s32[128]{0:T(128)}, u32[]{:S(2)}) copy-start(s32[128]{0:T(128)} %param.15) | copy-start | bytes 1540
  5.1 12.1 %copy-start.41 = (s32[128,2]{0,1:T(2,128)S(1)}, s32[128,2]{0,1:T(2,128)}, u32[]{:S(2)}) copy-start(s32[128,2]{0,1:T(2,128)} %param.16) | copy-start | bytes 3076
  5.1 14.4 %copy-start = (bf16[128,4096]{1,0:T(8,128)(2,1)S(1)}, bf16[128,4096]{1,0:T(8,128)(2,1)}, u32[]{:S(2)}) copy-start(bf16[128,4096]{1,0:T(8,128)(2,1)} %grad_ref.1) | copy-start | bytes 3145732
  5.1 14.3 %copy-start.1 = (bf16[192,192]{1,0:T(8,128)(2,1)S(1)}, bf16[192,192]{1,0:T(8,128)(2,1)}, u32[]{:S(2)}) copy-start(bf16[192,192]{1,0:T(8,128)(2,1)} %constant.46.clone.order_ref) | copy-start | bytes 221188
  5.1 53.9 %all-to-all-start = ((bf16[64,24,1024]{2,1,0:T(8,128)(2,1)}), bf16[64,24,1024]{2,1,0:T(8,128)(2,1)}, u32[]{:S(2)}, u32[]{:S(2)}) async-start(bf16[64,24,1024]{2,1,0:T(8,128)(2,1)} %bitcast.27), calls=%async_computation | async-start | bytes 6291456 | tf_op jit(solution)/shard_map/all_to_all | solution.py:66
  17.0 5.7 %copy-start.40 = (s32[768]{0:T(1024)S(1)}, s32[768]{0:T(1024)}, u32[]{:S(2)}) copy-start(s32[768]{0:T(1024)} %constant.52) | copy-start | bytes 9220
  17.1 1.3 copy-start.24
  17.9 4.8 %copy-start.22 = (f32[128,2]{1,0:T(8,128)}, f32[128,2]{1,0:T(8,128)S(1)}, u32[]{:S(2)}) copy-start(f32[128,2]{1,0:T(8,128)S(1)} %copy.24) | copy-start | bytes 3076
  18.0 4.7 %copy-start.26 = (f32[128]{0:T(128)}, f32[128]{0:T(128)S(1)}, u32[]{:S(2)}) copy-start(f32[128]{0:T(128)S(1)} %exponential_reduce_fusion) | copy-start | bytes 1540
  18.2 0.6 copy-start.38
  18.8 3.9 %copy-start.28 = (f32[128]{0:T(128)}, f32[128]{0:T(128)S(1)}, u32[]{:S(2)}) copy-start(f32[128]{0:T(128)S(1)} %fusion.4) | copy-start | bytes 1540
  59.1 18.8 %collective-permute-start = (bf16[1536,1024]{1,0:T(8,128)(2,1)}, bf16[1536,1024]{1,0:T(8,128)(2,1)}, u32[]{:S(2)}, u32[]{:S(2)}) collective-permute-start(bf16[1536,1024]{1,0:T(8,128)(2,1)} %bitcast.3.lines_ref), channel_id=1, source_target_pairs={{0,1},{1,0},{2,3},{3,2},{4,5},{5,4},{6,7},{7,6},{8,9},{9,8},{10,11... | collective-permute-start | bytes 9437192 | tf_op jit(solution)/shard_map/ppermute | solution.py:71
  59.1 7.3 %copy-start.10 = (bf16[192,192]{1,0:T(8,128)(2,1)S(1)}, bf16[192,192]{1,0:T(8,128)(2,1)}, u32[]{:S(2)}) copy-start(bf16[192,192]{1,0:T(8,128)(2,1)} %constant.47.clone.order_ref) | copy-start | bytes 221188
  59.1 50.3 %all-to-all-start.1 = ((bf16[64,24,1024]{2,1,0:T(8,128)(2,1)}), bf16[64,24,1024]{2,1,0:T(8,128)(2,1)}, u32[]{:S(2)}, u32[]{:S(2)}) async-start(bf16[64,24,1024]{2,1,0:T(8,128)(2,1)} %bitcast.25), calls=%async_computation.1 | async-start | bytes 6291456 | tf_op jit(solution)/shard_map/all_to_all | solution.py:66
  76.2 0.8 copy-start.16
  77.0 0.8 copy-start.18
  77.8 14.5 %copy-start.4 = (bf16[384,384]{1,0:T(8,128)(2,1)}, bf16[384,384]{1,0:T(8,128)(2,1)S(1)}, u32[]{:S(2)}) copy-start(bf16[384,384]{1,0:T(8,128)(2,1)S(1)} %get-tuple-element.94.hidden_ref.hidden_own) | copy-start | bytes 884740
  91.2 0.8 copy-start.12
  92.0 6.3 %copy-start.14 = (f32[384,384]{1,0:T(8,128)}, f32[384,384]{1,0:T(8,128)S(1)}, u32[]{:S(2)}) copy-start(f32[384,384]{1,0:T(8,128)S(1)} %get-tuple-element.71.u_ref) | copy-start | bytes 1769476
  92.0 6.3 %collective-permute-start.1 = (bf16[384,4096]{1,0:T(8,128)(2,1)}, bf16[384,4096]{1,0:T(8,128)(2,1)}, u32[]{:S(2)}, u32[]{:S(2)}) collective-permute-start(bf16[384,4096]{1,0:T(8,128)(2,1)} %get-tuple-element.60), channel_id=1, source_target_pairs={{0,1},{1,0},{2,3},{3,2},{4,5},{5,4},{6,7},{7,6},{8,9},{9,8},{10,11... | collective-permute-start | bytes 9437192 | tf_op jit(solution)/shard_map/ppermute | solution.py:71
  92.3 6.0 %copy-start.2 = (bf16[192,192]{1,0:T(8,128)(2,1)S(1)}, bf16[192,192]{1,0:T(8,128)(2,1)}, u32[]{:S(2)}) copy-start(bf16[192,192]{1,0:T(8,128)(2,1)} %constant.46.clone.order_ref) | copy-start | bytes 221188
  109.4 18.3 %collective-permute-start.2 = (bf16[1536,1024]{1,0:T(8,128)(2,1)}, bf16[1536,1024]{1,0:T(8,128)(2,1)}, u32[]{:S(2)}, u32[]{:S(2)}) collective-permute-start(bf16[1536,1024]{1,0:T(8,128)(2,1)} %bitcast.12.lines_ref), channel_id=1, source_target_pairs={{0,1},{1,0},{2,3},{3,2},{4,5},{5,4},{6,7},{7,6},{8,9},{9,8},{10,11... | collective-permute-start | bytes 9437192 | tf_op jit(solution)/shard_map/ppermute | solution.py:71
  109.4 51.0 %all-to-all-start.2 = ((bf16[64,24,1024]{2,1,0:T(8,128)(2,1)}), bf16[64,24,1024]{2,1,0:T(8,128)(2,1)}, u32[]{:S(2)}, u32[]{:S(2)}) async-start(bf16[64,24,1024]{2,1,0:T(8,128)(2,1)} %bitcast.26), calls=%async_computation.2 | async-start | bytes 6291456 | tf_op jit(solution)/shard_map/all_to_all | solution.py:66
  117.3 1.1 copy-start.17
  118.4 1.1 copy-start.19
  119.4 8.3 %copy-start.11 = (bf16[192,192]{1,0:T(8,128)(2,1)S(1)}, bf16[192,192]{1,0:T(8,128)(2,1)}, u32[]{:S(2)}) copy-start(bf16[192,192]{1,0:T(8,128)(2,1)} %constant.47.clone.order_ref) | copy-start | bytes 221188
  119.4 8.3 %copy-start.13 = (f32[384,384]{1,0:T(8,128)S(1)}, f32[384,384]{1,0:T(8,128)}, u32[]{:S(2)}) copy-start(f32[384,384]{1,0:T(8,128)} %copy-done.12) | copy-start | bytes 1769476
  119.4 8.3 %copy-start.15 = (f32[384,384]{1,0:T(8,128)S(1)}, f32[384,384]{1,0:T(8,128)}, u32[]{:S(2)}) copy-start(f32[384,384]{1,0:T(8,128)} %copy-done.14) | copy-start | bytes 1769476
  142.0 7.9 %copy-start.6 = (bf16[384,384]{1,0:T(8,128)(2,1)}, bf16[384,384]{1,0:T(8,128)(2,1)S(1)}, u32[]{:S(2)}) copy-start(bf16[384,384]{1,0:T(8,128)(2,1)S(1)} %get-tuple-element.89.dg_other) | copy-start | bytes 884740
  142.0 7.9 %copy-start.8 = (bf16[384,384]{1,0:T(8,128)(2,1)}, bf16[384,384]{1,0:T(8,128)(2,1)S(1)}, u32[]{:S(2)}) copy-start(bf16[384,384]{1,0:T(8,128)(2,1)S(1)} %get-tuple-element.91.du_other) | copy-start | bytes 884740
  142.0 7.9 %collective-permute-start.3 = (bf16[384,4096]{1,0:T(8,128)(2,1)}, bf16[384,4096]{1,0:T(8,128)(2,1)}, u32[]{:S(2)}, u32[]{:S(2)}) collective-permute-start(bf16[384,4096]{1,0:T(8,128)(2,1)} %get-tuple-element.72), channel_id=1, source_target_pairs={{0,1},{1,0},{2,3},{3,2},{4,5},{5,4},{6,7},{7,6},{8,9},{9,8},{10,11... | collective-permute-start | bytes 9437192 | tf_op jit(solution)/shard_map/ppermute | solution.py:71
  142.2 7.7 %copy-start.3 = (bf16[192,192]{1,0:T(8,128)(2,1)S(1)}, bf16[192,192]{1,0:T(8,128)(2,1)}, u32[]{:S(2)}) copy-start(bf16[192,192]{1,0:T(8,128)(2,1)} %constant.46.clone.order_ref) | copy-start | bytes 221188
  160.3 8.3 %copy-start.27 = (f32[128]{0:T(128)S(1)}, f32[128]{0:T(128)}, u32[]{:S(2)}) copy-start(f32[128]{0:T(128)} %copy-done.26) | copy-start | bytes 1540
  160.4 8.3 %copy-start.39 = (f32[128]{0:T(128)S(1)}, f32[128]{0:T(128)}, u32[]{:S(2)}) copy-start(f32[128]{0:T(128)} %copy-done.38) | copy-start | bytes 1540
  160.4 8.8 %copy-start.29 = (f32[128]{0:T(128)S(1)}, f32[128]{0:T(128)}, u32[]{:S(2)}) copy-start(f32[128]{0:T(128)} %copy-done.28) | copy-start | bytes 1540
  160.4 8.8 %copy-start.35 = (pred[128]{0:T(512)(128)(4,1)S(1)}, pred[128]{0:T(512)(128)(4,1)}, u32[]{:S(2)}) copy-start(pred[128]{0:T(512)(128)(4,1)} %copy-done.34) | copy-start | bytes 388
  160.4 9.8 %copy-start.5 = (bf16[384,384]{1,0:T(8,128)(2,1)S(1)}, bf16[384,384]{1,0:T(8,128)(2,1)}, u32[]{:S(2)}) copy-start(bf16[384,384]{1,0:T(8,128)(2,1)} %copy-done.4) | copy-start | bytes 884740
  160.4 48.7 %all-to-all-start.3 = ((bf16[64,24,1024]{2,1,0:T(8,128)(2,1)}), bf16[64,24,1024]{2,1,0:T(8,128)(2,1)}, u32[]{:S(2)}, u32[]{:S(2)}) async-start(bf16[64,24,1024]{2,1,0:T(8,128)(2,1)} %bitcast.24), calls=%async_computation.3 | async-start | bytes 6291456 | tf_op jit(solution)/shard_map/all_to_all | solution.py:66
  177.2 6.1 %copy-start.7 = (bf16[384,384]{1,0:T(8,128)(2,1)S(1)}, bf16[384,384]{1,0:T(8,128)(2,1)}, u32[]{:S(2)}) copy-start(bf16[384,384]{1,0:T(8,128)(2,1)} %copy-done.6) | copy-start | bytes 884740
  177.2 6.1 %copy-start.9 = (bf16[384,384]{1,0:T(8,128)(2,1)S(1)}, bf16[384,384]{1,0:T(8,128)(2,1)}, u32[]{:S(2)}) copy-start(bf16[384,384]{1,0:T(8,128)(2,1)} %copy-done.8) | copy-start | bytes 884740
  183.3 11.6 %copy-start.23 = (f32[128,2]{1,0:T(8,128)S(1)}, f32[128,2]{1,0:T(8,128)}, u32[]{:S(2)}) copy-start(f32[128,2]{1,0:T(8,128)} %copy-done.22) | copy-start | bytes 3076
  183.3 12.0 %copy-start.21 = (f32[128,128]{1,0:T(8,128)S(1)}, f32[128,128]{1,0:T(8,128)}, u32[]{:S(2)}) copy-start(f32[128,128]{1,0:T(8,128)} %param.14) | copy-start | bytes 196612
  183.3 12.0 %copy-start.25 = (f32[128]{0:T(128)S(1)}, f32[128]{0:T(128)}, u32[]{:S(2)}) copy-start(f32[128]{0:T(128)} %copy-done.24) | copy-start | bytes 1540
  183.3 12.0 %copy-start.33 = (s32[128]{0:T(128)S(1)}, s32[128]{0:T(128)}, u32[]{:S(2)}) copy-start(s32[128]{0:T(128)} %param.15) | copy-start | bytes 1540
  183.3 12.0 %copy-start.37 = (s32[128]{0:T(128)S(1)}, s32[128]{0:T(128)}, u32[]{:S(2)}) copy-start(s32[128]{0:T(128)} %copy-done.36) | copy-start | bytes 1540
  183.3 12.0 %copy-start.42 = (f32[128]{0:T(128)S(1)}, f32[128]{0:T(128)}, u32[]{:S(2)}) copy-start(f32[128]{0:T(128)} %multiply_divide_fusion) | copy-start | bytes 1540
  183.4 12.3 %copy-start.31 = (s32[128,2]{0,1:T(2,128)S(1)}, s32[128,2]{0,1:T(2,128)}, u32[]{:S(2)}) copy-start(s32[128,2]{0,1:T(2,128)} %copy-done.30) | copy-start | bytes 3076
  (3 other events, 1.6 us)

commit v3 on v2

--- a/solution.py
+++ b/solution.py
@@ -245,7 +245,8 @@
     wide = jax.ShapeDtypeStruct((half, model_width), BF16)
     weight_spec = pl.BlockSpec((None, width, units), lambda k: (0, k, 0))
     act = whole((half, units))
-    outs = [wide] + [jax.ShapeDtypeStruct((half, units), t) for t in (F32, F32, BF16)]
+    outs = [wide, pltpu.HBM((half, units), F32), pltpu.HBM((half, units), F32)]
+    outs.append(jax.ShapeDtypeStruct((half, units), BF16))
     if not own:
         outs.append(wide)
     down_shape = (None, units, model_width if not own else width)
@@ -326,7 +327,7 @@
         ],
         out_specs=[whole(wide.shape), act, act, whole(wide.shape)][: len(outs)],
         scratch_shapes=[pltpu.VMEM((half, units), F32)],
-    )(lines, order, w_down, gate_pre, up_pre, w_gate, w_up)
+    )(lines, order, w_down, in_hbm(gate_pre), in_hbm(up_pre), w_gate, w_up)
 
 
 def out_kernel(hidden_ref, down_ref, total_ref):

time: 215 us -> 215 us (level)
  local copies, waits for them, and re-layouts: 6.16 us -> 1.61 us
  waiting for transfers between devices: 57.6 us -> 60.7 us
    unnamed x86 -> x70, local copies, waits for them, and re-layouts: 5.93 us -> 1.38 us
    all_to_all x4, waiting for transfers between devices: 57.6 us -> 60.7 us  [exchange(): out = lax.all_to_all(blocks, WIDE, split_axis=0, concat_axis=0, tiled=True)]
where the time goes in v3:
time: 215 us; the launch traced here: 214 us
  Pallas kernels  110 us (51%)
  waiting for transfers between devices  60.7 us (28%)
  starting transfers between devices  35.7 us (17%)
  other arithmetic  4.31 us (2%)
    all_to_all x4, waiting for transfers between devices, exchange(): out = lax.all_to_all(blocks, WIDE, split_axis=0, concat_axis=0, tiled=True)  60.7 us
    all_to_all x4, starting transfers between devices, exchange(): out = lax.all_to_all(blocks, WIDE, split_axis=0, concat_axis=0, tiled=True)  35.2 us
    pallas_call x2, Pallas kernels, forward(): call(forward_kernel, 'forward_own' if own else 'forward_other', outs, BUS...  24 us
    pallas_call x2, Pallas kernels, backward(): call(backward_kernel, 'backward_own' if own else 'backward_other', outs,...  23.1 us
    pallas_call x2, Pallas kernels, to_lines(): call(lines_kernel, 'to_lines', jax.ShapeDtypeStruct((half * CUT, width),...  12.5 us
    pallas_call x1, Pallas kernels, columns_grad(): call(columns_grad_kernel, 'columns_grad', [jax.ShapeDtypeStruct((1, model...  11.5 us
    pallas_call x1, Pallas kernels, product_in(): call(in_kernel, 'product_in', jax.ShapeDtypeStruct((half, model_width), F...  7.69 us
    pallas_call x1, Pallas kernels, rows_grad(): call(rows_grad_kernel, 'rows_grad', jax.ShapeDtypeStruct((1, units, model...  7.06 us
  transfers between devices with their start and end apart: 8, of which 4 were waited for; matrix products, arithmetic and copies ran while one was open for 2% of the time, Pallas kernels for 47%

profile of v3, /device:TPU:0, one launch (start us, length us, event | category | flops | bytes accessed | tf_op | source)
XLA Modules:
  0.0 213.5 jit_solution(10798753714773929967)
XLA Ops:
  0.6 4.4 %pack_tokens.1 = (bf16[2,768,1024]{2,1,0:T(8,128)(2,1)}, s32[2,128]{1,0:T(2,128)S(1)}) custom-call(s32[1,128]{1,0:T(1,128)} %bitcast.28, s32[2,128]{1,0:T(2,128)} %bitcast.29, bf16[128,4096]{1,0:T(8,128)(2,1)} %rows_in.1), custom_call_target="tpu_custom_call" | custom-call | flops 1 | bytes 1 | tf_op jit(solution)/shard_map/pack_tokens/pallas_call | solution.py:152
  5.1 11.9 %all-to-all-start = ((bf16[64,24,1024]{2,1,0:T(8,128)(2,1)}), bf16[64,24,1024]{2,1,0:T(8,128)(2,1)}, u32[]{:S(2)}, u32[]{:S(2)}) async-start(bf16[64,24,1024]{2,1,0:T(8,128)(2,1)} %bitcast.27), calls=%async_computation | async-start | bytes 6291456 | tf_op jit(solution)/shard_map/all_to_all | solution.py:66
  17.0 0.0 copy-start.32
  17.0 0.1 reduce_max.18
  17.2 0.2 select_reduce_fusion.1
  17.4 0.4 copy-done.22
  17.8 0.1 copy.24
  17.9 0.1 exponential_reduce_fusion
  18.0 0.2 fusion.7
  18.2 0.2 fusion.4
  18.4 0.1 copy-done.28
  18.5 0.3 copy-done.30
  18.8 0.5 copy-done.26
  19.3 0.1 fusion.8
  19.4 0.1 copy.26.weight_ref
  19.5 3.2 %pack_grads.1 = bf16[2,768,1024]{2,1,0:T(8,128)(2,1)} custom-call(s32[2,128]{1,0:T(2,128)S(1)} %get-tuple-element.53.slot_ref, f32[2,128]{1,0:T(2,128)S(1)} %copy.26.weight_ref, bf16[128,4096]{1,0:T(8,128)(2,1)S(1)} %copy-done, bf16[192,192]{1,0:T(8,128)(2,1)S(1)} %copy-done.1), custom_call_target="tpu_custom_call" | custom-call | flops 1 | bytes 1 | tf_op jit(solution)/shard_map/pack_grads/pallas_call | solution.py:188
  22.7 0.4 fusion
  23.1 35.9 %all-to-all-done = bf16[64,24,1024]{2,1,0:T(8,128)(2,1)} async-done(((bf16[64,24,1024]{2,1,0:T(8,128)(2,1)}), bf16[64,24,1024]{2,1,0:T(8,128)(2,1)}, u32[]{:S(2)}, u32[]{:S(2)}) %all-to-all-start) | async-done | bytes 3145760 | tf_op jit(solution)/shard_map/all_to_all | solution.py:66
  59.0 7.2 %all-to-all-start.1 = ((bf16[64,24,1024]{2,1,0:T(8,128)(2,1)}), bf16[64,24,1024]{2,1,0:T(8,128)(2,1)}, u32[]{:S(2)}, u32[]{:S(2)}) async-start(bf16[64,24,1024]{2,1,0:T(8,128)(2,1)} %bitcast.25), calls=%async_computation.1 | async-start | bytes 6291456 | tf_op jit(solution)/shard_map/all_to_all | solution.py:66
  66.2 10.2 %forward_own.1 = (bf16[384,4096]{1,0:T(8,128)(2,1)}, f32[384,384]{1,0:T(8,128)}, f32[384,384]{1,0:T(8,128)}, bf16[384,384]{1,0:T(8,128)(2,1)S(1)}) custom-call(bf16[1536,1024]{1,0:T(8,128)(2,1)} %bitcast.3.lines_ref, bf16[192,192]{1,0:T(8,128)(2,1)S(1)} %copy-done.10, bf16[1,4096,384]{2,1,0:T(8,128)(2,1)} %gate_ref.9, bf16[1,4096,384]{2,1,0:T(8,128)(2,1)} %up_ref.9, ...), custom_call_target="tpu_custom_call" | custom-call | flops 199999995904 | bytes 1 | tf_op jit(solution)/shard_map/forward_own/pallas_call | solution.py:253
  76.4 13.8 %forward_other.1 = (bf16[384,4096]{1,0:T(8,128)(2,1)}, f32[384,384]{1,0:T(8,128)}, f32[384,384]{1,0:T(8,128)}, bf16[384,384]{1,0:T(8,128)(2,1)S(1)}, bf16[384,4096]{1,0:T(8,128)(2,1)}) custom-call(bf16[1536,1024]{1,0:T(8,128)(2,1)} %collective-permute-done.lines_ref, bf16[192,192]{1,0:T(8,128)(2,1)S(1)} %copy-done.10, bf16[1,4096,384]{2,1,0:T(8,128)(2,1)} %gate_ref.9, ...), custom_call_target="tpu_custom_call" | custom-call | flops 199999995904 | bytes 1 | tf_op jit(solution)/shard_map/forward_other/pallas_call | solution.py:253
  90.2 0.2 collective-permute-start.1
  90.5 6.0 %product_out.1.total_ref = f32[384,4096]{1,0:T(8,128)} custom-call(bf16[384,384]{1,0:T(8,128)(2,1)S(1)} %get-tuple-element.94.hidden_ref.hidden_own, bf16[1,384,4096]{2,1,0:T(8,128)(2,1)} %down_ref.9), custom_call_target="tpu_custom_call" | custom-call | flops 199999995904 | bytes 1 | tf_op jit(solution)/shard_map/product_out/pallas_call | solution.py:341
  96.5 6.2 %to_lines.2 = bf16[1536,1024]{1,0:T(8,128)(2,1)} custom-call(f32[384,4096]{1,0:T(8,128)} %product_out.1.total_ref, bf16[384,4096]{1,0:T(8,128)(2,1)} %collective-permute-done.1.arrived_ref, bf16[192,192]{1,0:T(8,128)(2,1)S(1)} %copy-done.2), custom_call_target="tpu_custom_call" | custom-call | flops 1 | bytes 1 | tf_op jit(solution)/shard_map/to_lines/pallas_call | solution.py:393
  102.7 6.5 %all-to-all-done.1 = bf16[64,24,1024]{2,1,0:T(8,128)(2,1)} async-done(((bf16[64,24,1024]{2,1,0:T(8,128)(2,1)}), bf16[64,24,1024]{2,1,0:T(8,128)(2,1)}, u32[]{:S(2)}, u32[]{:S(2)}) %all-to-all-start.1) | async-done | bytes 3145760 | tf_op jit(solution)/shard_map/all_to_all | solution.py:66
  109.3 7.9 %all-to-all-start.2 = ((bf16[64,24,1024]{2,1,0:T(8,128)(2,1)}), bf16[64,24,1024]{2,1,0:T(8,128)(2,1)}, u32[]{:S(2)}, u32[]{:S(2)}) async-start(bf16[64,24,1024]{2,1,0:T(8,128)(2,1)} %bitcast.26), calls=%async_computation.2 | async-start | bytes 6291456 | tf_op jit(solution)/shard_map/all_to_all | solution.py:66
  117.2 0.0 copy-start.11
  117.2 8.6 %backward_own.1 = (bf16[384,4096]{1,0:T(8,128)(2,1)}, bf16[384,384]{1,0:T(8,128)(2,1)S(1)}, bf16[384,384]{1,0:T(8,128)(2,1)S(1)}) custom-call(bf16[1536,1024]{1,0:T(8,128)(2,1)} %bitcast.12.lines_ref, bf16[192,192]{1,0:T(8,128)(2,1)S(1)} %copy-done.10, bf16[1,384,4096]{2,1,0:T(8,128)(2,1)} %down_ref.9, f32[384,384]{1,0:T(8,128)} %get-tuple-element.63.g_ref, ...), custom_call_target="tpu_custom_call" | custom-call | flops 199999995904 | bytes 1 | tf_op jit(solution)/shard_map/backward_own/pallas_call | solution.py:313
  125.8 14.5 %backward_other.1 = (bf16[384,4096]{1,0:T(8,128)(2,1)}, bf16[384,384]{1,0:T(8,128)(2,1)S(1)}, bf16[384,384]{1,0:T(8,128)(2,1)S(1)}, bf16[384,4096]{1,0:T(8,128)(2,1)}) custom-call(bf16[1536,1024]{1,0:T(8,128)(2,1)} %collective-permute-done.2.lines_ref, bf16[192,192]{1,0:T(8,128)(2,1)S(1)} %copy-done.11, bf16[1,384,4096]{2,1,0:T(8,128)(2,1)} %down_ref.9, ...), custom_call_target="tpu_custom_call" | custom-call | flops 199999995904 | bytes 1 | tf_op jit(solution)/shard_map/backward_other/pallas_call | solution.py:313
  140.3 0.2 collective-permute-start.3
  140.6 7.7 %product_in.1.total_ref = f32[384,4096]{1,0:T(8,128)} custom-call(bf16[384,384]{1,0:T(8,128)(2,1)S(1)} %get-tuple-element.88.dg_ref.dg_own, bf16[384,384]{1,0:T(8,128)(2,1)S(1)} %get-tuple-element.90.du_ref.du_own, bf16[1,4096,384]{2,1,0:T(8,128)(2,1)} %gate_ref.9, bf16[1,4096,384]{2,1,0:T(8,128)(2,1)} %up_ref.9), custom_call_target="tpu_custom_call" | custom-call | flops 199999995904 | bytes 1 | tf_op jit(solution)/shard_map/product_in/pallas_call | solution.py:364
  148.3 6.2 %to_lines.3 = bf16[1536,1024]{1,0:T(8,128)(2,1)} custom-call(f32[384,4096]{1,0:T(8,128)} %product_in.1.total_ref, bf16[384,4096]{1,0:T(8,128)(2,1)} %collective-permute-done.3.arrived_ref, bf16[192,192]{1,0:T(8,128)(2,1)S(1)} %copy-done.3), custom_call_target="tpu_custom_call" | custom-call | flops 1 | bytes 1 | tf_op jit(solution)/shard_map/to_lines/pallas_call | solution.py:393
  154.5 5.7 %all-to-all-done.2 = bf16[64,24,1024]{2,1,0:T(8,128)(2,1)} async-done(((bf16[64,24,1024]{2,1,0:T(8,128)(2,1)}), bf16[64,24,1024]{2,1,0:T(8,128)(2,1)}, u32[]{:S(2)}, u32[]{:S(2)}) %all-to-all-start.2) | async-done | bytes 3145760 | tf_op jit(solution)/shard_map/all_to_all | solution.py:66
  160.3 8.3 %all-to-all-start.3 = ((bf16[64,24,1024]{2,1,0:T(8,128)(2,1)}), bf16[64,24,1024]{2,1,0:T(8,128)(2,1)}, u32[]{:S(2)}, u32[]{:S(2)}) async-start(bf16[64,24,1024]{2,1,0:T(8,128)(2,1)} %bitcast.24), calls=%async_computation.3 | async-start | bytes 6291456 | tf_op jit(solution)/shard_map/all_to_all | solution.py:66
  168.6 0.5 multiply_divide_fusion
  169.1 1.0 multiply_select_fusion.weight_ref
  170.1 7.1 %rows_grad.1 = bf16[1,384,4096]{2,1,0:T(8,128)(2,1)} custom-call(bf16[384,384]{1,0:T(8,128)(2,1)S(1)} %copy-done.5, bf16[384,384]{1,0:T(8,128)(2,1)S(1)} %get-tuple-element.95.hidden_other, bf16[384,4096]{1,0:T(8,128)(2,1)} %get-tuple-element.96.own, bf16[384,4096]{1,0:T(8,128)(2,1)} %get-tuple-element.97.other), custom_call_target="tpu_custom_call" | custom-call | flops 1 | bytes 1 | tf_op jit(solution)/shard_map/rows_grad/pallas_call | solution.py:440
  177.2 6.1 %mix.1 = (bf16[128,4096]{1,0:T(8,128)(2,1)}, f32[128,2]{1,0:T(8,128)S(1)}) custom-call(bf16[512,768]{1,0:T(8,128)(2,1)S(1)} %get-tuple-element.54.first_ref, bf16[512,768]{1,0:T(8,128)(2,1)S(1)} %get-tuple-element.55.second_ref, bf16[1536,1024]{1,0:T(8,128)(2,1)} %bitcast.14.lines_ref, bf16[128,4096]{1,0:T(8,128)(2,1)} %grad_ref.1, ...), custom_call_target="tpu_custom_call" | custom-call | flops 1 | bytes 1 | tf_op jit(solution)/shard_map/mix/pallas_call | solution.py:481
  183.3 11.5 %columns_grad.1 = (bf16[1,4096,384]{2,1,0:T(8,128)(2,1)}, bf16[1,4096,384]{2,1,0:T(8,128)(2,1)}) custom-call(bf16[384,4096]{1,0:T(8,128)(2,1)} %get-tuple-element.86.own, bf16[384,4096]{1,0:T(8,128)(2,1)} %get-tuple-element.87.other, bf16[384,384]{1,0:T(8,128)(2,1)S(1)} %get-tuple-element.88.dg_ref.dg_own, bf16[384,384]{1,0:T(8,128)(2,1)S(1)} %copy-done.7, ...), custom_call_target="tpu_custom_call" | custom-call | flops 1 | bytes 1 | tf_op jit(solution)/shard_map/columns_grad/pallas_call | solution.py:419
  194.9 0.2 multiply_reduce_fusion
  195.1 0.1 add_multiply_fusion
  195.2 0.1 copy.28
  195.3 0.0 copy-done.25
  195.3 0.2 fusion.6
  195.6 0.1 select_reduce_fusion
  195.7 0.8 fusion.3
  196.5 12.5 %all-to-all-done.3 = bf16[64,24,1024]{2,1,0:T(8,128)(2,1)} async-done(((bf16[64,24,1024]{2,1,0:T(8,128)(2,1)}), bf16[64,24,1024]{2,1,0:T(8,128)(2,1)}, u32[]{:S(2)}, u32[]{:S(2)}) %all-to-all-start.3) | async-done | bytes 3145760 | tf_op jit(solution)/shard_map/all_to_all | solution.py:66
  209.0 4.5 %unpack.1 = bf16[128,4096]{1,0:T(8,128)(2,1)} custom-call(bf16[512,768]{1,0:T(8,128)(2,1)S(1)} %get-tuple-element.83.either_ref, bf16[1536,1024]{1,0:T(8,128)(2,1)} %bitcast.16.lines_ref), custom_call_target="tpu_custom_call" | custom-call | flops 1 | bytes 1 | tf_op jit(solution)/shard_map/unpack/pallas_call | solution.py:513
  (81 shorter events, 0.2 us)
Async XLA Ops:
  5.1 11.9 %copy-start.12 = (f32[128,128]{1,0:T(8,128)S(1)}, f32[128,128]{1,0:T(8,128)}, u32[]{:S(2)}) copy-start(f32[128,128]{1,0:T(8,128)} %param.14) | copy-start | bytes 196612
  5.1 12.1 %copy-start.24 = (s32[128]{0:T(128)S(1)}, s32[128]{0:T(128)}, u32[]{:S(2)}) copy-start(s32[128]{0:T(128)} %param.15) | copy-start | bytes 1540
  5.1 12.1 %copy-start.33 = (s32[128,2]{0,1:T(2,128)S(1)}, s32[128,2]{0,1:T(2,128)}, u32[]{:S(2)}) copy-start(s32[128,2]{0,1:T(2,128)} %param.16) | copy-start | bytes 3076
  5.1 14.4 %copy-start = (bf16[128,4096]{1,0:T(8,128)(2,1)S(1)}, bf16[128,4096]{1,0:T(8,128)(2,1)}, u32[]{:S(2)}) copy-start(bf16[128,4096]{1,0:T(8,128)(2,1)} %grad_ref.1) | copy-start | bytes 3145732
  5.1 14.4 %copy-start.1 = (bf16[192,192]{1,0:T(8,128)(2,1)S(1)}, bf16[192,192]{1,0:T(8,128)(2,1)}, u32[]{:S(2)}) copy-start(bf16[192,192]{1,0:T(8,128)(2,1)} %constant.46.clone.order_ref) | copy-start | bytes 221188
  5.1 53.9 %all-to-all-start = ((bf16[64,24,1024]{2,1,0:T(8,128)(2,1)}), bf16[64,24,1024]{2,1,0:T(8,128)(2,1)}, u32[]{:S(2)}, u32[]{:S(2)}) async-start(bf16[64,24,1024]{2,1,0:T(8,128)(2,1)} %bitcast.27), calls=%async_computation | async-start | bytes 6291456 | tf_op jit(solution)/shard_map/all_to_all | solution.py:66
  17.0 5.7 %copy-start.32 = (s32[768]{0:T(1024)S(1)}, s32[768]{0:T(1024)}, u32[]{:S(2)}) copy-start(s32[768]{0:T(1024)} %constant.52) | copy-start | bytes 9220
  17.1 1.3 copy-start.16
  17.2 0.6 copy-start.22
  17.9 4.8 %copy-start.14 = (f32[128,2]{1,0:T(8,128)}, f32[128,2]{1,0:T(8,128)S(1)}, u32[]{:S(2)}) copy-start(f32[128,2]{1,0:T(8,128)S(1)} %copy.24) | copy-start | bytes 3076
  17.9 0.6 copy-start.28
  18.0 4.7 %copy-start.18 = (f32[128]{0:T(128)}, f32[128]{0:T(128)S(1)}, u32[]{:S(2)}) copy-start(f32[128]{0:T(128)S(1)} %exponential_reduce_fusion) | copy-start | bytes 1540
  18.2 0.5 copy-start.30
  18.8 3.9 %copy-start.20 = (f32[128]{0:T(128)}, f32[128]{0:T(128)S(1)}, u32[]{:S(2)}) copy-start(f32[128]{0:T(128)S(1)} %fusion.4) | copy-start | bytes 1540
  18.8 0.5 copy-start.26
  59.0 17.4 %collective-permute-start = (bf16[1536,1024]{1,0:T(8,128)(2,1)}, bf16[1536,1024]{1,0:T(8,128)(2,1)}, u32[]{:S(2)}, u32[]{:S(2)}) collective-permute-start(bf16[1536,1024]{1,0:T(8,128)(2,1)} %bitcast.3.lines_ref), channel_id=1, source_target_pairs={{0,1},{1,0},{2,3},{3,2},{4,5},{5,4},{6,7},{7,6},{8,9},{9,8},{10,11... | collective-permute-start | bytes 9437192 | tf_op jit(solution)/shard_map/ppermute | solution.py:71
  59.0 7.2 %copy-start.10 = (bf16[192,192]{1,0:T(8,128)(2,1)S(1)}, bf16[192,192]{1,0:T(8,128)(2,1)}, u32[]{:S(2)}) copy-start(bf16[192,192]{1,0:T(8,128)(2,1)} %constant.47.clone.order_ref) | copy-start | bytes 221188
  59.0 50.2 %all-to-all-start.1 = ((bf16[64,24,1024]{2,1,0:T(8,128)(2,1)}), bf16[64,24,1024]{2,1,0:T(8,128)(2,1)}, u32[]{:S(2)}, u32[]{:S(2)}) async-start(bf16[64,24,1024]{2,1,0:T(8,128)(2,1)} %bitcast.25), calls=%async_computation.1 | async-start | bytes 6291456 | tf_op jit(solution)/shard_map/all_to_all | solution.py:66
  76.4 14.0 %copy-start.4 = (bf16[384,384]{1,0:T(8,128)(2,1)}, bf16[384,384]{1,0:T(8,128)(2,1)S(1)}, u32[]{:S(2)}) copy-start(bf16[384,384]{1,0:T(8,128)(2,1)S(1)} %get-tuple-element.94.hidden_ref.hidden_own) | copy-start | bytes 884740
  90.2 6.2 %collective-permute-start.1 = (bf16[384,4096]{1,0:T(8,128)(2,1)}, bf16[384,4096]{1,0:T(8,128)(2,1)}, u32[]{:S(2)}, u32[]{:S(2)}) collective-permute-start(bf16[384,4096]{1,0:T(8,128)(2,1)} %get-tuple-element.60), channel_id=1, source_target_pairs={{0,1},{1,0},{2,3},{3,2},{4,5},{5,4},{6,7},{7,6},{8,9},{9,8},{10,11... | collective-permute-start | bytes 9437192 | tf_op jit(solution)/shard_map/ppermute | solution.py:71
  90.5 6.0 %copy-start.2 = (bf16[192,192]{1,0:T(8,128)(2,1)S(1)}, bf16[192,192]{1,0:T(8,128)(2,1)}, u32[]{:S(2)}) copy-start(bf16[192,192]{1,0:T(8,128)(2,1)} %constant.46.clone.order_ref) | copy-start | bytes 221188
  109.3 16.5 %collective-permute-start.2 = (bf16[1536,1024]{1,0:T(8,128)(2,1)}, bf16[1536,1024]{1,0:T(8,128)(2,1)}, u32[]{:S(2)}, u32[]{:S(2)}) collective-permute-start(bf16[1536,1024]{1,0:T(8,128)(2,1)} %bitcast.12.lines_ref), channel_id=1, source_target_pairs={{0,1},{1,0},{2,3},{3,2},{4,5},{5,4},{6,7},{7,6},{8,9},{9,8},{10,11... | collective-permute-start | bytes 9437192 | tf_op jit(solution)/shard_map/ppermute | solution.py:71
  109.3 51.0 %all-to-all-start.2 = ((bf16[64,24,1024]{2,1,0:T(8,128)(2,1)}), bf16[64,24,1024]{2,1,0:T(8,128)(2,1)}, u32[]{:S(2)}, u32[]{:S(2)}) async-start(bf16[64,24,1024]{2,1,0:T(8,128)(2,1)} %bitcast.26), calls=%async_computation.2 | async-start | bytes 6291456 | tf_op jit(solution)/shard_map/all_to_all | solution.py:66
  117.2 8.6 %copy-start.11 = (bf16[192,192]{1,0:T(8,128)(2,1)S(1)}, bf16[192,192]{1,0:T(8,128)(2,1)}, u32[]{:S(2)}) copy-start(bf16[192,192]{1,0:T(8,128)(2,1)} %constant.47.clone.order_ref) | copy-start | bytes 221188
  140.3 7.9 %copy-start.6 = (bf16[384,384]{1,0:T(8,128)(2,1)}, bf16[384,384]{1,0:T(8,128)(2,1)S(1)}, u32[]{:S(2)}) copy-start(bf16[384,384]{1,0:T(8,128)(2,1)S(1)} %get-tuple-element.89.dg_other) | copy-start | bytes 884740
  140.3 7.9 %copy-start.8 = (bf16[384,384]{1,0:T(8,128)(2,1)}, bf16[384,384]{1,0:T(8,128)(2,1)S(1)}, u32[]{:S(2)}) copy-start(bf16[384,384]{1,0:T(8,128)(2,1)S(1)} %get-tuple-element.91.du_other) | copy-start | bytes 884740
  140.3 7.9 %collective-permute-start.3 = (bf16[384,4096]{1,0:T(8,128)(2,1)}, bf16[384,4096]{1,0:T(8,128)(2,1)}, u32[]{:S(2)}, u32[]{:S(2)}) collective-permute-start(bf16[384,4096]{1,0:T(8,128)(2,1)} %get-tuple-element.72), channel_id=1, source_target_pairs={{0,1},{1,0},{2,3},{3,2},{4,5},{5,4},{6,7},{7,6},{8,9},{9,8},{10,11... | collective-permute-start | bytes 9437192 | tf_op jit(solution)/shard_map/ppermute | solution.py:71
  140.6 7.7 %copy-start.3 = (bf16[192,192]{1,0:T(8,128)(2,1)S(1)}, bf16[192,192]{1,0:T(8,128)(2,1)}, u32[]{:S(2)}) copy-start(bf16[192,192]{1,0:T(8,128)(2,1)} %constant.46.clone.order_ref) | copy-start | bytes 221188
  160.2 8.3 %copy-start.19 = (f32[128]{0:T(128)S(1)}, f32[128]{0:T(128)}, u32[]{:S(2)}) copy-start(f32[128]{0:T(128)} %copy-done.18) | copy-start | bytes 1540
  160.3 8.3 %copy-start.31 = (f32[128]{0:T(128)S(1)}, f32[128]{0:T(128)}, u32[]{:S(2)}) copy-start(f32[128]{0:T(128)} %copy-done.30) | copy-start | bytes 1540
  160.3 8.9 %copy-start.21 = (f32[128]{0:T(128)S(1)}, f32[128]{0:T(128)}, u32[]{:S(2)}) copy-start(f32[128]{0:T(128)} %copy-done.20) | copy-start | bytes 1540
  160.3 8.9 %copy-start.27 = (pred[128]{0:T(512)(128)(4,1)S(1)}, pred[128]{0:T(512)(128)(4,1)}, u32[]{:S(2)}) copy-start(pred[128]{0:T(512)(128)(4,1)} %copy-done.26) | copy-start | bytes 388
  160.3 9.8 %copy-start.5 = (bf16[384,384]{1,0:T(8,128)(2,1)S(1)}, bf16[384,384]{1,0:T(8,128)(2,1)}, u32[]{:S(2)}) copy-start(bf16[384,384]{1,0:T(8,128)(2,1)} %copy-done.4) | copy-start | bytes 884740
  160.3 48.7 %all-to-all-start.3 = ((bf16[64,24,1024]{2,1,0:T(8,128)(2,1)}), bf16[64,24,1024]{2,1,0:T(8,128)(2,1)}, u32[]{:S(2)}, u32[]{:S(2)}) async-start(bf16[64,24,1024]{2,1,0:T(8,128)(2,1)} %bitcast.24), calls=%async_computation.3 | async-start | bytes 6291456 | tf_op jit(solution)/shard_map/all_to_all | solution.py:66
  177.1 6.1 %copy-start.7 = (bf16[384,384]{1,0:T(8,128)(2,1)S(1)}, bf16[384,384]{1,0:T(8,128)(2,1)}, u32[]{:S(2)}) copy-start(bf16[384,384]{1,0:T(8,128)(2,1)} %copy-done.6) | copy-start | bytes 884740
  177.2 6.1 %copy-start.9 = (bf16[384,384]{1,0:T(8,128)(2,1)S(1)}, bf16[384,384]{1,0:T(8,128)(2,1)}, u32[]{:S(2)}) copy-start(bf16[384,384]{1,0:T(8,128)(2,1)} %copy-done.8) | copy-start | bytes 884740
  183.2 11.6 %copy-start.15 = (f32[128,2]{1,0:T(8,128)S(1)}, f32[128,2]{1,0:T(8,128)}, u32[]{:S(2)}) copy-start(f32[128,2]{1,0:T(8,128)} %copy-done.14) | copy-start | bytes 3076
  183.2 12.0 %copy-start.13 = (f32[128,128]{1,0:T(8,128)S(1)}, f32[128,128]{1,0:T(8,128)}, u32[]{:S(2)}) copy-start(f32[128,128]{1,0:T(8,128)} %param.14) | copy-start | bytes 196612
  183.3 12.0 %copy-start.17 = (f32[128]{0:T(128)S(1)}, f32[128]{0:T(128)}, u32[]{:S(2)}) copy-start(f32[128]{0:T(128)} %copy-done.16) | copy-start | bytes 1540
  183.3 12.0 %copy-start.25 = (s32[128]{0:T(128)S(1)}, s32[128]{0:T(128)}, u32[]{:S(2)}) copy-start(s32[128]{0:T(128)} %param.15) | copy-start | bytes 1540
  183.3 12.0 %copy-start.29 = (s32[128]{0:T(128)S(1)}, s32[128]{0:T(128)}, u32[]{:S(2)}) copy-start(s32[128]{0:T(128)} %copy-done.28) | copy-start | bytes 1540
  183.3 12.0 %copy-start.34 = (f32[128]{0:T(128)S(1)}, f32[128]{0:T(128)}, u32[]{:S(2)}) copy-start(f32[128]{0:T(128)} %multiply_divide_fusion) | copy-start | bytes 1540
  183.3 12.3 %copy-start.23 = (s32[128,2]{0,1:T(2,128)S(1)}, s32[128,2]{0,1:T(2,128)}, u32[]{:S(2)}) copy-start(s32[128,2]{0,1:T(2,128)} %copy-done.22) | copy-start | bytes 3076

commit v4 on v3

--- a/solution.py
+++ b/solution.py
@@ -14,7 +14,6 @@
 TEAM = 8
 LINES = CUT * CAP
 BUSY = 200_000_000_000
-WIDE = ("h", "y", "x", "l")
 ALL = ("y", "x", "l", "h", "c")
 NODE = ("y", "x", "l")
 LOCAL = ("h", "c")
@@ -61,9 +60,25 @@
     return jnp.where(inside[:, None], group_mass[:, None] * pair_share, 0.0)
 
 
+def half_turn():
+    ys, xs, ls = (lax.axis_size(name) for name in NODE)
+    return ((ys // 2) * xs + xs // 2) * ls
+
+
+def peer_groups():
+    ys, xs, ls, hs, cores = (lax.axis_size(name) for name in ALL)
+    experts = ys * xs * ls
+    return [
+        [(((e ^ (half_turn() * c)) * hs) + (h ^ c)) * cores + c for h in range(hs) for e in range(experts)]
+        for c in range(cores)
+    ]
+
+
 def exchange(value):
     blocks = value.reshape(-1, LINES, value.shape[-1])
-    out = lax.all_to_all(blocks, WIDE, split_axis=0, concat_axis=0, tiled=True)
+    out = lax.all_to_all(
+        blocks, ALL, split_axis=0, concat_axis=0, axis_index_groups=peer_groups(), tiled=True
+    )
     return out.reshape(-1, value.shape[-1])
 
 
@@ -115,12 +130,14 @@
         count = group_ref.shape[1]
         group = group_ref[...]
         inside = group < expert_total // GSIZE
+        turn = half_turn() * lax.axis_index("c")
         down = lax.broadcasted_iota(jnp.int32, (count, count), 0)
         along = lax.broadcasted_iota(jnp.int32, (count, count), 1)
         expert = lax.broadcasted_iota(jnp.int32, (expert_total, count), 0)
         targets, hots = [], []
         for k in range(2):
-            target = jnp.where(inside, group * GSIZE + expert_ref[k : k + 1, :], expert_total)
+            place = (group * GSIZE + expert_ref[k : k + 1, :]) ^ turn
+            target = jnp.where(inside, place, expert_total)
             targets.append(target)
             hots.append((expert == target).astype(F32))
         before = (down < along).astype(F32).astype(BF16)

time: 215 us -> 215 us (level)
  waiting for transfers between devices: 60.7 us -> 44 us
  starting transfers between devices: 35.7 us -> 52 us
    all_to_all x4, waiting for transfers between devices: 60.7 us -> 44 us  [exchange(): lax.all_to_all(blocks, ALL, split_axis=0, concat_axis=0, axis_index_group...]
    all_to_all x4, starting transfers between devices: 35.2 us -> 44.7 us  [exchange(): lax.all_to_all(blocks, ALL, split_axis=0, concat_axis=0, axis_index_group...]
    ppermute x4, starting transfers between devices: 0.46 us -> 7.27 us  [swap(): return lax.ppermute(value, 'c', [(0, 1), (1, 0)])]
  transfers between devices with their start and end apart: 8 -> 8, of which waited for: 4 -> 3; matrix products, arithmetic and copies ran while one was open for 2% -> 2% of each run, Pallas kernels for 47% -> 47%
where the time goes in v4:
time: 215 us; the launch traced here: 213 us
  Pallas kernels  110 us (51%)
  starting transfers between devices  52 us (24%)
  waiting for transfers between devices  44 us (20%)
  other arithmetic  4.31 us (2%)
    all_to_all x4, starting transfers between devices, exchange(): lax.all_to_all(blocks, ALL, split_axis=0, concat_axis=0, axis_index_group...  44.7 us
    all_to_all x4, waiting for transfers between devices, exchange(): lax.all_to_all(blocks, ALL, split_axis=0, concat_axis=0, axis_index_group...  44 us
    pallas_call x2, Pallas kernels, forward(): call(forward_kernel, 'forward_own' if own else 'forward_other', outs, BUS...  24 us
    pallas_call x2, Pallas kernels, backward(): call(backward_kernel, 'backward_own' if own else 'backward_other', outs,...  23.1 us
    pallas_call x2, Pallas kernels, to_lines(): call(lines_kernel, 'to_lines', jax.ShapeDtypeStruct((half * CUT, width),...  12.5 us
    pallas_call x1, Pallas kernels, columns_grad(): call(columns_grad_kernel, 'columns_grad', [jax.ShapeDtypeStruct((1, model...  11.5 us
    pallas_call x1, Pallas kernels, product_in(): call(in_kernel, 'product_in', jax.ShapeDtypeStruct((half, model_width), F...  7.69 us
    ppermute x4, starting transfers between devices, swap(): return lax.ppermute(value, 'c', [(0, 1), (1, 0)])  7.27 us
  transfers between devices with their start and end apart: 8, of which 3 were waited for; matrix products, arithmetic and copies ran while one was open for 2% of the time, Pallas kernels for 47%

profile of v4, /device:TPU:0, one launch (start us, length us, event | category | flops | bytes accessed | tf_op | source)
XLA Modules:
  0.0 213.1 jit_solution(8511902155110296276)
XLA Ops:
  0.6 4.4 %pack_tokens.1 = (bf16[2,768,1024]{2,1,0:T(8,128)(2,1)}, s32[2,128]{1,0:T(2,128)S(1)}) custom-call(s32[1,128]{1,0:T(1,128)} %bitcast.28, s32[2,128]{1,0:T(2,128)} %bitcast.29, bf16[128,4096]{1,0:T(8,128)(2,1)} %rows_in.1), custom_call_target="tpu_custom_call" | custom-call | flops 1 | bytes 1 | tf_op jit(solution)/shard_map/pack_tokens/pallas_call | solution.py:169
  5.1 0.0 copy-start.1
  5.1 11.9 %all-to-all-start = ((bf16[64,24,1024]{2,1,0:T(8,128)(2,1)}), bf16[64,24,1024]{2,1,0:T(8,128)(2,1)}, u32[]{:S(2)}, u32[]{:S(2)}) async-start(bf16[64,24,1024]{2,1,0:T(8,128)(2,1)} %bitcast.27), calls=%async_computation | async-start | bytes 6291456 | tf_op jit(solution)/shard_map/all_to_all | solution.py:79
  17.0 0.0 copy-start.32
  17.0 0.1 reduce_max.18
  17.2 0.2 select_reduce_fusion.1
  17.4 0.4 copy-done.22
  17.8 0.1 copy.24
  17.9 0.1 exponential_reduce_fusion
  18.0 0.2 fusion.7
  18.2 0.2 fusion.4
  18.4 0.1 copy-done.28
  18.5 0.3 copy-done.30
  18.8 0.5 copy-done.26
  19.3 0.1 fusion.8
  19.4 0.1 copy.26.weight_ref
  19.5 3.2 %pack_grads.1 = bf16[2,768,1024]{2,1,0:T(8,128)(2,1)} custom-call(s32[2,128]{1,0:T(2,128)S(1)} %get-tuple-element.53.slot_ref, f32[2,128]{1,0:T(2,128)S(1)} %copy.26.weight_ref, bf16[128,4096]{1,0:T(8,128)(2,1)S(1)} %copy-done, bf16[192,192]{1,0:T(8,128)(2,1)S(1)} %copy-done.1), custom_call_target="tpu_custom_call" | custom-call | flops 1 | bytes 1 | tf_op jit(solution)/shard_map/pack_grads/pallas_call | solution.py:205
  22.7 0.4 fusion
  23.1 32.2 %all-to-all-done = bf16[64,24,1024]{2,1,0:T(8,128)(2,1)} async-done(((bf16[64,24,1024]{2,1,0:T(8,128)(2,1)}), bf16[64,24,1024]{2,1,0:T(8,128)(2,1)}, u32[]{:S(2)}, u32[]{:S(2)}) %all-to-all-start) | async-done | bytes 3145760 | tf_op jit(solution)/shard_map/all_to_all | solution.py:79
  55.3 14.1 %all-to-all-start.1 = ((bf16[64,24,1024]{2,1,0:T(8,128)(2,1)}), bf16[64,24,1024]{2,1,0:T(8,128)(2,1)}, u32[]{:S(2)}, u32[]{:S(2)}) async-start(bf16[64,24,1024]{2,1,0:T(8,128)(2,1)} %bitcast.25), calls=%async_computation.1 | async-start | bytes 6291456 | tf_op jit(solution)/shard_map/all_to_all | solution.py:79
  69.4 10.2 %forward_own.1 = (bf16[384,4096]{1,0:T(8,128)(2,1)}, f32[384,384]{1,0:T(8,128)}, f32[384,384]{1,0:T(8,128)}, bf16[384,384]{1,0:T(8,128)(2,1)S(1)}) custom-call(bf16[1536,1024]{1,0:T(8,128)(2,1)} %bitcast.3.lines_ref, bf16[192,192]{1,0:T(8,128)(2,1)S(1)} %copy-done.10, bf16[1,4096,384]{2,1,0:T(8,128)(2,1)} %gate_ref.9, bf16[1,4096,384]{2,1,0:T(8,128)(2,1)} %up_ref.9, ...), custom_call_target="tpu_custom_call" | custom-call | flops 199999995904 | bytes 1 | tf_op jit(solution)/shard_map/forward_own/pallas_call | solution.py:270
  79.6 13.8 %forward_other.1 = (bf16[384,4096]{1,0:T(8,128)(2,1)}, f32[384,384]{1,0:T(8,128)}, f32[384,384]{1,0:T(8,128)}, bf16[384,384]{1,0:T(8,128)(2,1)S(1)}, bf16[384,4096]{1,0:T(8,128)(2,1)}) custom-call(bf16[1536,1024]{1,0:T(8,128)(2,1)} %collective-permute-done.lines_ref, bf16[192,192]{1,0:T(8,128)(2,1)S(1)} %copy-done.10, bf16[1,4096,384]{2,1,0:T(8,128)(2,1)} %gate_ref.9, ...), custom_call_target="tpu_custom_call" | custom-call | flops 199999995904 | bytes 1 | tf_op jit(solution)/shard_map/forward_other/pallas_call | solution.py:270
  93.4 3.0 %collective-permute-start.1 = (bf16[384,4096]{1,0:T(8,128)(2,1)}, bf16[384,4096]{1,0:T(8,128)(2,1)}, u32[]{:S(2)}, u32[]{:S(2)}) collective-permute-start(bf16[384,4096]{1,0:T(8,128)(2,1)} %get-tuple-element.60), channel_id=1, source_target_pairs={{0,1},{1,0},{2,3},{3,2},{4,5},{5,4},{6,7},{7,6},{8,9},{9,8},{10,11... | collective-permute-start | bytes 9437192 | tf_op jit(solution)/shard_map/ppermute | solution.py:86
  96.4 6.0 %product_out.1.total_ref = f32[384,4096]{1,0:T(8,128)} custom-call(bf16[384,384]{1,0:T(8,128)(2,1)S(1)} %get-tuple-element.94.hidden_ref.hidden_own, bf16[1,384,4096]{2,1,0:T(8,128)(2,1)} %down_ref.9), custom_call_target="tpu_custom_call" | custom-call | flops 199999995904 | bytes 1 | tf_op jit(solution)/shard_map/product_out/pallas_call | solution.py:358
  102.4 6.2 %to_lines.2 = bf16[1536,1024]{1,0:T(8,128)(2,1)} custom-call(f32[384,4096]{1,0:T(8,128)} %product_out.1.total_ref, bf16[384,4096]{1,0:T(8,128)(2,1)} %collective-permute-done.1.arrived_ref, bf16[192,192]{1,0:T(8,128)(2,1)S(1)} %copy-done.2), custom_call_target="tpu_custom_call" | custom-call | flops 1 | bytes 1 | tf_op jit(solution)/shard_map/to_lines/pallas_call | solution.py:410
  108.7 1.0 all-to-all-done.1
  109.7 8.2 %all-to-all-start.2 = ((bf16[64,24,1024]{2,1,0:T(8,128)(2,1)}), bf16[64,24,1024]{2,1,0:T(8,128)(2,1)}, u32[]{:S(2)}, u32[]{:S(2)}) async-start(bf16[64,24,1024]{2,1,0:T(8,128)(2,1)} %bitcast.26), calls=%async_computation.2 | async-start | bytes 6291456 | tf_op jit(solution)/shard_map/all_to_all | solution.py:79
  117.9 0.0 copy-start.11
  117.9 8.6 %backward_own.1 = (bf16[384,4096]{1,0:T(8,128)(2,1)}, bf16[384,384]{1,0:T(8,128)(2,1)S(1)}, bf16[384,384]{1,0:T(8,128)(2,1)S(1)}) custom-call(bf16[1536,1024]{1,0:T(8,128)(2,1)} %bitcast.12.lines_ref, bf16[192,192]{1,0:T(8,128)(2,1)S(1)} %copy-done.10, bf16[1,384,4096]{2,1,0:T(8,128)(2,1)} %down_ref.9, f32[384,384]{1,0:T(8,128)} %get-tuple-element.63.g_ref, ...), custom_call_target="tpu_custom_call" | custom-call | flops 199999995904 | bytes 1 | tf_op jit(solution)/shard_map/backward_own/pallas_call | solution.py:330
  126.5 14.5 %backward_other.1 = (bf16[384,4096]{1,0:T(8,128)(2,1)}, bf16[384,384]{1,0:T(8,128)(2,1)S(1)}, bf16[384,384]{1,0:T(8,128)(2,1)S(1)}, bf16[384,4096]{1,0:T(8,128)(2,1)}) custom-call(bf16[1536,1024]{1,0:T(8,128)(2,1)} %collective-permute-done.2.lines_ref, bf16[192,192]{1,0:T(8,128)(2,1)S(1)} %copy-done.11, bf16[1,384,4096]{2,1,0:T(8,128)(2,1)} %down_ref.9, ...), custom_call_target="tpu_custom_call" | custom-call | flops 199999995904 | bytes 1 | tf_op jit(solution)/shard_map/backward_other/pallas_call | solution.py:330
  141.0 4.3 %collective-permute-start.3 = (bf16[384,4096]{1,0:T(8,128)(2,1)}, bf16[384,4096]{1,0:T(8,128)(2,1)}, u32[]{:S(2)}, u32[]{:S(2)}) collective-permute-start(bf16[384,4096]{1,0:T(8,128)(2,1)} %get-tuple-element.72), channel_id=1, source_target_pairs={{0,1},{1,0},{2,3},{3,2},{4,5},{5,4},{6,7},{7,6},{8,9},{9,8},{10,11... | collective-permute-start | bytes 9437192 | tf_op jit(solution)/shard_map/ppermute | solution.py:86
  145.3 7.7 %product_in.1.total_ref = f32[384,4096]{1,0:T(8,128)} custom-call(bf16[384,384]{1,0:T(8,128)(2,1)S(1)} %get-tuple-element.88.dg_ref.dg_own, bf16[384,384]{1,0:T(8,128)(2,1)S(1)} %get-tuple-element.90.du_ref.du_own, bf16[1,4096,384]{2,1,0:T(8,128)(2,1)} %gate_ref.9, bf16[1,4096,384]{2,1,0:T(8,128)(2,1)} %up_ref.9), custom_call_target="tpu_custom_call" | custom-call | flops 199999995904 | bytes 1 | tf_op jit(solution)/shard_map/product_in/pallas_call | solution.py:381
  153.0 6.2 %to_lines.3 = bf16[1536,1024]{1,0:T(8,128)(2,1)} custom-call(f32[384,4096]{1,0:T(8,128)} %product_in.1.total_ref, bf16[384,4096]{1,0:T(8,128)(2,1)} %collective-permute-done.3.arrived_ref, bf16[192,192]{1,0:T(8,128)(2,1)S(1)} %copy-done.3), custom_call_target="tpu_custom_call" | custom-call | flops 1 | bytes 1 | tf_op jit(solution)/shard_map/to_lines/pallas_call | solution.py:410
  159.3 10.6 %all-to-all-start.3 = ((bf16[64,24,1024]{2,1,0:T(8,128)(2,1)}), bf16[64,24,1024]{2,1,0:T(8,128)(2,1)}, u32[]{:S(2)}, u32[]{:S(2)}) async-start(bf16[64,24,1024]{2,1,0:T(8,128)(2,1)} %bitcast.24), calls=%async_computation.3 | async-start | bytes 6291456 | tf_op jit(solution)/shard_map/all_to_all | solution.py:79
  169.9 0.5 multiply_divide_fusion
  170.4 1.0 multiply_select_fusion.weight_ref
  171.4 7.1 %rows_grad.1 = bf16[1,384,4096]{2,1,0:T(8,128)(2,1)} custom-call(bf16[384,384]{1,0:T(8,128)(2,1)S(1)} %copy-done.5, bf16[384,384]{1,0:T(8,128)(2,1)S(1)} %get-tuple-element.95.hidden_other, bf16[384,4096]{1,0:T(8,128)(2,1)} %get-tuple-element.96.own, bf16[384,4096]{1,0:T(8,128)(2,1)} %get-tuple-element.97.other), custom_call_target="tpu_custom_call" | custom-call | flops 1 | bytes 1 | tf_op jit(solution)/shard_map/rows_grad/pallas_call | solution.py:457
  178.5 6.1 %mix.1 = (bf16[128,4096]{1,0:T(8,128)(2,1)}, f32[128,2]{1,0:T(8,128)S(1)}) custom-call(bf16[512,768]{1,0:T(8,128)(2,1)S(1)} %get-tuple-element.54.first_ref, bf16[512,768]{1,0:T(8,128)(2,1)S(1)} %get-tuple-element.55.second_ref, bf16[1536,1024]{1,0:T(8,128)(2,1)} %bitcast.14.lines_ref, bf16[128,4096]{1,0:T(8,128)(2,1)} %grad_ref.1, ...), custom_call_target="tpu_custom_call" | custom-call | flops 1 | bytes 1 | tf_op jit(solution)/shard_map/mix/pallas_call | solution.py:498
  184.6 11.5 %columns_grad.1 = (bf16[1,4096,384]{2,1,0:T(8,128)(2,1)}, bf16[1,4096,384]{2,1,0:T(8,128)(2,1)}) custom-call(bf16[384,4096]{1,0:T(8,128)(2,1)} %get-tuple-element.86.own, bf16[384,4096]{1,0:T(8,128)(2,1)} %get-tuple-element.87.other, bf16[384,384]{1,0:T(8,128)(2,1)S(1)} %get-tuple-element.88.dg_ref.dg_own, bf16[384,384]{1,0:T(8,128)(2,1)S(1)} %copy-done.7, ...), custom_call_target="tpu_custom_call" | custom-call | flops 1 | bytes 1 | tf_op jit(solution)/shard_map/columns_grad/pallas_call | solution.py:436
  196.2 0.2 multiply_reduce_fusion
  196.4 0.1 add_multiply_fusion
  196.5 0.1 copy.28
  196.6 0.0 copy-done.25
  196.6 0.2 fusion.6
  196.9 0.1 select_reduce_fusion
  197.0 0.8 fusion.3
  197.8 10.8 %all-to-all-done.3 = bf16[64,24,1024]{2,1,0:T(8,128)(2,1)} async-done(((bf16[64,24,1024]{2,1,0:T(8,128)(2,1)}), bf16[64,24,1024]{2,1,0:T(8,128)(2,1)}, u32[]{:S(2)}, u32[]{:S(2)}) %all-to-all-start.3) | async-done | bytes 3145760 | tf_op jit(solution)/shard_map/all_to_all | solution.py:79
  208.6 4.5 %unpack.1 = bf16[128,4096]{1,0:T(8,128)(2,1)} custom-call(bf16[512,768]{1,0:T(8,128)(2,1)S(1)} %get-tuple-element.83.either_ref, bf16[1536,1024]{1,0:T(8,128)(2,1)} %bitcast.16.lines_ref), custom_call_target="tpu_custom_call" | custom-call | flops 1 | bytes 1 | tf_op jit(solution)/shard_map/unpack/pallas_call | solution.py:530
  (81 shorter events, 0.2 us)
Async XLA Ops:
  5.1 11.9 %copy-start.12 = (f32[128,128]{1,0:T(8,128)S(1)}, f32[128,128]{1,0:T(8,128)}, u32[]{:S(2)}) copy-start(f32[128,128]{1,0:T(8,128)} %param.14) | copy-start | bytes 196612
  5.1 12.1 %copy-start.24 = (s32[128]{0:T(128)S(1)}, s32[128]{0:T(128)}, u32[]{:S(2)}) copy-start(s32[128]{0:T(128)} %param.15) | copy-start | bytes 1540
  5.1 12.1 %copy-start.33 = (s32[128,2]{0,1:T(2,128)S(1)}, s32[128,2]{0,1:T(2,128)}, u32[]{:S(2)}) copy-start(s32[128,2]{0,1:T(2,128)} %param.16) | copy-start | bytes 3076
  5.1 14.4 %copy-start = (bf16[128,4096]{1,0:T(8,128)(2,1)S(1)}, bf16[128,4096]{1,0:T(8,128)(2,1)}, u32[]{:S(2)}) copy-start(bf16[128,4096]{1,0:T(8,128)(2,1)} %grad_ref.1) | copy-start | bytes 3145732
  5.1 14.4 %copy-start.1 = (bf16[192,192]{1,0:T(8,128)(2,1)S(1)}, bf16[192,192]{1,0:T(8,128)(2,1)}, u32[]{:S(2)}) copy-start(bf16[192,192]{1,0:T(8,128)(2,1)} %constant.46.clone.order_ref) | copy-start | bytes 221188
  5.1 50.2 %all-to-all-start = ((bf16[64,24,1024]{2,1,0:T(8,128)(2,1)}), bf16[64,24,1024]{2,1,0:T(8,128)(2,1)}, u32[]{:S(2)}, u32[]{:S(2)}) async-start(bf16[64,24,1024]{2,1,0:T(8,128)(2,1)} %bitcast.27), calls=%async_computation | async-start | bytes 6291456 | tf_op jit(solution)/shard_map/all_to_all | solution.py:79
  17.0 5.7 %copy-start.32 = (s32[768]{0:T(1024)S(1)}, s32[768]{0:T(1024)}, u32[]{:S(2)}) copy-start(s32[768]{0:T(1024)} %constant.52) | copy-start | bytes 9220
  17.1 1.3 copy-start.16
  17.2 0.6 copy-start.22
  17.9 4.8 %copy-start.14 = (f32[128,2]{1,0:T(8,128)}, f32[128,2]{1,0:T(8,128)S(1)}, u32[]{:S(2)}) copy-start(f32[128,2]{1,0:T(8,128)S(1)} %copy.24) | copy-start | bytes 3076
  17.9 0.6 copy-start.28
  18.0 4.7 %copy-start.18 = (f32[128]{0:T(128)}, f32[128]{0:T(128)S(1)}, u32[]{:S(2)}) copy-start(f32[128]{0:T(128)S(1)} %exponential_reduce_fusion) | copy-start | bytes 1540
  18.2 0.5 copy-start.30
  18.8 3.9 %copy-start.20 = (f32[128]{0:T(128)}, f32[128]{0:T(128)S(1)}, u32[]{:S(2)}) copy-start(f32[128]{0:T(128)S(1)} %fusion.4) | copy-start | bytes 1540
  18.8 0.5 copy-start.26
  55.3 24.3 %collective-permute-start = (bf16[1536,1024]{1,0:T(8,128)(2,1)}, bf16[1536,1024]{1,0:T(8,128)(2,1)}, u32[]{:S(2)}, u32[]{:S(2)}) collective-permute-start(bf16[1536,1024]{1,0:T(8,128)(2,1)} %bitcast.3.lines_ref), channel_id=1, source_target_pairs={{0,1},{1,0},{2,3},{3,2},{4,5},{5,4},{6,7},{7,6},{8,9},{9,8},{10,11... | collective-permute-start | bytes 9437192 | tf_op jit(solution)/shard_map/ppermute | solution.py:86
  55.3 14.1 %copy-start.10 = (bf16[192,192]{1,0:T(8,128)(2,1)S(1)}, bf16[192,192]{1,0:T(8,128)(2,1)}, u32[]{:S(2)}) copy-start(bf16[192,192]{1,0:T(8,128)(2,1)} %constant.47.clone.order_ref) | copy-start | bytes 221188
  55.3 54.4 %all-to-all-start.1 = ((bf16[64,24,1024]{2,1,0:T(8,128)(2,1)}), bf16[64,24,1024]{2,1,0:T(8,128)(2,1)}, u32[]{:S(2)}, u32[]{:S(2)}) async-start(bf16[64,24,1024]{2,1,0:T(8,128)(2,1)} %bitcast.25), calls=%async_computation.1 | async-start | bytes 6291456 | tf_op jit(solution)/shard_map/all_to_all | solution.py:79
  79.6 16.8 %copy-start.4 = (bf16[384,384]{1,0:T(8,128)(2,1)}, bf16[384,384]{1,0:T(8,128)(2,1)S(1)}, u32[]{:S(2)}) copy-start(bf16[384,384]{1,0:T(8,128)(2,1)S(1)} %get-tuple-element.94.hidden_ref.hidden_own) | copy-start | bytes 884740
  93.4 9.0 %collective-permute-start.1 = (bf16[384,4096]{1,0:T(8,128)(2,1)}, bf16[384,4096]{1,0:T(8,128)(2,1)}, u32[]{:S(2)}, u32[]{:S(2)}) collective-permute-start(bf16[384,4096]{1,0:T(8,128)(2,1)} %get-tuple-element.60), channel_id=1, source_target_pairs={{0,1},{1,0},{2,3},{3,2},{4,5},{5,4},{6,7},{7,6},{8,9},{9,8},{10,11... | collective-permute-start | bytes 9437192 | tf_op jit(solution)/shard_map/ppermute | solution.py:86
  96.4 6.0 %copy-start.2 = (bf16[192,192]{1,0:T(8,128)(2,1)S(1)}, bf16[192,192]{1,0:T(8,128)(2,1)}, u32[]{:S(2)}) copy-start(bf16[192,192]{1,0:T(8,128)(2,1)} %constant.46.clone.order_ref) | copy-start | bytes 221188
  109.7 16.8 %collective-permute-start.2 = (bf16[1536,1024]{1,0:T(8,128)(2,1)}, bf16[1536,1024]{1,0:T(8,128)(2,1)}, u32[]{:S(2)}, u32[]{:S(2)}) collective-permute-start(bf16[1536,1024]{1,0:T(8,128)(2,1)} %bitcast.12.lines_ref), channel_id=1, source_target_pairs={{0,1},{1,0},{2,3},{3,2},{4,5},{5,4},{6,7},{7,6},{8,9},{9,8},{10,11... | collective-permute-start | bytes 9437192 | tf_op jit(solution)/shard_map/ppermute | solution.py:86
  109.7 49.5 %all-to-all-start.2 = ((bf16[64,24,1024]{2,1,0:T(8,128)(2,1)}), bf16[64,24,1024]{2,1,0:T(8,128)(2,1)}, u32[]{:S(2)}, u32[]{:S(2)}) async-start(bf16[64,24,1024]{2,1,0:T(8,128)(2,1)} %bitcast.26), calls=%async_computation.2 | async-start | bytes 6291456 | tf_op jit(solution)/shard_map/all_to_all | solution.py:79
  117.9 8.6 %copy-start.11 = (bf16[192,192]{1,0:T(8,128)(2,1)S(1)}, bf16[192,192]{1,0:T(8,128)(2,1)}, u32[]{:S(2)}) copy-start(bf16[192,192]{1,0:T(8,128)(2,1)} %constant.47.clone.order_ref) | copy-start | bytes 221188
  141.0 12.0 %copy-start.6 = (bf16[384,384]{1,0:T(8,128)(2,1)}, bf16[384,384]{1,0:T(8,128)(2,1)S(1)}, u32[]{:S(2)}) copy-start(bf16[384,384]{1,0:T(8,128)(2,1)S(1)} %get-tuple-element.89.dg_other) | copy-start | bytes 884740
  141.0 12.0 %copy-start.8 = (bf16[384,384]{1,0:T(8,128)(2,1)}, bf16[384,384]{1,0:T(8,128)(2,1)S(1)}, u32[]{:S(2)}) copy-start(bf16[384,384]{1,0:T(8,128)(2,1)S(1)} %get-tuple-element.91.du_other) | copy-start | bytes 884740
  141.0 12.0 %collective-permute-start.3 = (bf16[384,4096]{1,0:T(8,128)(2,1)}, bf16[384,4096]{1,0:T(8,128)(2,1)}, u32[]{:S(2)}, u32[]{:S(2)}) collective-permute-start(bf16[384,4096]{1,0:T(8,128)(2,1)} %get-tuple-element.72), channel_id=1, source_target_pairs={{0,1},{1,0},{2,3},{3,2},{4,5},{5,4},{6,7},{7,6},{8,9},{9,8},{10,11... | collective-permute-start | bytes 9437192 | tf_op jit(solution)/shard_map/ppermute | solution.py:86
  145.3 7.7 %copy-start.3 = (bf16[192,192]{1,0:T(8,128)(2,1)S(1)}, bf16[192,192]{1,0:T(8,128)(2,1)}, u32[]{:S(2)}) copy-start(bf16[192,192]{1,0:T(8,128)(2,1)} %constant.46.clone.order_ref) | copy-start | bytes 221188
  159.2 10.6 %copy-start.19 = (f32[128]{0:T(128)S(1)}, f32[128]{0:T(128)}, u32[]{:S(2)}) copy-start(f32[128]{0:T(128)} %copy-done.18) | copy-start | bytes 1540
  159.2 10.7 %copy-start.31 = (f32[128]{0:T(128)S(1)}, f32[128]{0:T(128)}, u32[]{:S(2)}) copy-start(f32[128]{0:T(128)} %copy-done.30) | copy-start | bytes 1540
  159.2 11.2 %copy-start.21 = (f32[128]{0:T(128)S(1)}, f32[128]{0:T(128)}, u32[]{:S(2)}) copy-start(f32[128]{0:T(128)} %copy-done.20) | copy-start | bytes 1540
  159.2 11.2 %copy-start.27 = (pred[128]{0:T(512)(128)(4,1)S(1)}, pred[128]{0:T(512)(128)(4,1)}, u32[]{:S(2)}) copy-start(pred[128]{0:T(512)(128)(4,1)} %copy-done.26) | copy-start | bytes 388
  159.2 12.1 %copy-start.5 = (bf16[384,384]{1,0:T(8,128)(2,1)S(1)}, bf16[384,384]{1,0:T(8,128)(2,1)}, u32[]{:S(2)}) copy-start(bf16[384,384]{1,0:T(8,128)(2,1)} %copy-done.4) | copy-start | bytes 884740
  159.3 49.4 %all-to-all-start.3 = ((bf16[64,24,1024]{2,1,0:T(8,128)(2,1)}), bf16[64,24,1024]{2,1,0:T(8,128)(2,1)}, u32[]{:S(2)}, u32[]{:S(2)}) async-start(bf16[64,24,1024]{2,1,0:T(8,128)(2,1)} %bitcast.24), calls=%async_computation.3 | async-start | bytes 6291456 | tf_op jit(solution)/shard_map/all_to_all | solution.py:79
  178.5 6.1 %copy-start.7 = (bf16[384,384]{1,0:T(8,128)(2,1)S(1)}, bf16[384,384]{1,0:T(8,128)(2,1)}, u32[]{:S(2)}) copy-start(bf16[384,384]{1,0:T(8,128)(2,1)} %copy-done.6) | copy-start | bytes 884740
  178.5 6.1 %copy-start.9 = (bf16[384,384]{1,0:T(8,128)(2,1)S(1)}, bf16[384,384]{1,0:T(8,128)(2,1)}, u32[]{:S(2)}) copy-start(bf16[384,384]{1,0:T(8,128)(2,1)} %copy-done.8) | copy-start | bytes 884740
  184.5 11.6 %copy-start.15 = (f32[128,2]{1,0:T(8,128)S(1)}, f32[128,2]{1,0:T(8,128)}, u32[]{:S(2)}) copy-start(f32[128,2]{1,0:T(8,128)} %copy-done.14) | copy-start | bytes 3076
  184.5 12.0 %copy-start.13 = (f32[128,128]{1,0:T(8,128)S(1)}, f32[128,128]{1,0:T(8,128)}, u32[]{:S(2)}) copy-start(f32[128,128]{1,0:T(8,128)} %param.14) | copy-start | bytes 196612
  184.6 12.0 %copy-start.17 = (f32[128]{0:T(128)S(1)}, f32[128]{0:T(128)}, u32[]{:S(2)}) copy-start(f32[128]{0:T(128)} %copy-done.16) | copy-start | bytes 1540
  184.6 12.0 %copy-start.25 = (s32[128]{0:T(128)S(1)}, s32[128]{0:T(128)}, u32[]{:S(2)}) copy-start(s32[128]{0:T(128)} %param.15) | copy-start | bytes 1540
  184.6 12.0 %copy-start.29 = (s32[128]{0:T(128)S(1)}, s32[128]{0:T(128)}, u32[]{:S(2)}) copy-start(s32[128]{0:T(128)} %copy-done.28) | copy-start | bytes 1540
  184.6 12.0 %copy-start.34 = (f32[128]{0:T(128)S(1)}, f32[128]{0:T(128)}, u32[]{:S(2)}) copy-start(f32[128]{0:T(128)} %multiply_divide_fusion) | copy-start | bytes 1540
  184.6 12.3 %copy-start.23 = (s32[128,2]{0,1:T(2,128)S(1)}, s32[128,2]{0,1:T(2,128)}, u32[]{:S(2)}) copy-start(s32[128,2]{0,1:T(2,128)} %copy-done.22) | copy-start | bytes 3076

commit v5 on v4

--- a/solution.py
+++ b/solution.py
@@ -348,7 +348,7 @@
 
 
 def out_kernel(hidden_ref, down_ref, total_ref):
-    total_ref[...] = dot(hidden_ref[...], down_ref[...])
+    total_ref[...] = dot(hidden_ref[...], down_ref[...]).astype(BF16)
 
 
 def product_out(hidden, w_down):
@@ -358,7 +358,7 @@
     return call(
         out_kernel,
         "product_out",
-        jax.ShapeDtypeStruct((half, model_width), F32),
+        jax.ShapeDtypeStruct((half, model_width), BF16),
         BUSY,
         grid=(CUT,),
         in_specs=[
@@ -370,7 +370,9 @@
 
 
 def in_kernel(dg_ref, du_ref, gate_ref, up_ref, total_ref):
-    total_ref[...] = across(dg_ref[...], gate_ref[...]) + across(du_ref[...], up_ref[...])
+    total_ref[...] = (
+        across(dg_ref[...], gate_ref[...]) + across(du_ref[...], up_ref[...])
+    ).astype(BF16)
 
 
 def product_in(dg, du, w_gate, w_up):
@@ -381,7 +383,7 @@
     return call(
         in_kernel,
         "product_in",
-        jax.ShapeDtypeStruct((half, model_width), F32),
+        jax.ShapeDtypeStruct((half, model_width), BF16),
         BUSY,
         grid=(CUT,),
         in_specs=[whole((half, units)), whole((half, units)), weight_spec, weight_spec],
@@ -397,7 +399,8 @@
         pieces = []
         for j in range(CUT):
             part = slice(j * width, (j + 1) * width)
-            pieces.append((total_ref[team, part] + arrived_ref[team, part].astype(F32)).astype(BF16))
+            both = total_ref[team, part].astype(F32) + arrived_ref[team, part].astype(F32)
+            pieces.append(both.astype(BF16))
         held = jnp.concatenate(pieces, axis=0)
         out_ref[t * step : (t + 1) * step, :] = dot(order_ref[...], held).astype(BF16)
 

time: 215 us -> 213 us (level)
  Pallas kernels: 110 us -> 107 us
  transfers between devices with their start and end apart: 8 -> 8, of which waited for: 3 -> 5; matrix products, arithmetic and copies ran while one was open for 2% -> 2% of each run, Pallas kernels for 47% -> 47%
where the time goes in v5:
time: 213 us; the launch traced here: 211 us
  Pallas kernels  107 us (50%)
  starting transfers between devices  52.3 us (25%)
  waiting for transfers between devices  44.1 us (21%)
  other arithmetic  4.3 us (2%)
    all_to_all x4, starting transfers between devices, exchange(): lax.all_to_all(blocks, ALL, split_axis=0, concat_axis=0, axis_index_group...  45 us
    all_to_all x4, waiting for transfers between devices, exchange(): lax.all_to_all(blocks, ALL, split_axis=0, concat_axis=0, axis_index_group...  43.7 us
    pallas_call x2, Pallas kernels, forward(): call(forward_kernel, 'forward_own' if own else 'forward_other', outs, BUS...  24 us
    pallas_call x2, Pallas kernels, backward(): call(backward_kernel, 'backward_own' if own else 'backward_other', outs,...  23.1 us
    pallas_call x1, Pallas kernels, columns_grad(): call(columns_grad_kernel, 'columns_grad', [jax.ShapeDtypeStruct((1, model...  11.5 us
    pallas_call x2, Pallas kernels, to_lines(): call(lines_kernel, 'to_lines', jax.ShapeDtypeStruct((half * CUT, width),...  11.1 us
    ppermute x4, starting transfers between devices, swap(): return lax.ppermute(value, 'c', [(0, 1), (1, 0)])  7.2 us
    pallas_call x1, Pallas kernels, product_in(): call(in_kernel, 'product_in', jax.ShapeDtypeStruct((half, model_width), B...  7.11 us
  transfers between devices with their start and end apart: 8, of which 5 were waited for; matrix products, arithmetic and copies ran while one was open for 2% of the time, Pallas kernels for 47%

profile of v5, /device:TPU:0, one launch (start us, length us, event | category | flops | bytes accessed | tf_op | source)
XLA Modules:
  0.0 210.6 jit_solution(9979862094432988712)
XLA Ops:
  0.6 4.4 %pack_tokens.1 = (bf16[2,768,1024]{2,1,0:T(8,128)(2,1)}, s32[2,128]{1,0:T(2,128)S(1)}) custom-call(s32[1,128]{1,0:T(1,128)} %bitcast.28, s32[2,128]{1,0:T(2,128)} %bitcast.29, bf16[128,4096]{1,0:T(8,128)(2,1)} %rows_in.1), custom_call_target="tpu_custom_call" | custom-call | flops 1 | bytes 1 | tf_op jit(solution)/shard_map/pack_tokens/pallas_call | solution.py:169
  5.1 0.0 copy-start.1
  5.1 11.9 %all-to-all-start = ((bf16[64,24,1024]{2,1,0:T(8,128)(2,1)}), bf16[64,24,1024]{2,1,0:T(8,128)(2,1)}, u32[]{:S(2)}, u32[]{:S(2)}) async-start(bf16[64,24,1024]{2,1,0:T(8,128)(2,1)} %bitcast.27), calls=%async_computation | async-start | bytes 6291456 | tf_op jit(solution)/shard_map/all_to_all | solution.py:79
  17.0 0.1 reduce_max.18
  17.2 0.2 select_reduce_fusion.1
  17.4 0.4 copy-done.22
  17.7 0.1 copy.24
  17.9 0.1 exponential_reduce_fusion
  18.0 0.2 fusion.7
  18.2 0.2 fusion.4
  18.4 0.0 copy-done.28
  18.5 0.3 copy-done.30
  18.7 0.6 copy-done.26
  19.3 0.1 fusion.8
  19.4 0.1 copy.26.weight_ref
  19.5 3.2 %pack_grads.1 = bf16[2,768,1024]{2,1,0:T(8,128)(2,1)} custom-call(s32[2,128]{1,0:T(2,128)S(1)} %get-tuple-element.53.slot_ref, f32[2,128]{1,0:T(2,128)S(1)} %copy.26.weight_ref, bf16[128,4096]{1,0:T(8,128)(2,1)S(1)} %copy-done, bf16[192,192]{1,0:T(8,128)(2,1)S(1)} %copy-done.1), custom_call_target="tpu_custom_call" | custom-call | flops 1 | bytes 1 | tf_op jit(solution)/shard_map/pack_grads/pallas_call | solution.py:205
  22.7 0.4 fusion
  23.1 32.2 %all-to-all-done = bf16[64,24,1024]{2,1,0:T(8,128)(2,1)} async-done(((bf16[64,24,1024]{2,1,0:T(8,128)(2,1)}), bf16[64,24,1024]{2,1,0:T(8,128)(2,1)}, u32[]{:S(2)}, u32[]{:S(2)}) %all-to-all-start) | async-done | bytes 3145760 | tf_op jit(solution)/shard_map/all_to_all | solution.py:79
  55.3 14.1 %all-to-all-start.1 = ((bf16[64,24,1024]{2,1,0:T(8,128)(2,1)}), bf16[64,24,1024]{2,1,0:T(8,128)(2,1)}, u32[]{:S(2)}, u32[]{:S(2)}) async-start(bf16[64,24,1024]{2,1,0:T(8,128)(2,1)} %bitcast.25), calls=%async_computation.1 | async-start | bytes 6291456 | tf_op jit(solution)/shard_map/all_to_all | solution.py:79
  69.4 10.2 %forward_own.1 = (bf16[384,4096]{1,0:T(8,128)(2,1)}, f32[384,384]{1,0:T(8,128)}, f32[384,384]{1,0:T(8,128)}, bf16[384,384]{1,0:T(8,128)(2,1)S(1)}) custom-call(bf16[1536,1024]{1,0:T(8,128)(2,1)} %bitcast.3.lines_ref, bf16[192,192]{1,0:T(8,128)(2,1)S(1)} %copy-done.10, bf16[1,4096,384]{2,1,0:T(8,128)(2,1)} %gate_ref.9, bf16[1,4096,384]{2,1,0:T(8,128)(2,1)} %up_ref.9, ...), custom_call_target="tpu_custom_call" | custom-call | flops 199999995904 | bytes 1 | tf_op jit(solution)/shard_map/forward_own/pallas_call | solution.py:270
  79.6 13.8 %forward_other.1 = (bf16[384,4096]{1,0:T(8,128)(2,1)}, f32[384,384]{1,0:T(8,128)}, f32[384,384]{1,0:T(8,128)}, bf16[384,384]{1,0:T(8,128)(2,1)S(1)}, bf16[384,4096]{1,0:T(8,128)(2,1)}) custom-call(bf16[1536,1024]{1,0:T(8,128)(2,1)} %collective-permute-done.lines_ref, bf16[192,192]{1,0:T(8,128)(2,1)S(1)} %copy-done.10, bf16[1,4096,384]{2,1,0:T(8,128)(2,1)} %gate_ref.9, ...), custom_call_target="tpu_custom_call" | custom-call | flops 199999995904 | bytes 1 | tf_op jit(solution)/shard_map/forward_other/pallas_call | solution.py:270
  93.4 3.0 %collective-permute-start.1 = (bf16[384,4096]{1,0:T(8,128)(2,1)}, bf16[384,4096]{1,0:T(8,128)(2,1)}, u32[]{:S(2)}, u32[]{:S(2)}) collective-permute-start(bf16[384,4096]{1,0:T(8,128)(2,1)} %get-tuple-element.60), channel_id=1, source_target_pairs={{0,1},{1,0},{2,3},{3,2},{4,5},{5,4},{6,7},{7,6},{8,9},{9,8},{10,11... | collective-permute-start | bytes 9437192 | tf_op jit(solution)/shard_map/ppermute | solution.py:86
  96.4 5.3 %product_out.1.total_ref = bf16[384,4096]{1,0:T(8,128)(2,1)} custom-call(bf16[384,384]{1,0:T(8,128)(2,1)S(1)} %get-tuple-element.94.hidden_ref.hidden_own, bf16[1,384,4096]{2,1,0:T(8,128)(2,1)} %down_ref.9), custom_call_target="tpu_custom_call" | custom-call | flops 199999995904 | bytes 1 | tf_op jit(solution)/shard_map/product_out/pallas_call | solution.py:358
  101.7 0.4 collective-permute-done.1.arrived_ref
  102.1 5.5 %to_lines.2 = bf16[1536,1024]{1,0:T(8,128)(2,1)} custom-call(bf16[384,4096]{1,0:T(8,128)(2,1)} %product_out.1.total_ref, bf16[384,4096]{1,0:T(8,128)(2,1)} %collective-permute-done.1.arrived_ref, bf16[192,192]{1,0:T(8,128)(2,1)S(1)} %copy-done.2), custom_call_target="tpu_custom_call" | custom-call | flops 1 | bytes 1 | tf_op jit(solution)/shard_map/to_lines/pallas_call | solution.py:413
  107.6 2.2 %all-to-all-done.1 = bf16[64,24,1024]{2,1,0:T(8,128)(2,1)} async-done(((bf16[64,24,1024]{2,1,0:T(8,128)(2,1)}), bf16[64,24,1024]{2,1,0:T(8,128)(2,1)}, u32[]{:S(2)}, u32[]{:S(2)}) %all-to-all-start.1) | async-done | bytes 3145760 | tf_op jit(solution)/shard_map/all_to_all | solution.py:79
  109.8 8.1 %all-to-all-start.2 = ((bf16[64,24,1024]{2,1,0:T(8,128)(2,1)}), bf16[64,24,1024]{2,1,0:T(8,128)(2,1)}, u32[]{:S(2)}, u32[]{:S(2)}) async-start(bf16[64,24,1024]{2,1,0:T(8,128)(2,1)} %bitcast.26), calls=%async_computation.2 | async-start | bytes 6291456 | tf_op jit(solution)/shard_map/all_to_all | solution.py:79
  118.0 8.6 %backward_own.1 = (bf16[384,4096]{1,0:T(8,128)(2,1)}, bf16[384,384]{1,0:T(8,128)(2,1)S(1)}, bf16[384,384]{1,0:T(8,128)(2,1)S(1)}) custom-call(bf16[1536,1024]{1,0:T(8,128)(2,1)} %bitcast.12.lines_ref, bf16[192,192]{1,0:T(8,128)(2,1)S(1)} %copy-done.10, bf16[1,384,4096]{2,1,0:T(8,128)(2,1)} %down_ref.9, f32[384,384]{1,0:T(8,128)} %get-tuple-element.63.g_ref, ...), custom_call_target="tpu_custom_call" | custom-call | flops 199999995904 | bytes 1 | tf_op jit(solution)/shard_map/backward_own/pallas_call | solution.py:330
  126.5 14.5 %backward_other.1 = (bf16[384,4096]{1,0:T(8,128)(2,1)}, bf16[384,384]{1,0:T(8,128)(2,1)S(1)}, bf16[384,384]{1,0:T(8,128)(2,1)S(1)}, bf16[384,4096]{1,0:T(8,128)(2,1)}) custom-call(bf16[1536,1024]{1,0:T(8,128)(2,1)} %collective-permute-done.2.lines_ref, bf16[192,192]{1,0:T(8,128)(2,1)S(1)} %copy-done.11, bf16[1,384,4096]{2,1,0:T(8,128)(2,1)} %down_ref.9, ...), custom_call_target="tpu_custom_call" | custom-call | flops 199999995904 | bytes 1 | tf_op jit(solution)/shard_map/backward_other/pallas_call | solution.py:330
  141.0 4.2 %collective-permute-start.3 = (bf16[384,4096]{1,0:T(8,128)(2,1)}, bf16[384,4096]{1,0:T(8,128)(2,1)}, u32[]{:S(2)}, u32[]{:S(2)}) collective-permute-start(bf16[384,4096]{1,0:T(8,128)(2,1)} %get-tuple-element.72), channel_id=1, source_target_pairs={{0,1},{1,0},{2,3},{3,2},{4,5},{5,4},{6,7},{7,6},{8,9},{9,8},{10,11... | collective-permute-start | bytes 9437192 | tf_op jit(solution)/shard_map/ppermute | solution.py:86
  145.2 7.1 %product_in.1.total_ref = bf16[384,4096]{1,0:T(8,128)(2,1)} custom-call(bf16[384,384]{1,0:T(8,128)(2,1)S(1)} %get-tuple-element.88.dg_ref.dg_own, bf16[384,384]{1,0:T(8,128)(2,1)S(1)} %get-tuple-element.90.du_ref.du_own, bf16[1,4096,384]{2,1,0:T(8,128)(2,1)} %gate_ref.9, bf16[1,4096,384]{2,1,0:T(8,128)(2,1)} %up_ref.9), custom_call_target="tpu_custom_call" | custom-call | flops 199999995904 | bytes 1 | tf_op jit(solution)/shard_map/product_in/pallas_call | solution.py:383
  152.3 5.6 %to_lines.3 = bf16[1536,1024]{1,0:T(8,128)(2,1)} custom-call(bf16[384,4096]{1,0:T(8,128)(2,1)} %product_in.1.total_ref, bf16[384,4096]{1,0:T(8,128)(2,1)} %collective-permute-done.3.arrived_ref, bf16[192,192]{1,0:T(8,128)(2,1)S(1)} %copy-done.3), custom_call_target="tpu_custom_call" | custom-call | flops 1 | bytes 1 | tf_op jit(solution)/shard_map/to_lines/pallas_call | solution.py:413
  157.9 0.1 all-to-all-done.2
  158.0 10.9 %all-to-all-start.3 = ((bf16[64,24,1024]{2,1,0:T(8,128)(2,1)}), bf16[64,24,1024]{2,1,0:T(8,128)(2,1)}, u32[]{:S(2)}, u32[]{:S(2)}) async-start(bf16[64,24,1024]{2,1,0:T(8,128)(2,1)} %bitcast.24), calls=%async_computation.3 | async-start | bytes 6291456 | tf_op jit(solution)/shard_map/all_to_all | solution.py:79
  169.0 0.5 multiply_divide_fusion
  169.5 1.0 multiply_select_fusion.weight_ref
  170.5 7.1 %rows_grad.1 = bf16[1,384,4096]{2,1,0:T(8,128)(2,1)} custom-call(bf16[384,384]{1,0:T(8,128)(2,1)S(1)} %copy-done.5, bf16[384,384]{1,0:T(8,128)(2,1)S(1)} %get-tuple-element.95.hidden_other, bf16[384,4096]{1,0:T(8,128)(2,1)} %get-tuple-element.96.own, bf16[384,4096]{1,0:T(8,128)(2,1)} %get-tuple-element.97.other), custom_call_target="tpu_custom_call" | custom-call | flops 1 | bytes 1 | tf_op jit(solution)/shard_map/rows_grad/pallas_call | solution.py:460
  177.5 6.1 %mix.1 = (bf16[128,4096]{1,0:T(8,128)(2,1)}, f32[128,2]{1,0:T(8,128)S(1)}) custom-call(bf16[512,768]{1,0:T(8,128)(2,1)S(1)} %get-tuple-element.54.first_ref, bf16[512,768]{1,0:T(8,128)(2,1)S(1)} %get-tuple-element.55.second_ref, bf16[1536,1024]{1,0:T(8,128)(2,1)} %bitcast.14.lines_ref, bf16[128,4096]{1,0:T(8,128)(2,1)} %grad_ref.1, ...), custom_call_target="tpu_custom_call" | custom-call | flops 1 | bytes 1 | tf_op jit(solution)/shard_map/mix/pallas_call | solution.py:501
  183.7 11.5 %columns_grad.1 = (bf16[1,4096,384]{2,1,0:T(8,128)(2,1)}, bf16[1,4096,384]{2,1,0:T(8,128)(2,1)}) custom-call(bf16[384,4096]{1,0:T(8,128)(2,1)} %get-tuple-element.86.own, bf16[384,4096]{1,0:T(8,128)(2,1)} %get-tuple-element.87.other, bf16[384,384]{1,0:T(8,128)(2,1)S(1)} %get-tuple-element.88.dg_ref.dg_own, bf16[384,384]{1,0:T(8,128)(2,1)S(1)} %copy-done.7, ...), custom_call_target="tpu_custom_call" | custom-call | flops 1 | bytes 1 | tf_op jit(solution)/shard_map/columns_grad/pallas_call | solution.py:439
  195.2 0.2 multiply_reduce_fusion
  195.4 0.1 add_multiply_fusion
  195.6 0.1 copy.28
  195.7 0.0 copy-done.25
  195.7 0.2 fusion.6
  195.9 0.1 select_reduce_fusion
  196.1 0.8 fusion.3
  196.9 9.2 %all-to-all-done.3 = bf16[64,24,1024]{2,1,0:T(8,128)(2,1)} async-done(((bf16[64,24,1024]{2,1,0:T(8,128)(2,1)}), bf16[64,24,1024]{2,1,0:T(8,128)(2,1)}, u32[]{:S(2)}, u32[]{:S(2)}) %all-to-all-start.3) | async-done | bytes 3145760 | tf_op jit(solution)/shard_map/all_to_all | solution.py:79
  206.1 4.5 %unpack.1 = bf16[128,4096]{1,0:T(8,128)(2,1)} custom-call(bf16[512,768]{1,0:T(8,128)(2,1)S(1)} %get-tuple-element.83.either_ref, bf16[1536,1024]{1,0:T(8,128)(2,1)} %bitcast.16.lines_ref), custom_call_target="tpu_custom_call" | custom-call | flops 1 | bytes 1 | tf_op jit(solution)/shard_map/unpack/pallas_call | solution.py:533
  (81 shorter events, 0.2 us)
Async XLA Ops:
  5.1 11.9 %copy-start.12 = (f32[128,128]{1,0:T(8,128)S(1)}, f32[128,128]{1,0:T(8,128)}, u32[]{:S(2)}) copy-start(f32[128,128]{1,0:T(8,128)} %param.14) | copy-start | bytes 196612
  5.1 12.1 %copy-start.24 = (s32[128]{0:T(128)S(1)}, s32[128]{0:T(128)}, u32[]{:S(2)}) copy-start(s32[128]{0:T(128)} %param.15) | copy-start | bytes 1540
  5.1 12.1 %copy-start.33 = (s32[128,2]{0,1:T(2,128)S(1)}, s32[128,2]{0,1:T(2,128)}, u32[]{:S(2)}) copy-start(s32[128,2]{0,1:T(2,128)} %param.16) | copy-start | bytes 3076
  5.1 14.4 %copy-start = (bf16[128,4096]{1,0:T(8,128)(2,1)S(1)}, bf16[128,4096]{1,0:T(8,128)(2,1)}, u32[]{:S(2)}) copy-start(bf16[128,4096]{1,0:T(8,128)(2,1)} %grad_ref.1) | copy-start | bytes 3145732
  5.1 14.4 %copy-start.1 = (bf16[192,192]{1,0:T(8,128)(2,1)S(1)}, bf16[192,192]{1,0:T(8,128)(2,1)}, u32[]{:S(2)}) copy-start(bf16[192,192]{1,0:T(8,128)(2,1)} %constant.46.clone.order_ref) | copy-start | bytes 221188
  5.1 50.2 %all-to-all-start = ((bf16[64,24,1024]{2,1,0:T(8,128)(2,1)}), bf16[64,24,1024]{2,1,0:T(8,128)(2,1)}, u32[]{:S(2)}, u32[]{:S(2)}) async-start(bf16[64,24,1024]{2,1,0:T(8,128)(2,1)} %bitcast.27), calls=%async_computation | async-start | bytes 6291456 | tf_op jit(solution)/shard_map/all_to_all | solution.py:79
  17.0 5.7 %copy-start.32 = (s32[768]{0:T(1024)S(1)}, s32[768]{0:T(1024)}, u32[]{:S(2)}) copy-start(s32[768]{0:T(1024)} %constant.52) | copy-start | bytes 9220
  17.1 1.3 copy-start.16
  17.2 0.6 copy-start.22
  17.9 4.8 %copy-start.14 = (f32[128,2]{1,0:T(8,128)}, f32[128,2]{1,0:T(8,128)S(1)}, u32[]{:S(2)}) copy-start(f32[128,2]{1,0:T(8,128)S(1)} %copy.24) | copy-start | bytes 3076
  17.9 0.6 copy-start.28
  18.0 4.7 %copy-start.18 = (f32[128]{0:T(128)}, f32[128]{0:T(128)S(1)}, u32[]{:S(2)}) copy-start(f32[128]{0:T(128)S(1)} %exponential_reduce_fusion) | copy-start | bytes 1540
  18.2 0.5 copy-start.30
  18.7 4.0 %copy-start.20 = (f32[128]{0:T(128)}, f32[128]{0:T(128)S(1)}, u32[]{:S(2)}) copy-start(f32[128]{0:T(128)S(1)} %fusion.4) | copy-start | bytes 1540
  18.7 0.6 copy-start.26
  55.3 24.4 %collective-permute-start = (bf16[1536,1024]{1,0:T(8,128)(2,1)}, bf16[1536,1024]{1,0:T(8,128)(2,1)}, u32[]{:S(2)}, u32[]{:S(2)}) collective-permute-start(bf16[1536,1024]{1,0:T(8,128)(2,1)} %bitcast.3.lines_ref), channel_id=1, source_target_pairs={{0,1},{1,0},{2,3},{3,2},{4,5},{5,4},{6,7},{7,6},{8,9},{9,8},{10,11... | collective-permute-start | bytes 9437192 | tf_op jit(solution)/shard_map/ppermute | solution.py:86
  55.3 14.2 %copy-start.10 = (bf16[192,192]{1,0:T(8,128)(2,1)S(1)}, bf16[192,192]{1,0:T(8,128)(2,1)}, u32[]{:S(2)}) copy-start(bf16[192,192]{1,0:T(8,128)(2,1)} %constant.47.clone.order_ref) | copy-start | bytes 221188
  55.3 54.5 %all-to-all-start.1 = ((bf16[64,24,1024]{2,1,0:T(8,128)(2,1)}), bf16[64,24,1024]{2,1,0:T(8,128)(2,1)}, u32[]{:S(2)}, u32[]{:S(2)}) async-start(bf16[64,24,1024]{2,1,0:T(8,128)(2,1)} %bitcast.25), calls=%async_computation.1 | async-start | bytes 6291456 | tf_op jit(solution)/shard_map/all_to_all | solution.py:79
  79.6 16.8 %copy-start.4 = (bf16[384,384]{1,0:T(8,128)(2,1)}, bf16[384,384]{1,0:T(8,128)(2,1)S(1)}, u32[]{:S(2)}) copy-start(bf16[384,384]{1,0:T(8,128)(2,1)S(1)} %get-tuple-element.94.hidden_ref.hidden_own) | copy-start | bytes 884740
  93.4 8.6 %collective-permute-start.1 = (bf16[384,4096]{1,0:T(8,128)(2,1)}, bf16[384,4096]{1,0:T(8,128)(2,1)}, u32[]{:S(2)}, u32[]{:S(2)}) collective-permute-start(bf16[384,4096]{1,0:T(8,128)(2,1)} %get-tuple-element.60), channel_id=1, source_target_pairs={{0,1},{1,0},{2,3},{3,2},{4,5},{5,4},{6,7},{7,6},{8,9},{9,8},{10,11... | collective-permute-start | bytes 9437192 | tf_op jit(solution)/shard_map/ppermute | solution.py:86
  96.4 5.6 %copy-start.2 = (bf16[192,192]{1,0:T(8,128)(2,1)S(1)}, bf16[192,192]{1,0:T(8,128)(2,1)}, u32[]{:S(2)}) copy-start(bf16[192,192]{1,0:T(8,128)(2,1)} %constant.46.clone.order_ref) | copy-start | bytes 221188
  109.8 16.7 %collective-permute-start.2 = (bf16[1536,1024]{1,0:T(8,128)(2,1)}, bf16[1536,1024]{1,0:T(8,128)(2,1)}, u32[]{:S(2)}, u32[]{:S(2)}) collective-permute-start(bf16[1536,1024]{1,0:T(8,128)(2,1)} %bitcast.12.lines_ref), channel_id=1, source_target_pairs={{0,1},{1,0},{2,3},{3,2},{4,5},{5,4},{6,7},{7,6},{8,9},{9,8},{10,11... | collective-permute-start | bytes 9437192 | tf_op jit(solution)/shard_map/ppermute | solution.py:86
  109.8 48.2 %all-to-all-start.2 = ((bf16[64,24,1024]{2,1,0:T(8,128)(2,1)}), bf16[64,24,1024]{2,1,0:T(8,128)(2,1)}, u32[]{:S(2)}, u32[]{:S(2)}) async-start(bf16[64,24,1024]{2,1,0:T(8,128)(2,1)} %bitcast.26), calls=%async_computation.2 | async-start | bytes 6291456 | tf_op jit(solution)/shard_map/all_to_all | solution.py:79
  117.9 8.6 %copy-start.11 = (bf16[192,192]{1,0:T(8,128)(2,1)S(1)}, bf16[192,192]{1,0:T(8,128)(2,1)}, u32[]{:S(2)}) copy-start(bf16[192,192]{1,0:T(8,128)(2,1)} %constant.47.clone.order_ref) | copy-start | bytes 221188
  141.0 11.3 %copy-start.6 = (bf16[384,384]{1,0:T(8,128)(2,1)}, bf16[384,384]{1,0:T(8,128)(2,1)S(1)}, u32[]{:S(2)}) copy-start(bf16[384,384]{1,0:T(8,128)(2,1)S(1)} %get-tuple-element.89.dg_other) | copy-start | bytes 884740
  141.0 11.3 %copy-start.8 = (bf16[384,384]{1,0:T(8,128)(2,1)}, bf16[384,384]{1,0:T(8,128)(2,1)S(1)}, u32[]{:S(2)}) copy-start(bf16[384,384]{1,0:T(8,128)(2,1)S(1)} %get-tuple-element.91.du_other) | copy-start | bytes 884740
  141.0 11.3 %collective-permute-start.3 = (bf16[384,4096]{1,0:T(8,128)(2,1)}, bf16[384,4096]{1,0:T(8,128)(2,1)}, u32[]{:S(2)}, u32[]{:S(2)}) collective-permute-start(bf16[384,4096]{1,0:T(8,128)(2,1)} %get-tuple-element.72), channel_id=1, source_target_pairs={{0,1},{1,0},{2,3},{3,2},{4,5},{5,4},{6,7},{7,6},{8,9},{9,8},{10,11... | collective-permute-start | bytes 9437192 | tf_op jit(solution)/shard_map/ppermute | solution.py:86
  145.2 7.1 %copy-start.3 = (bf16[192,192]{1,0:T(8,128)(2,1)S(1)}, bf16[192,192]{1,0:T(8,128)(2,1)}, u32[]{:S(2)}) copy-start(bf16[192,192]{1,0:T(8,128)(2,1)} %constant.46.clone.order_ref) | copy-start | bytes 221188
  158.0 10.9 %copy-start.19 = (f32[128]{0:T(128)S(1)}, f32[128]{0:T(128)}, u32[]{:S(2)}) copy-start(f32[128]{0:T(128)} %copy-done.18) | copy-start | bytes 1540
  158.0 10.9 %copy-start.31 = (f32[128]{0:T(128)S(1)}, f32[128]{0:T(128)}, u32[]{:S(2)}) copy-start(f32[128]{0:T(128)} %copy-done.30) | copy-start | bytes 1540
  158.0 11.5 %copy-start.21 = (f32[128]{0:T(128)S(1)}, f32[128]{0:T(128)}, u32[]{:S(2)}) copy-start(f32[128]{0:T(128)} %copy-done.20) | copy-start | bytes 1540
  158.0 11.5 %copy-start.27 = (pred[128]{0:T(512)(128)(4,1)S(1)}, pred[128]{0:T(512)(128)(4,1)}, u32[]{:S(2)}) copy-start(pred[128]{0:T(512)(128)(4,1)} %copy-done.26) | copy-start | bytes 388
  158.0 12.4 %copy-start.5 = (bf16[384,384]{1,0:T(8,128)(2,1)S(1)}, bf16[384,384]{1,0:T(8,128)(2,1)}, u32[]{:S(2)}) copy-start(bf16[384,384]{1,0:T(8,128)(2,1)} %copy-done.4) | copy-start | bytes 884740
  158.0 48.1 %all-to-all-start.3 = ((bf16[64,24,1024]{2,1,0:T(8,128)(2,1)}), bf16[64,24,1024]{2,1,0:T(8,128)(2,1)}, u32[]{:S(2)}, u32[]{:S(2)}) async-start(bf16[64,24,1024]{2,1,0:T(8,128)(2,1)} %bitcast.24), calls=%async_computation.3 | async-start | bytes 6291456 | tf_op jit(solution)/shard_map/all_to_all | solution.py:79
  177.5 6.1 %copy-start.7 = (bf16[384,384]{1,0:T(8,128)(2,1)S(1)}, bf16[384,384]{1,0:T(8,128)(2,1)}, u32[]{:S(2)}) copy-start(bf16[384,384]{1,0:T(8,128)(2,1)} %copy-done.6) | copy-start | bytes 884740
  177.5 6.1 %copy-start.9 = (bf16[384,384]{1,0:T(8,128)(2,1)S(1)}, bf16[384,384]{1,0:T(8,128)(2,1)}, u32[]{:S(2)}) copy-start(bf16[384,384]{1,0:T(8,128)(2,1)} %copy-done.8) | copy-start | bytes 884740
  183.6 11.6 %copy-start.15 = (f32[128,2]{1,0:T(8,128)S(1)}, f32[128,2]{1,0:T(8,128)}, u32[]{:S(2)}) copy-start(f32[128,2]{1,0:T(8,128)} %copy-done.14) | copy-start | bytes 3076
  183.6 12.0 %copy-start.13 = (f32[128,128]{1,0:T(8,128)S(1)}, f32[128,128]{1,0:T(8,128)}, u32[]{:S(2)}) copy-start(f32[128,128]{1,0:T(8,128)} %param.14) | copy-start | bytes 196612
  183.6 12.0 %copy-start.17 = (f32[128]{0:T(128)S(1)}, f32[128]{0:T(128)}, u32[]{:S(2)}) copy-start(f32[128]{0:T(128)} %copy-done.16) | copy-start | bytes 1540
  183.6 12.0 %copy-start.25 = (s32[128]{0:T(128)S(1)}, s32[128]{0:T(128)}, u32[]{:S(2)}) copy-start(s32[128]{0:T(128)} %param.15) | copy-start | bytes 1540
  183.6 12.0 %copy-start.29 = (s32[128]{0:T(128)S(1)}, s32[128]{0:T(128)}, u32[]{:S(2)}) copy-start(s32[128]{0:T(128)} %copy-done.28) | copy-start | bytes 1540
  183.7 12.0 %copy-start.34 = (f32[128]{0:T(128)S(1)}, f32[128]{0:T(128)}, u32[]{:S(2)}) copy-start(f32[128]{0:T(128)} %multiply_divide_fusion) | copy-start | bytes 1540
  183.7 12.3 %copy-start.23 = (s32[128,2]{0,1:T(2,128)S(1)}, s32[128,2]{0,1:T(2,128)}, u32[]{:S(2)}) copy-start(s32[128,2]{0,1:T(2,128)} %copy-done.22) | copy-start | bytes 3076
